TPU v7x, 32 devices: a whole 2x2x4 slice. The times are simulated.
32 devices in a mesh: section: 4 (over z), dp: 8 (over y, x, core).
Axes of the slice: x: 2, y: 2, z: 4, core: 2. Of those that a mesh axis runs over, the one named last changes fastest.
Arguments:
- pages_in: bfloat16 [16, 512, 768], P('dp'), may hold values from -6 to 6
- coords: int32 [16, 2, 512], P('dp'), may hold values from 0 to 999
- boxes: int32 [16, 16, 4], P('dp'), may hold values from 0 to 512, as said below
- qkv_weight: bfloat16 [2, 768, 2304], P(None, 'dp'), may hold values from -0.21875 to 0.21875
- attn_bias: bfloat16 [2, 3, 768], P(None, None, 'dp'), may hold values from -3 to 3
- pos_weight: bfloat16 [2, 768, 768], P(None, 'dp'), may hold values from -0.21875 to 0.21875
- out_weight: bfloat16 [2, 768, 768], P(None, 'dp'), may hold values from -2.5 to 2.5
- ffn_in: bfloat16 [2, 768, 3072], P(None, 'dp'), may hold values from -0.21875 to 0.21875
- ffn_in_bias: bfloat16 [2, 3072], P(None, 'dp'), may hold values from -3 to 3
- ffn_out: bfloat16 [2, 3072, 768], P(None, 'dp'), may hold values from -0.109375 to 0.109375
- ffn_out_bias: bfloat16 [2, 768], P(None, 'dp'), may hold values from -3 to 3
- ln_gain: bfloat16 [2, 2, 768], P(None, None, 'dp'), may hold values from 0.25 to 1.75
- ln_bias: bfloat16 [2, 2, 768], P(None, None, 'dp'), may hold values from -2 to 2
- cotangent: bfloat16 [16, 512, 768], P('dp'), may hold values from -6 to 6
Outputs:
- final: bfloat16 [16, 512, 768], P('dp', 'section')
- input_grad: float32 [16, 512, 768], P('dp', 'section')
- qkv_grad: float32 [2, 768, 2304], P(None, 'dp')
- attn_bias_grad: float32 [2, 3, 768], P(None, None, 'dp')
- pos_grad: float32 [2, 768, 768], P(None, 'dp')
- out_grad: float32 [2, 768, 768], P(None, 'dp')
- ffn_in_grad: float32 [2, 768, 3072], P(None, 'dp')
- ffn_in_bias_grad: float32 [2, 3072], P(None, 'dp')
- ffn_out_grad: float32 [2, 3072, 768], P(None, 'dp')
- ffn_out_bias_grad: float32 [2, 768], P(None, 'dp')
- ln_gain_grad: float32 [2, 2, 768], P(None, None, 'dp')
- ln_bias_grad: float32 [2, 2, 768], P(None, None, 'dp')
Inputs may be any that keep to these rules, and one draw needn't show every extreme that they name: `boxes`: A box slot masks keys c to e - 1 for queries a to b - 1; a slot with a = b is empty. Each page has between 1 and 16 non-empty slots, and some page has all 16; key starts are 1 or more, so that key 0 is never masked; a box spans at most 256 queries and 256 keys.
All inputs are finite; a program needn't handle non-finite values.
Results may differ from a plain program's by a relative error of at most 0.019.
Values may be sent and summed in bfloat16 or wider, within the bound.
A program may use at most 256 MiB of HBM per device.

v0:
```python
from functools import partial
import math

import jax
import jax.numpy as jnp
from jax import lax
from jax.sharding import PartitionSpec as P

HEAD_DIM = 64


EPSILON = 1e-06
NEGATIVE = -1e30


def for_sending(array):

    def short(part):
        return part.astype(jnp.bfloat16) if part.dtype == jnp.float32 else part

    return jax.tree.map(short, array)


def shifted(array, axis, by):
    devices = lax.axis_size(axis)
    pairs = [(i, i + by) for i in range(devices) if 0 <= i + by < devices]
    return lax.ppermute(array, axis, pairs)


def sinusoid(coord_pair, model_width):
    quarter = model_width // 4
    frequency = jnp.exp(jnp.arange(quarter, dtype=jnp.float32) * (-math.log(10000.0) / quarter))
    pieces = []
    for coord_axis in range(2):
        angles = coord_pair[coord_axis].astype(jnp.float32)[:, None] * frequency[None, :]
        pieces.append(jnp.sin(angles))
        pieces.append(jnp.cos(angles))
    return jnp.concatenate(pieces, axis=1)


def visible_of(box_page, length):
    places = jnp.arange(length, dtype=jnp.int32)
    row_hit = ((places[None, :] >= box_page[:, 0:1]) & (places[None, :] < box_page[:, 1:2])).astype(
        jnp.float32
    )
    col_hit = ((places[None, :] >= box_page[:, 2:3]) & (places[None, :] < box_page[:, 3:4])).astype(
        jnp.float32
    )
    covered = jnp.dot(row_hit.T, col_hit, precision=lax.Precision.HIGHEST)
    return covered < 0.5


def layer_norm(summed, gain_row, offset_row):
    center = summed - jnp.mean(summed, axis=-1, keepdims=True)
    spread = jnp.mean(center * center, axis=-1, keepdims=True)
    return center * lax.rsqrt(spread + EPSILON) * gain_row + offset_row


def norm_back(summed, gain_row, offset_row, grad_out):
    normed_out, pullback = jax.vjp(
        layer_norm, summed, gain_row.astype(jnp.float32), offset_row.astype(jnp.float32)
    )
    return pullback(grad_out)


def exact_gelu(inner):
    return jax.nn.gelu(inner, approximate=False)


def by_heads(matrix):
    return matrix.reshape(matrix.shape[0], matrix.shape[1] // HEAD_DIM, HEAD_DIM)


def attention_parts(hidden, placed_in, visible, weights):
    qkv_full, pos_full, out_full, bias_full, gain_row, offset_row = weights
    model_width = hidden.shape[1]
    projected = jnp.dot(hidden, qkv_full, preferred_element_type=jnp.float32)
    queries = by_heads((projected[:, :model_width] + bias_full[0]).astype(jnp.bfloat16))
    key_rows = by_heads(projected[:, model_width : 2 * model_width].astype(jnp.bfloat16))
    value_rows = by_heads((projected[:, 2 * model_width :] + bias_full[1]).astype(jnp.bfloat16))
    position_rows = by_heads(
        jnp.dot(placed_in, pos_full, preferred_element_type=jnp.float32).astype(jnp.bfloat16)
    )
    left_side = jnp.concatenate([queries, queries, position_rows], axis=2)
    right_side = jnp.concatenate([key_rows, position_rows, key_rows], axis=2)
    score_scale = 1.0 / math.sqrt(3.0 * HEAD_DIM)
    scores = (
        jnp.einsum("ihe,jhe->hij", left_side, right_side, preferred_element_type=jnp.float32)
        * score_scale
    )
    masked = jnp.where(visible[None, :, :], scores, NEGATIVE)
    row_max = jnp.max(masked, axis=2, keepdims=True)
    powered = jnp.exp(masked - row_max)
    probs_full = powered / jnp.sum(powered, axis=2, keepdims=True)
    probs_low = probs_full.astype(jnp.bfloat16)
    mixed = jnp.einsum("hij,jhe->ihe", probs_low, value_rows, preferred_element_type=jnp.float32)
    context = mixed.reshape(hidden.shape).astype(jnp.bfloat16)
    branch = jnp.dot(context, out_full, preferred_element_type=jnp.float32) + bias_full[2]
    summed = hidden.astype(jnp.float32) + branch
    output_full = layer_norm(summed, gain_row.astype(jnp.float32), offset_row.astype(jnp.float32))
    return (
        output_full,
        (left_side, right_side, probs_full, probs_low, value_rows, context, summed),
    )


def attention_back(hidden, placed_in, visible, weights, grad_out):
    qkv_full, pos_full, out_full, bias_full, gain_row, offset_row = weights
    output_full, saved = attention_parts(hidden, placed_in, visible, weights)
    left_side, right_side, probs_full, probs_low, value_rows, context, summed = saved
    grad_summed, grad_gain, grad_offset = norm_back(summed, gain_row, offset_row, grad_out)
    grad_branch = grad_summed.astype(jnp.bfloat16)
    grad_out_w = jnp.einsum("ia,ib->ab", context, grad_branch, preferred_element_type=jnp.float32)
    grad_out_b = jnp.sum(grad_branch.astype(jnp.float32), axis=0)
    grad_context = by_heads(
        jnp.einsum("ib,ab->ia", grad_branch, out_full, preferred_element_type=jnp.float32).astype(
            jnp.bfloat16
        )
    )
    grad_probs = jnp.einsum(
        "ihe,jhe->hij", grad_context, value_rows, preferred_element_type=jnp.float32
    )
    grad_values = jnp.einsum(
        "hij,ihe->jhe", probs_low, grad_context, preferred_element_type=jnp.float32
    ).astype(jnp.bfloat16)
    row_dot = jnp.sum(grad_probs * probs_full, axis=2, keepdims=True)
    grad_scores = (probs_full * (grad_probs - row_dot)).astype(jnp.bfloat16)
    score_scale = 1.0 / math.sqrt(3.0 * HEAD_DIM)
    grad_left = (
        jnp.einsum("hij,jhe->ihe", grad_scores, right_side, preferred_element_type=jnp.float32)
        * score_scale
    )
    grad_right = (
        jnp.einsum("hij,ihe->jhe", grad_scores, left_side, preferred_element_type=jnp.float32)
        * score_scale
    )
    head_size = HEAD_DIM
    flat_shape = hidden.shape
    grad_queries = (
        (grad_left[:, :, :head_size] + grad_left[:, :, head_size : 2 * head_size])
        .astype(jnp.bfloat16)
        .reshape(flat_shape)
    )
    grad_keys = (
        (grad_right[:, :, :head_size] + grad_right[:, :, 2 * head_size :])
        .astype(jnp.bfloat16)
        .reshape(flat_shape)
    )
    grad_position = (
        (grad_left[:, :, 2 * head_size :] + grad_right[:, :, head_size : 2 * head_size])
        .astype(jnp.bfloat16)
        .reshape(flat_shape)
    )
    grad_joint = jnp.concatenate([grad_queries, grad_keys, grad_values.reshape(flat_shape)], axis=1)
    grad_qkv_w = jnp.einsum("ia,ib->ab", hidden, grad_joint, preferred_element_type=jnp.float32)
    grad_pos_w = jnp.einsum(
        "ia,ib->ab", placed_in, grad_position, preferred_element_type=jnp.float32
    )
    grad_bias = jnp.stack(
        [
            jnp.sum(grad_queries.astype(jnp.float32), axis=0),
            jnp.sum(grad_values.reshape(flat_shape).astype(jnp.float32), axis=0),
            grad_out_b,
        ]
    )
    grad_hidden = grad_summed + jnp.einsum(
        "ib,ab->ia", grad_joint, qkv_full, preferred_element_type=jnp.float32
    )
    return (grad_hidden, (grad_qkv_w, grad_pos_w, grad_out_w, grad_bias, grad_gain, grad_offset))


def feed_parts(hidden, weights):
    in_full, down_full, in_bias, down_bias, gain_row, offset_row = weights
    inner = jnp.dot(hidden, in_full, preferred_element_type=jnp.float32) + in_bias
    active = exact_gelu(inner).astype(jnp.bfloat16)
    branch = jnp.dot(active, down_full, preferred_element_type=jnp.float32) + down_bias
    summed = hidden.astype(jnp.float32) + branch
    output_full = layer_norm(summed, gain_row.astype(jnp.float32), offset_row.astype(jnp.float32))
    return (output_full, (inner, active, summed))


def feed_back(hidden, weights, grad_out):
    in_full, down_full, in_bias, down_bias, gain_row, offset_row = weights
    output_full, saved = feed_parts(hidden, weights)
    inner, active, summed = saved
    grad_summed, grad_gain, grad_offset = norm_back(summed, gain_row, offset_row, grad_out)
    grad_branch = grad_summed.astype(jnp.bfloat16)
    grad_down_w = jnp.einsum("ia,ib->ab", active, grad_branch, preferred_element_type=jnp.float32)
    grad_down_b = jnp.sum(grad_branch.astype(jnp.float32), axis=0)
    grad_active = jnp.einsum(
        "ib,ab->ia", grad_branch, down_full, preferred_element_type=jnp.float32
    ).astype(jnp.bfloat16)
    gelu_out, gelu_pull = jax.vjp(exact_gelu, inner)
    grad_inner = gelu_pull(grad_active.astype(jnp.float32))[0].astype(jnp.bfloat16)
    grad_in_w = jnp.einsum("ia,ib->ab", hidden, grad_inner, preferred_element_type=jnp.float32)
    grad_in_b = jnp.sum(grad_inner.astype(jnp.float32), axis=0)
    grad_hidden = grad_summed + jnp.einsum(
        "ib,ab->ia", grad_inner, in_full, preferred_element_type=jnp.float32
    )
    return (grad_hidden, (grad_in_w, grad_down_w, grad_in_b, grad_down_b, grad_gain, grad_offset))


def segment_sizes(model_width, hidden_units, groups):
    part_model = model_width // groups
    part_hidden = hidden_units // groups
    attend_sizes = [
        part_model * 3 * model_width,
        part_model * model_width,
        part_model * model_width,
        3 * part_model,
        part_model,
        part_model,
    ]
    feed_sizes = [
        part_model * hidden_units,
        part_hidden * model_width,
        part_hidden,
        part_model,
        part_model,
        part_model,
    ]
    return (attend_sizes, feed_sizes)


def flat_pad(pieces, bundle, dtype_of):
    joined = jnp.concatenate([piece_item.reshape(-1) for piece_item in pieces])
    return jnp.concatenate([joined, jnp.zeros((bundle - joined.shape[0],), dtype_of)])


def grid_pad(pieces, groups, bundle):
    joined = jnp.concatenate([piece_item.reshape(groups, -1) for piece_item in pieces], axis=1)
    return jnp.concatenate(
        [joined, jnp.zeros((groups, bundle - joined.shape[1]), jnp.float32)], axis=1
    )


def cut_pieces(grid, sizes):
    pieces = []
    start_at = 0
    for size_one in sizes:
        pieces.append(grid[..., start_at : start_at + size_one])
        start_at = start_at + size_one
    return pieces


def spread_bias(bias_grad, groups):
    rows_of = bias_grad.shape[0]
    return bias_grad.reshape(rows_of, groups, -1).transpose(1, 0, 2).reshape(groups, -1)


def shards(
    pages_in,
    coords,
    boxes,
    qkv_weight,
    attn_bias,
    pos_weight,
    out_weight,
    ffn_in,
    ffn_in_bias,
    ffn_out,
    ffn_out_bias,
    ln_gain,
    ln_bias,
    cotangent,
):
    section_count = lax.axis_size("section")
    groups = lax.axis_size("dp")
    section_index = lax.axis_index("section")
    layer_index = section_index // 2
    kind_index = section_index % 2
    micro_count, length, model_width = pages_in.shape
    hidden_units = ffn_in.shape[2]
    part_model = model_width // groups
    part_hidden = hidden_units // groups
    attend_sizes, feed_sizes = segment_sizes(model_width, hidden_units, groups)
    bundle = max(sum(attend_sizes), sum(feed_sizes))

    def layer_slice(array_in):
        return lax.dynamic_index_in_dim(array_in, layer_index, 0, keepdims=False)

    gain_pair = layer_slice(ln_gain)
    offset_pair = layer_slice(ln_bias)
    attend_own = [
        layer_slice(qkv_weight),
        layer_slice(pos_weight),
        layer_slice(out_weight),
        layer_slice(attn_bias),
        gain_pair[0],
        offset_pair[0],
    ]
    feed_own = [
        layer_slice(ffn_in),
        layer_slice(ffn_out),
        layer_slice(ffn_in_bias),
        layer_slice(ffn_out_bias),
        gain_pair[1],
        offset_pair[1],
    ]
    own_bundle = jnp.where(
        kind_index == 0,
        flat_pad(attend_own, bundle, jnp.bfloat16),
        flat_pad(feed_own, bundle, jnp.bfloat16),
    )
    gathered = lax.all_gather(own_bundle, "dp", axis=0, tiled=True).reshape(groups, bundle)
    attend_cut = cut_pieces(gathered, attend_sizes)
    attend_full = (
        attend_cut[0].reshape(model_width, 3 * model_width),
        attend_cut[1].reshape(model_width, model_width),
        attend_cut[2].reshape(model_width, model_width),
        attend_cut[3].reshape(groups, 3, part_model).transpose(1, 0, 2).reshape(3, model_width),
        attend_cut[4].reshape(model_width),
        attend_cut[5].reshape(model_width),
    )
    feed_cut = cut_pieces(gathered, feed_sizes)
    feed_full = (
        feed_cut[0].reshape(model_width, hidden_units),
        feed_cut[1].reshape(hidden_units, model_width),
        feed_cut[2].reshape(hidden_units),
        feed_cut[3].reshape(model_width),
        feed_cut[4].reshape(model_width),
        feed_cut[5].reshape(model_width),
    )
    placed_all = jax.vmap(partial(sinusoid, model_width=model_width))(coords).astype(jnp.bfloat16)

    def page_context(slot):
        placed_in = lax.dynamic_index_in_dim(placed_all, slot, 0, keepdims=False)
        visible = visible_of(lax.dynamic_index_in_dim(boxes, slot, 0, keepdims=False), length)
        return (placed_in, visible)

    def spare_forward(section_in, slot):
        return jnp.zeros((length, model_width), jnp.bfloat16)

    def attend_forward(section_in, slot):
        placed_in, visible = page_context(slot)
        return attention_parts(section_in, placed_in, visible, attend_full)[0].astype(jnp.bfloat16)

    def feed_forward(section_in, slot):
        return feed_parts(section_in, feed_full)[0].astype(jnp.bfloat16)

    def forward_step(moment, carry):
        kept, finals, incoming = carry
        micro = moment - section_index
        active = (micro >= 0) & (micro < micro_count)
        slot = jnp.clip(micro, 0, micro_count - 1)
        fresh = lax.dynamic_index_in_dim(
            pages_in, jnp.minimum(moment, micro_count - 1), 0, keepdims=False
        )
        section_in = jnp.where(section_index == 0, fresh, incoming)
        result = lax.switch(
            jnp.where(active, kind_index + 1, 0),
            [spare_forward, attend_forward, feed_forward],
            section_in,
            slot,
        )
        kept = jnp.where(active, lax.dynamic_update_index_in_dim(kept, section_in, slot, 0), kept)
        finals = jnp.where(
            active & (section_index == section_count - 1),
            lax.dynamic_update_index_in_dim(finals, result, slot, 0),
            finals,
        )
        incoming = jax.tree.map(
            lambda part, own: part.astype(own.dtype),
            shifted(for_sending(result), "section", 1),
            result,
        )
        return (kept, finals, incoming)

    blank = jnp.zeros((micro_count, length, model_width), jnp.bfloat16)
    kept, finals, incoming = lax.fori_loop(
        0,
        micro_count + section_count - 1,
        forward_step,
        (blank, blank, jnp.zeros((length, model_width), jnp.bfloat16)),
    )

    def spare_backward(section_in, grad_in, slot):
        return (
            jnp.zeros((length, model_width), jnp.float32),
            jnp.zeros((groups, bundle), jnp.float32),
        )

    def attend_backward(section_in, grad_in, slot):
        placed_in, visible = page_context(slot)
        grad_hidden, grads = attention_back(section_in, placed_in, visible, attend_full, grad_in)
        pieces = [grads[0], grads[1], grads[2], spread_bias(grads[3], groups), grads[4], grads[5]]
        return (grad_hidden, grid_pad(pieces, groups, bundle))

    def feed_backward(section_in, grad_in, slot):
        grad_hidden, grads = feed_back(section_in, feed_full, grad_in)
        return (grad_hidden, grid_pad(list(grads), groups, bundle))

    def backward_step(moment, carry):
        accum, input_grads, incoming = carry
        micro = moment - (section_count - 1 - section_index)
        active = (micro >= 0) & (micro < micro_count)
        slot = jnp.clip(micro, 0, micro_count - 1)
        fresh = lax.dynamic_index_in_dim(
            cotangent, jnp.minimum(moment, micro_count - 1), 0, keepdims=False
        )
        grad_in = jnp.where(section_index == section_count - 1, fresh, incoming).astype(jnp.float32)
        section_in = lax.dynamic_index_in_dim(kept, slot, 0, keepdims=False)
        grad_hidden, grad_bundle = lax.switch(
            jnp.where(active, kind_index + 1, 0),
            [spare_backward, attend_backward, feed_backward],
            section_in,
            grad_in,
            slot,
        )
        input_grads = jnp.where(
            active & (section_index == 0),
            lax.dynamic_update_index_in_dim(input_grads, grad_hidden, slot, 0),
            input_grads,
        )
        accum = accum + grad_bundle
        incoming = shifted(grad_hidden.astype(jnp.bfloat16), "section", -1)
        return (accum, input_grads, incoming)

    accum_start = jnp.zeros((groups, bundle), jnp.float32)
    accum, input_grads, incoming = lax.fori_loop(
        0,
        micro_count + section_count - 1,
        backward_step,
        (
            accum_start,
            jnp.zeros((micro_count, length, model_width), jnp.float32),
            jnp.zeros((length, model_width), jnp.bfloat16),
        ),
    )
    shard = lax.psum_scatter(accum, "dp", scatter_dimension=0, tiled=True).reshape(bundle)
    is_attend = kind_index == 0
    attend_shard = cut_pieces(shard, attend_sizes)
    feed_shard = cut_pieces(shard, feed_sizes)

    def place_layer(piece, on_kind):
        base = jnp.zeros((2,) + piece.shape, jnp.float32)
        return jnp.where(
            on_kind, lax.dynamic_update_index_in_dim(base, piece, layer_index, 0), base
        )

    qkv_part = place_layer(attend_shard[0].reshape(part_model, 3 * model_width), is_attend)
    pos_part = place_layer(attend_shard[1].reshape(part_model, model_width), is_attend)
    out_part = place_layer(attend_shard[2].reshape(part_model, model_width), is_attend)
    bias_part = place_layer(attend_shard[3].reshape(3, part_model), is_attend)
    in_part = place_layer(feed_shard[0].reshape(part_model, hidden_units), ~is_attend)
    down_part = place_layer(feed_shard[1].reshape(part_hidden, model_width), ~is_attend)
    in_bias_part = place_layer(feed_shard[2], ~is_attend)
    down_bias_part = place_layer(feed_shard[3], ~is_attend)
    gain_piece = jnp.where(is_attend, attend_shard[4], feed_shard[4])
    offset_piece = jnp.where(is_attend, attend_shard[5], feed_shard[5])
    norm_base = jnp.zeros((2, 2, part_model), jnp.float32)
    zero_index = jnp.zeros((), jnp.int32)
    gain_part = lax.dynamic_update_slice(
        norm_base, gain_piece[None, None, :], (layer_index, kind_index, zero_index)
    )
    offset_part = lax.dynamic_update_slice(
        norm_base, offset_piece[None, None, :], (layer_index, kind_index, zero_index)
    )
    summed_parts = (
        lax.psum(qkv_part.astype(jnp.bfloat16), "section").astype(jnp.float32),
        lax.psum(bias_part.astype(jnp.bfloat16), "section").astype(jnp.float32),
        lax.psum(pos_part.astype(jnp.bfloat16), "section").astype(jnp.float32),
        lax.psum(out_part.astype(jnp.bfloat16), "section").astype(jnp.float32),
        lax.psum(in_part.astype(jnp.bfloat16), "section").astype(jnp.float32),
        lax.psum(in_bias_part.astype(jnp.bfloat16), "section").astype(jnp.float32),
        lax.psum(down_part.astype(jnp.bfloat16), "section").astype(jnp.float32),
        lax.psum(down_bias_part.astype(jnp.bfloat16), "section").astype(jnp.float32),
        lax.psum(gain_part.astype(jnp.bfloat16), "section").astype(jnp.float32),
        lax.psum(offset_part.astype(jnp.bfloat16), "section").astype(jnp.float32),
    )
    final_term = jnp.where(section_index == section_count - 1, finals.astype(jnp.float32), 0.0)
    input_term = jnp.where(section_index == 0, input_grads, 0.0)
    final_part, input_part = (
        lax.psum_scatter(
            final_term.astype(jnp.bfloat16), "section", scatter_dimension=1, tiled=True
        ).astype(jnp.float32),
        lax.psum_scatter(
            input_term.astype(jnp.bfloat16), "section", scatter_dimension=1, tiled=True
        ).astype(jnp.float32),
    )
    final_low = final_part.astype(jnp.bfloat16)
    return (
        final_low,
        input_part,
        summed_parts[0],
        summed_parts[1],
        summed_parts[2],
        summed_parts[3],
        summed_parts[4],
        summed_parts[5],
        summed_parts[6],
        summed_parts[7],
        summed_parts[8],
        summed_parts[9],
    )


def solution(mesh):
    in_specs = (
        P("dp", None, None),
        P("dp", None, None),
        P("dp", None, None),
        P(None, "dp", None),
        P(None, None, "dp"),
        P(None, "dp", None),
        P(None, "dp", None),
        P(None, "dp", None),
        P(None, "dp"),
        P(None, "dp", None),
        P(None, "dp"),
        P(None, None, "dp"),
        P(None, None, "dp"),
        P("dp", None, None),
    )
    out_specs = (
        P("dp", "section", None),
        P("dp", "section", None),
        P(None, "dp", None),
        P(None, None, "dp"),
        P(None, "dp", None),
        P(None, "dp", None),
        P(None, "dp", None),
        P(None, "dp"),
        P(None, "dp", None),
        P(None, "dp"),
        P(None, None, "dp"),
        P(None, None, "dp"),
    )
    return jax.shard_map(shards, mesh=mesh, in_specs=in_specs, out_specs=out_specs, check_vma=False)
```

profile of v0, /device:TPU:0, one launch (start us, length us, event | category | flops | bytes accessed | tf_op | source)
XLA Modules:
  0.0 1815.1 jit_solution(2209130499949220197)
XLA Ops:
  17.4 14.8 concatenate.32
  37.5 18.9 %dynamic-update-slice.23 = bf16[4723968]{0:T(1024)(128)(2,1)} dynamic-update-slice(bf16[4723968]{0:T(1024)(128)(2,1)} %broadcast.537, bf16[590496]{0:T(1024)(128)(2,1)S(1)} %copy-done.29, u32[]{:T(128)} %bitcast.45) | dynamic-update-slice | bytes 2361988
  57.1 7.9 fusion.138
  66.9 131.4 %all-reduce.8.cloned.1.call-done = bf16[4723968]{0:T(1024)(128)(2,1)} async-done(((bf16[4723968]{0:T(1024)(128)(2,1)}), bf16[4723968]{0:T(1024)(128)(2,1)}) %all-reduce.8.cloned.1.call-update) | async-done | bytes 9447952
  198.3 19.8 %reshape.460 = bf16[8,590496]{1,0:T(8,128)(2,1)} reshape(bf16[4723968]{0:T(1024)(128)(2,1)} %all-reduce.8.cloned.1.call-done) | data formatting | bytes 18895872 | tf_op jit(solution)/shard_map/reshape | solution.py:305
  229.0 5.4 reshape.461
  237.9 6.6 reshape.468
  244.5 6.6 reshape.470
  254.0 256.3 %while.39 = (s32[]{:T(128)}, bf16[2,512,768]{2,1,0:T(8,128)(2,1)}, bf16[2,512,768]{2,1,0:T(8,128)(2,1)}, bf16[512,768]{1,0:T(8,128)(2,1)S(1)}, s32[]{:T(128)}, /...) while((s32[]{:T(128)}, bf16[2,512,768]{2,1,0:T(8,128)(2,1)}, ...), condition=%wide.region_10.11_spmd, body=%wide.region_0.10_spmd.sunk | while | flops 4943517696 | bytes 136041488 | solution.py:370
  276.5 33.5 %conditional.5 = (bf16[512,768]{1,0:T(8,128)(2,1)S(1)}, bf16[1,512,768]{2,1,0:T(8,128)(2,1)S(1)}) conditional(s32[]{:T(128)} %clamp.21, () %tuple.166, (bf16[512,768]{1,0:T(8,128)(2,1)S(1)}, bf16[768,2304]{1,0:T(8,128)(2,1)}, bf16[3,768]{1,0:T(4,128)(2,1)S(1)}, s32[]{:T(128)}, s32[2,16,4]{1,2,0:T(4,128)S(1)}, ...), branch_computations={%region_1.1_spmd, %region_2.6_spmd, %region_7.9_spmd} | conditional | flops 4942338048 | bytes 123456456 | solution.py:350
  289.1 5.7 fusion.61
  295.6 10.9 fusion.156
  314.4 15.2 collective-permute-done
  332.1 33.5 %conditional.5 = (bf16[512,768]{1,0:T(8,128)(2,1)S(1)}, bf16[1,512,768]{2,1,0:T(8,128)(2,1)S(1)}) conditional(s32[]{:T(128)} %clamp.21, () %tuple.166, (bf16[512,768]{1,0:T(8,128)(2,1)S(1)}, bf16[768,2304]{1,0:T(8,128)(2,1)}, bf16[3,768]{1,0:T(4,128)(2,1)S(1)}, s32[]{:T(128)}, s32[2,16,4]{1,2,0:T(4,128)S(1)}, ...), branch_computations={%region_1.1_spmd, %region_2.6_spmd, %region_7.9_spmd} | conditional | flops 4942338048 | bytes 123456456 | solution.py:350
  344.7 5.7 fusion.61
  351.3 10.9 fusion.156
  370.1 14.6 collective-permute-done
  388.2 27.2 %collective-permute-start = (bf16[512,768]{1,0:T(8,128)(2,1)}, bf16[512,768]{1,0:T(8,128)(2,1)S(1)}, u32[]{:S(2)}, u32[]{:S(2)}) collective-permute-start(bf16[512,768]{1,0:T(8,128)(2,1)} %copy-done.25), channel_id=1, source_target_pairs={{0,8},{8,16},{16,24},{1,9},{9,17},{17,25},{2,10},{10,18},{18,26},{... | collective-permute-start | bytes 2359304 | tf_op jit(solution)/shard_map/while/body/eval_jaxpr/ppermute | solution.py:27
  417.6 13.7 collective-permute-done
  434.9 5.0 collective-permute-start
  442.1 12.8 collective-permute-done
  458.5 37.7 %collective-permute-start = (bf16[512,768]{1,0:T(8,128)(2,1)}, bf16[512,768]{1,0:T(8,128)(2,1)S(1)}, u32[]{:S(2)}, u32[]{:S(2)}) collective-permute-start(bf16[512,768]{1,0:T(8,128)(2,1)} %copy-done.25), channel_id=1, source_target_pairs={{0,8},{8,16},{16,24},{1,9},{9,17},{17,25},{2,10},{10,18},{18,26},{... | collective-permute-start | bytes 2359304 | tf_op jit(solution)/shard_map/while/body/eval_jaxpr/ppermute | solution.py:27
  498.4 11.9 collective-permute-done
  512.4 829.0 %while.40 = (s32[]{:T(128)}, f32[8,590496]{1,0:T(8,128)}, bf16[2,512,768]{2,1,0:T(8,128)(2,1)}, bf16[512,768]{1,0:T(8,128)(2,1)}, s32[]{:T(128)}, /*index=5*/s32...) while((s32[]{:T(128)}, f32[8,590496]{1,0:T(8,128)}, ...), condition=%wide.region_36.37_spmd.clone, body=%wide.region_12.36_spmd.clone.sunk | while | flops 14651242496 | bytes 609144384 | solution.py:420
  520.6 9.2 conditional.6
  521.6 6.7 broadcast.489
  531.2 15.4 select_add_fusion.2
  551.3 7.7 conditional.6
  552.2 6.7 broadcast.489
  560.3 20.1 %select_add_fusion.2 = f32[8,590496]{1,0:T(8,128)} fusion(f32[8,590496]{1,0:T(8,128)} %get-tuple-element.1611, f32[8,590496]{1,0:T(8,128)} %get-tuple-element.1729, pred[]{:T(512)S(6)} %compare.6), kind=kLoop, calls=%fused_computation.248.clone.1 | loop fusion | flops 9447936 | bytes 56687616 | tf_op jit(solution)/shard_map/while/body/eval_jaxpr/add | solution.py:415
  580.7 17.4 collective-permute-done.1
  601.3 7.7 conditional.6
  602.3 6.7 broadcast.489
  610.4 20.1 %select_add_fusion.2 = f32[8,590496]{1,0:T(8,128)} fusion(f32[8,590496]{1,0:T(8,128)} %get-tuple-element.1611, f32[8,590496]{1,0:T(8,128)} %get-tuple-element.1729, pred[]{:T(512)S(6)} %compare.6), kind=kLoop, calls=%fused_computation.248.clone.1 | loop fusion | flops 9447936 | bytes 56687616 | tf_op jit(solution)/shard_map/while/body/eval_jaxpr/add | solution.py:415
  630.7 335.9 %collective-permute-done.1 = bf16[512,768]{1,0:T(8,128)(2,1)} collective-permute-done((bf16[512,768]{1,0:T(8,128)(2,1)}, bf16[512,768]{1,0:T(8,128)(2,1)}, u32[]{:S(2)}, u32[]{:S(2)}) %collective-permute-start.1) | collective-permute-done | bytes 786464 | tf_op jit(solution)/shard_map/while/body/eval_jaxpr/ppermute | solution.py:27
  969.9 154.4 %conditional.6 = (bf16[512,768]{1,0:T(8,128)(2,1)}, f32[8,590496]{1,0:T(8,128)}) conditional(s32[]{:T(128)} %clamp.22, () %tuple.170, (bf16[768]{0:T(1024)(128)(2,1)S(1)}, f32[512,768]{1,0:T(8,128)S(1)}, bf16[512,768]{1,0:T(8,128)(2,1)S(1)}, bf16[768,2304]{1,0:T(8,128)(2,1)S(1)}, bf16[3,768]{1,0:T(4,128)(2,1)S(1)}, ...), branch_computations={%region_13.13_spmd, %region_14.26_spmd, %region_27.35_spmd} | conditional | flops 14640614400 | bytes 512231488 | solution.py:403
  984.1 8.4 fusion.110
  993.3 11.0 fusion.159
  1015.3 7.6 convert_reduce_fusion.6
  1022.9 10.2 multiply_reduce_fusion.5
  1035.5 7.3 multiply_convert_fusion.1
  1057.1 8.0 copy.107
  1065.0 7.1 reshape.421
  1072.2 5.3 constant_dynamic-update-slice_fusion.5
  1097.0 19.9 %dynamic-update-slice.36 = f32[8,590496]{1,0:T(8,128)} dynamic-update-slice(f32[8,590496]{1,0:T(8,128)} %dynamic-update-slice.35, f32[8,221376]{1,0:T(8,128)} %broadcast.496, s32[]{} %constant.455, s32[]{} %constant.461) | dynamic-update-slice | bytes 14168068 | tf_op jit(solution)/shard_map/while/body/eval_jaxpr/cond/branch_1_fun/concatenate | solution.py:232
  1125.7 20.1 %select_add_fusion.2 = f32[8,590496]{1,0:T(8,128)} fusion(f32[8,590496]{1,0:T(8,128)} %get-tuple-element.1611, f32[8,590496]{1,0:T(8,128)} %get-tuple-element.1729, pred[]{:T(512)S(6)} %compare.6), kind=kLoop, calls=%fused_computation.248.clone.1 | loop fusion | flops 9447936 | bytes 56687616 | tf_op jit(solution)/shard_map/while/body/eval_jaxpr/add | solution.py:415
  1146.0 6.4 collective-permute-done.1
  1155.9 154.3 %conditional.6 = (bf16[512,768]{1,0:T(8,128)(2,1)}, f32[8,590496]{1,0:T(8,128)}) conditional(s32[]{:T(128)} %clamp.22, () %tuple.170, (bf16[768]{0:T(1024)(128)(2,1)S(1)}, f32[512,768]{1,0:T(8,128)S(1)}, bf16[512,768]{1,0:T(8,128)(2,1)S(1)}, bf16[768,2304]{1,0:T(8,128)(2,1)S(1)}, bf16[3,768]{1,0:T(4,128)(2,1)S(1)}, ...), branch_computations={%region_13.13_spmd, %region_14.26_spmd, %region_27.35_spmd} | conditional | flops 14640614400 | bytes 512231488 | solution.py:403
  1170.2 8.4 fusion.110
  1179.4 11.0 fusion.159
  1201.3 7.6 convert_reduce_fusion.6
  1208.9 10.2 multiply_reduce_fusion.5
  1221.5 7.0 multiply_convert_fusion.1
  1242.9 8.0 copy.107
  1250.9 7.1 reshape.421
  1258.0 5.3 constant_dynamic-update-slice_fusion.5
  1282.8 19.9 %dynamic-update-slice.36 = f32[8,590496]{1,0:T(8,128)} dynamic-update-slice(f32[8,590496]{1,0:T(8,128)} %dynamic-update-slice.35, f32[8,221376]{1,0:T(8,128)} %broadcast.496, s32[]{} %constant.455, s32[]{} %constant.461) | dynamic-update-slice | bytes 14168068 | tf_op jit(solution)/shard_map/while/body/eval_jaxpr/cond/branch_1_fun/concatenate | solution.py:232
  1311.7 20.1 %select_add_fusion.2 = f32[8,590496]{1,0:T(8,128)} fusion(f32[8,590496]{1,0:T(8,128)} %get-tuple-element.1611, f32[8,590496]{1,0:T(8,128)} %get-tuple-element.1729, pred[]{:T(512)S(6)} %compare.6), kind=kLoop, calls=%fused_computation.248.clone.1 | loop fusion | flops 9447936 | bytes 56687616 | tf_op jit(solution)/shard_map/while/body/eval_jaxpr/add | solution.py:415
  1344.4 239.3 %all-reduce.10.cloned.1.call-done = f32[8,590496]{1,0:T(8,128)} async-done(((f32[8,590496]{1,0:T(8,128)}), f32[8,590496]{1,0:T(8,128)}) %all-reduce.10.cloned.1.call-update) | async-done | bytes 18895888
  1583.7 9.9 fusion.142
  1600.1 16.4 fusion.137
  1633.9 12.4 all-reduce.2
  1649.2 122.1 %all-reduce.12.cloned.1.call-done = (bf16[2,96,2304]{2,1,0:T(8,128)(2,1)}, bf16[2,96,768]{2,1,0:T(8,128)(2,1)}, bf16[2,96,768]{2,1,0:T(8,128)(2,1)}, bf16[2,96,3072]{2,1,0:T(8,128)(2,1)}, bf16[2,384,768]{2,1,0:T(8,128)(2,1)}) async-done(((bf16[2,96,2304]{2,1,0:T(8,128)(2,1)}, bf16[2,96,768]{2,1,0:T(8,128)(2,1)}, bf16[2,96,768]{2,1,0:T(8,128)(2,1)}, bf16[2,96,3072]{2,1,0:T(8,128)(2,1)}, ...) | async-done | bytes 3833872 | tf_op jit(solution)/shard_map/psum | solution.py:460
  1780.8 27.4 %reduce-scatter.3.cloned.1.call-done = bf16[2,128,768]{2,1,0:T(8,128)(2,1)} async-done(((bf16[2,512,768]{2,1,0:T(8,128)(2,1)}), bf16[2,128,768]{2,1,0:T(8,128)(2,1)}) %reduce-scatter.3.cloned.1.call-update) | async-done | bytes 393232 | tf_op jit(solution)/shard_map/reduce_scatter | solution.py:474
  (582 shorter events, 291.9 us)
Async XLA Ops:
  7.2 8.0 copy-start.55
  7.2 7.9 copy-start.56
  7.2 8.0 copy-start.57
  7.2 191.0 %all-reduce.8.cloned.1.call-start = ((), (), s32[]{:S(2)}) async-start(), calls=%async_computation.4 | async-start | bytes 18898944
  56.4 1527.3 %all-reduce.10.cloned.1.call-start = ((), (), s32[]{:S(2)}) async-start(), calls=%async_computation.5 | async-start | bytes 37797888
  244.5 9.5 copy-start.53
  295.6 10.9 copy-start.24
  310.8 18.7 %collective-permute-start = (bf16[512,768]{1,0:T(8,128)(2,1)}, bf16[512,768]{1,0:T(8,128)(2,1)S(1)}, u32[]{:S(2)}, u32[]{:S(2)}) collective-permute-start(bf16[512,768]{1,0:T(8,128)(2,1)} %copy-done.25), channel_id=1, source_target_pairs={{0,8},{8,16},{16,24},{1,9},{9,17},{17,25},{2,10},{10,18},{18,26},{... | collective-permute-start | bytes 2359304 | tf_op jit(solution)/shard_map/while/body/eval_jaxpr/ppermute | solution.py:27
  351.3 10.9 copy-start.24
  366.5 18.2 %collective-permute-start = (bf16[512,768]{1,0:T(8,128)(2,1)}, bf16[512,768]{1,0:T(8,128)(2,1)S(1)}, u32[]{:S(2)}, u32[]{:S(2)}) collective-permute-start(bf16[512,768]{1,0:T(8,128)(2,1)} %copy-done.25), channel_id=1, source_target_pairs={{0,8},{8,16},{16,24},{1,9},{9,17},{17,25},{2,10},{10,18},{18,26},{... | collective-permute-start | bytes 2359304 | tf_op jit(solution)/shard_map/while/body/eval_jaxpr/ppermute | solution.py:27
  388.2 43.1 %collective-permute-start = (bf16[512,768]{1,0:T(8,128)(2,1)}, bf16[512,768]{1,0:T(8,128)(2,1)S(1)}, u32[]{:S(2)}, u32[]{:S(2)}) collective-permute-start(bf16[512,768]{1,0:T(8,128)(2,1)} %copy-done.25), channel_id=1, source_target_pairs={{0,8},{8,16},{16,24},{1,9},{9,17},{17,25},{2,10},{10,18},{18,26},{... | collective-permute-start | bytes 2359304 | tf_op jit(solution)/shard_map/while/body/eval_jaxpr/ppermute | solution.py:27
  434.9 20.0 %collective-permute-start = (bf16[512,768]{1,0:T(8,128)(2,1)}, bf16[512,768]{1,0:T(8,128)(2,1)S(1)}, u32[]{:S(2)}, u32[]{:S(2)}) collective-permute-start(bf16[512,768]{1,0:T(8,128)(2,1)} %copy-done.25), channel_id=1, source_target_pairs={{0,8},{8,16},{16,24},{1,9},{9,17},{17,25},{2,10},{10,18},{18,26},{... | collective-permute-start | bytes 2359304 | tf_op jit(solution)/shard_map/while/body/eval_jaxpr/ppermute | solution.py:27
  458.5 51.8 %collective-permute-start = (bf16[512,768]{1,0:T(8,128)(2,1)}, bf16[512,768]{1,0:T(8,128)(2,1)S(1)}, u32[]{:S(2)}, u32[]{:S(2)}) collective-permute-start(bf16[512,768]{1,0:T(8,128)(2,1)} %copy-done.25), channel_id=1, source_target_pairs={{0,8},{8,16},{16,24},{1,9},{9,17},{17,25},{2,10},{10,18},{18,26},{... | collective-permute-start | bytes 2359304 | tf_op jit(solution)/shard_map/while/body/eval_jaxpr/ppermute | solution.py:27
  529.8 18.3 %collective-permute-start.1 = (bf16[512,768]{1,0:T(8,128)(2,1)}, bf16[512,768]{1,0:T(8,128)(2,1)}, u32[]{:S(2)}, u32[]{:S(2)}) collective-permute-start(bf16[512,768]{1,0:T(8,128)(2,1)} %get-tuple-element.1612), channel_id=1, source_target_pairs={{8,0},{16,8},{24,16},{9,1},{17,9},{25,17},{10,2},{18,10},{26,18},{... | collective-permute-start | bytes 2359304 | tf_op jit(solution)/shard_map/while/body/eval_jaxpr/ppermute | solution.py:27
  531.1 15.4 copy-start.7
  531.1 15.4 copy-start.14
  531.1 16.9 copy-start.36
  531.2 16.9 copy-start.43
  531.2 16.9 copy-start.46
  531.2 16.9 copy-start.50
  558.9 39.2 %collective-permute-start.1 = (bf16[512,768]{1,0:T(8,128)(2,1)}, bf16[512,768]{1,0:T(8,128)(2,1)}, u32[]{:S(2)}, u32[]{:S(2)}) collective-permute-start(bf16[512,768]{1,0:T(8,128)(2,1)} %get-tuple-element.1612), channel_id=1, source_target_pairs={{8,0},{16,8},{24,16},{9,1},{17,9},{25,17},{10,2},{18,10},{26,18},{... | collective-permute-start | bytes 2359304 | tf_op jit(solution)/shard_map/while/body/eval_jaxpr/ppermute | solution.py:27
  560.2 20.2 %copy-start.7 = (bf16[512,768]{1,0:T(8,128)(2,1)S(1)}, bf16[512,768]{1,0:T(8,128)(2,1)}, u32[]{:S(2)}) copy-start(bf16[512,768]{1,0:T(8,128)(2,1)} %get-tuple-element.1612) | copy-start | bytes 2359300 | tf_op jit(solution)/shard_map/while
  560.2 20.2 %copy-start.14 = (bf16[2,512,768]{2,1,0:T(8,128)(2,1)S(1)}, bf16[2,512,768]{2,1,0:T(8,128)(2,1)}, u32[]{:S(2)}) copy-start(bf16[2,512,768]{2,1,0:T(8,128)(2,1)} %get-tuple-element.1730) | copy-start | bytes 4718596 | tf_op jit(solution)/shard_map/while
  560.2 37.9 %copy-start.36 = (bf16[3,768]{1,0:T(4,128)(2,1)S(1)}, bf16[3,768]{1,0:T(4,128)(2,1)}, u32[]{:S(2)}) copy-start(bf16[3,768]{1,0:T(4,128)(2,1)} %copy-done.35) | copy-start | bytes 13828 | tf_op jit(solution)/shard_map/while
  560.3 37.9 %copy-start.43 = (bf16[3072]{0:T(1024)(128)(2,1)S(1)}, bf16[3072]{0:T(1024)(128)(2,1)}, u32[]{:S(2)}) copy-start(bf16[3072]{0:T(1024)(128)(2,1)} %copy-done.42) | copy-start | bytes 18436 | tf_op jit(solution)/shard_map/while
  560.3 37.9 %copy-start.46 = (bf16[768]{0:T(1024)(128)(2,1)S(1)}, bf16[768]{0:T(1024)(128)(2,1)}, u32[]{:S(2)}) copy-start(bf16[768]{0:T(1024)(128)(2,1)} %copy-done.45) | copy-start | bytes 4612 | tf_op jit(solution)/shard_map/while
  560.3 37.9 %copy-start.50 = (bf16[768]{0:T(1024)(128)(2,1)S(1)}, bf16[768]{0:T(1024)(128)(2,1)}, u32[]{:S(2)}) copy-start(bf16[768]{0:T(1024)(128)(2,1)} %copy-done.49) | copy-start | bytes 4612 | tf_op jit(solution)/shard_map/while
  580.7 17.4 copy-start.15
  609.0 357.7 %collective-permute-start.1 = (bf16[512,768]{1,0:T(8,128)(2,1)}, bf16[512,768]{1,0:T(8,128)(2,1)}, u32[]{:S(2)}, u32[]{:S(2)}) collective-permute-start(bf16[512,768]{1,0:T(8,128)(2,1)} %get-tuple-element.1612), channel_id=1, source_target_pairs={{8,0},{16,8},{24,16},{9,1},{17,9},{25,17},{10,2},{18,10},{26,18},{... | collective-permute-start | bytes 2359304 | tf_op jit(solution)/shard_map/while/body/eval_jaxpr/ppermute | solution.py:27
  610.3 20.2 %copy-start.7 = (bf16[512,768]{1,0:T(8,128)(2,1)S(1)}, bf16[512,768]{1,0:T(8,128)(2,1)}, u32[]{:S(2)}) copy-start(bf16[512,768]{1,0:T(8,128)(2,1)} %get-tuple-element.1612) | copy-start | bytes 2359300 | tf_op jit(solution)/shard_map/while
  610.3 20.2 %copy-start.14 = (bf16[2,512,768]{2,1,0:T(8,128)(2,1)S(1)}, bf16[2,512,768]{2,1,0:T(8,128)(2,1)}, u32[]{:S(2)}) copy-start(bf16[2,512,768]{2,1,0:T(8,128)(2,1)} %get-tuple-element.1730) | copy-start | bytes 4718596 | tf_op jit(solution)/shard_map/while
  610.3 356.4 %copy-start.36 = (bf16[3,768]{1,0:T(4,128)(2,1)S(1)}, bf16[3,768]{1,0:T(4,128)(2,1)}, u32[]{:S(2)}) copy-start(bf16[3,768]{1,0:T(4,128)(2,1)} %copy-done.35) | copy-start | bytes 13828 | tf_op jit(solution)/shard_map/while
  610.3 356.4 %copy-start.43 = (bf16[3072]{0:T(1024)(128)(2,1)S(1)}, bf16[3072]{0:T(1024)(128)(2,1)}, u32[]{:S(2)}) copy-start(bf16[3072]{0:T(1024)(128)(2,1)} %copy-done.42) | copy-start | bytes 18436 | tf_op jit(solution)/shard_map/while
  610.3 356.4 %copy-start.46 = (bf16[768]{0:T(1024)(128)(2,1)S(1)}, bf16[768]{0:T(1024)(128)(2,1)}, u32[]{:S(2)}) copy-start(bf16[768]{0:T(1024)(128)(2,1)} %copy-done.45) | copy-start | bytes 4612 | tf_op jit(solution)/shard_map/while
  610.3 356.4 %copy-start.50 = (bf16[768]{0:T(1024)(128)(2,1)S(1)}, bf16[768]{0:T(1024)(128)(2,1)}, u32[]{:S(2)}) copy-start(bf16[768]{0:T(1024)(128)(2,1)} %copy-done.49) | copy-start | bytes 4612 | tf_op jit(solution)/shard_map/while
  630.7 335.9 %copy-start.15 = (bf16[2,512,768]{2,1,0:T(8,128)(2,1)}, bf16[2,512,768]{2,1,0:T(8,128)(2,1)S(1)}, u32[]{:S(2)}) copy-start(bf16[2,512,768]{2,1,0:T(8,128)(2,1)S(1)} %fusion.215) | copy-start | bytes 4718596 | tf_op jit(solution)/shard_map/while
  993.3 11.1 copy-start.22
  1022.8 10.2 slice-start
  1022.9 11.4 slice-start.1
  1022.9 12.6 slice-start.2
  1124.3 28.2 %collective-permute-start.1 = (bf16[512,768]{1,0:T(8,128)(2,1)}, bf16[512,768]{1,0:T(8,128)(2,1)}, u32[]{:S(2)}, u32[]{:S(2)}) collective-permute-start(bf16[512,768]{1,0:T(8,128)(2,1)} %get-tuple-element.1612), channel_id=1, source_target_pairs={{8,0},{16,8},{24,16},{9,1},{17,9},{25,17},{10,2},{18,10},{26,18},{... | collective-permute-start | bytes 2359304 | tf_op jit(solution)/shard_map/while/body/eval_jaxpr/ppermute | solution.py:27
  1125.6 20.2 %copy-start.7 = (bf16[512,768]{1,0:T(8,128)(2,1)S(1)}, bf16[512,768]{1,0:T(8,128)(2,1)}, u32[]{:S(2)}) copy-start(bf16[512,768]{1,0:T(8,128)(2,1)} %get-tuple-element.1612) | copy-start | bytes 2359300 | tf_op jit(solution)/shard_map/while
  1125.6 20.2 %copy-start.14 = (bf16[2,512,768]{2,1,0:T(8,128)(2,1)S(1)}, bf16[2,512,768]{2,1,0:T(8,128)(2,1)}, u32[]{:S(2)}) copy-start(bf16[2,512,768]{2,1,0:T(8,128)(2,1)} %get-tuple-element.1730) | copy-start | bytes 4718596 | tf_op jit(solution)/shard_map/while
  1125.6 26.8 %copy-start.36 = (bf16[3,768]{1,0:T(4,128)(2,1)S(1)}, bf16[3,768]{1,0:T(4,128)(2,1)}, u32[]{:S(2)}) copy-start(bf16[3,768]{1,0:T(4,128)(2,1)} %copy-done.35) | copy-start | bytes 13828 | tf_op jit(solution)/shard_map/while
  1125.6 26.8 %copy-start.43 = (bf16[3072]{0:T(1024)(128)(2,1)S(1)}, bf16[3072]{0:T(1024)(128)(2,1)}, u32[]{:S(2)}) copy-start(bf16[3072]{0:T(1024)(128)(2,1)} %copy-done.42) | copy-start | bytes 18436 | tf_op jit(solution)/shard_map/while
  1125.6 26.8 %copy-start.46 = (bf16[768]{0:T(1024)(128)(2,1)S(1)}, bf16[768]{0:T(1024)(128)(2,1)}, u32[]{:S(2)}) copy-start(bf16[768]{0:T(1024)(128)(2,1)} %copy-done.45) | copy-start | bytes 4612 | tf_op jit(solution)/shard_map/while
  1125.6 26.8 %copy-start.50 = (bf16[768]{0:T(1024)(128)(2,1)S(1)}, bf16[768]{0:T(1024)(128)(2,1)}, u32[]{:S(2)}) copy-start(bf16[768]{0:T(1024)(128)(2,1)} %copy-done.49) | copy-start | bytes 4612 | tf_op jit(solution)/shard_map/while
  1179.4 11.0 copy-start.22
  1201.3 7.6 copy-start.23
  1208.9 10.2 slice-start
  1208.9 11.4 slice-start.1
  1208.9 12.6 slice-start.2
  1310.3 21.8 %collective-permute-start.1 = (bf16[512,768]{1,0:T(8,128)(2,1)}, bf16[512,768]{1,0:T(8,128)(2,1)}, u32[]{:S(2)}, u32[]{:S(2)}) collective-permute-start(bf16[512,768]{1,0:T(8,128)(2,1)} %get-tuple-element.1612), channel_id=1, source_target_pairs={{8,0},{16,8},{24,16},{9,1},{17,9},{25,17},{10,2},{18,10},{26,18},{... | collective-permute-start | bytes 2359304 | tf_op jit(solution)/shard_map/while/body/eval_jaxpr/ppermute | solution.py:27
  1311.6 20.2 %copy-start.7 = (bf16[512,768]{1,0:T(8,128)(2,1)S(1)}, bf16[512,768]{1,0:T(8,128)(2,1)}, u32[]{:S(2)}) copy-start(bf16[512,768]{1,0:T(8,128)(2,1)} %get-tuple-element.1612) | copy-start | bytes 2359300 | tf_op jit(solution)/shard_map/while
  1311.6 20.2 %copy-start.14 = (bf16[2,512,768]{2,1,0:T(8,128)(2,1)S(1)}, bf16[2,512,768]{2,1,0:T(8,128)(2,1)}, u32[]{:S(2)}) copy-start(bf16[2,512,768]{2,1,0:T(8,128)(2,1)} %get-tuple-element.1730) | copy-start | bytes 4718596 | tf_op jit(solution)/shard_map/while
  1311.6 21.6 %copy-start.36 = (bf16[3,768]{1,0:T(4,128)(2,1)S(1)}, bf16[3,768]{1,0:T(4,128)(2,1)}, u32[]{:S(2)}) copy-start(bf16[3,768]{1,0:T(4,128)(2,1)} %copy-done.35) | copy-start | bytes 13828 | tf_op jit(solution)/shard_map/while
  1311.6 21.6 %copy-start.43 = (bf16[3072]{0:T(1024)(128)(2,1)S(1)}, bf16[3072]{0:T(1024)(128)(2,1)}, u32[]{:S(2)}) copy-start(bf16[3072]{0:T(1024)(128)(2,1)} %copy-done.42) | copy-start | bytes 18436 | tf_op jit(solution)/shard_map/while
  1311.6 21.6 %copy-start.46 = (bf16[768]{0:T(1024)(128)(2,1)S(1)}, bf16[768]{0:T(1024)(128)(2,1)}, u32[]{:S(2)}) copy-start(bf16[768]{0:T(1024)(128)(2,1)} %copy-done.45) | copy-start | bytes 4612 | tf_op jit(solution)/shard_map/while
  1311.6 21.6 %copy-start.50 = (bf16[768]{0:T(1024)(128)(2,1)S(1)}, bf16[768]{0:T(1024)(128)(2,1)}, u32[]{:S(2)}) copy-start(bf16[768]{0:T(1024)(128)(2,1)} %copy-done.49) | copy-start | bytes 4612 | tf_op jit(solution)/shard_map/while
  1341.5 285.9 %reduce-scatter.5.cloned.1.call-start = ((), (), s32[]{:S(2)}) async-start(), calls=%async_computation.3 | async-start | bytes 1966080 | tf_op jit(solution)/shard_map/reduce_scatter | solution.py:477
  1344.3 427.0 %all-reduce.12.cloned.1.call-start = ((), (), s32[]{:S(2)}) async-start(), calls=%async_computation.6 | async-start | bytes 7667712 | tf_op jit(solution)/shard_map/psum | solution.py:460
  1625.8 182.4 %reduce-scatter.3.cloned.1.call-start = ((), (), s32[]{:S(2)}) async-start(), calls=%async_computation.2 | async-start | bytes 1966080 | tf_op jit(solution)/shard_map/reduce_scatter | solution.py:474
  1771.3 7.9 copy-start.37
  1771.3 36.9 %copy-start.1 = (bf16[2,96,3072]{2,1,0:T(8,128)(2,1)S(1)}, bf16[2,96,3072]{2,1,0:T(8,128)(2,1)}, u32[]{:S(2)}) copy-start(bf16[2,96,3072]{2,1,0:T(8,128)(2,1)} %param.31) | copy-start | bytes 3538948
  (98 other events, 306.4 us)
Sparse Core Ops, SparseCore 0:
  56.5 141.7 all-reduce.7
  1341.6 242.0 all-reduce.9
  1586.7 35.2 reduce-scatter.4
  1625.9 145.3 all-reduce.11
  1774.0 34.1 reduce-scatter.2
where the time goes:
time: 1820 us
  waiting for transfers between devices  950 us (52%)
  local copies, waits for them, and re-layouts  322 us (18%)
  other arithmetic  258 us (14%)
  matrix products  126 us (7%)
  starting transfers between devices  79.3 us (4%)
  loops' own time  53 us (3%)
    ppermute x10, waiting for transfers between devices, shifted(): return lax.ppermute(array, axis, pairs)  429 us
    unnamed x7, waiting for transfers between devices  371 us
    psum x1, waiting for transfers between devices, shards(): lax.psum(qkv_part.astype(jnp.bfloat16), 'section').astype(jnp.float32)  122 us
    add x5, other arithmetic, backward_step(): accum = accum + grad_bundle  95.9 us
    ppermute x10, starting transfers between devices, shifted(): return lax.ppermute(array, axis, pairs)  78.9 us
    cond x128, local copies, waits for them, and re-layouts  61.2 us
    sub x4, other arithmetic, attention_parts(): powered = jnp.exp(masked - row_max)  43.7 us
    concatenate x2, local copies, waits for them, and re-layouts, grid_pad(): jnp.concatenate([joined, jnp.zeros((groups, bundle - joined.shape[1]), jn...  39.9 us
  transfers between devices with their start and end apart: 15, of which 13 were waited for; matrix products, arithmetic and copies ran while one was open for 10% of the time, Pallas kernels for 0%

commit v1 on v0

v1 whole, which is shorter than its diff:
```python
from functools import partial
import math

import jax
import jax.numpy as jnp
from jax import lax
from jax.experimental import pallas as pl
from jax.experimental.pallas import tpu as pltpu
from jax.sharding import PartitionSpec as P

HEAD_DIM = 64
PAIR = 2 * HEAD_DIM
EPSILON = 1e-06
NEGATIVE = -1e30
LOG2E = math.log2(math.e)
SCORE_SCALE = 1.0 / math.sqrt(3.0 * HEAD_DIM)
MESH = pl.DeviceIdType.MESH
BF = jnp.bfloat16
F32 = jnp.float32


def dot_nn(a, b):
    return jnp.dot(a, b, preferred_element_type=F32)


def dot_nt(a, b):
    return lax.dot_general(a, b, (((1,), (1,)), ((), ())), preferred_element_type=F32)


def dot_tn(a, b):
    return lax.dot_general(a, b, (((0,), (0,)), ((), ())), preferred_element_type=F32)


def gelu_and_slope(x):
    bell = jnp.exp2(x * x * (-0.5 * LOG2E))
    t = 1.0 / (1.0 + (0.3275911 / math.sqrt(2.0)) * jnp.abs(x))
    series = t * (
        0.254829592
        + t * (-0.284496736 + t * (1.421413741 + t * (-1.453152027 + t * 1.061405429)))
    )
    tail = 0.5 * series * bell
    cdf = jnp.where(x >= 0.0, 1.0 - tail, tail)
    return x * cdf, cdf + x * bell * (1.0 / math.sqrt(2.0 * math.pi))


def pipeline_kernel(
    rows,
    pages,
    cot,
    place,
    hide,
    wa,
    wb,
    vec,
    final_o,
    igrad_o,
    dwa_o,
    dwb_o,
    small_o,
    h_in,
    g_in,
    h_out,
    g_out,
    saved,
    qkvp,
    kplus,
    context,
    zed,
    rstd,
    db,
    dc,
    dy,
    fin_in,
    ig_in,
    stage,
    fsend,
    frecv,
    bsend,
    brecv,
    fin_send,
    fin_recv,
    ig_send,
    ig_recv,
    stage_sem,
):
    sections = lax.axis_size("section")
    s = lax.axis_index("section")
    last = sections - 1
    micro, length, width = h_in.shape
    hidden = wa.shape[1]
    chunks = length // rows
    quarter = length // sections
    per_chunk = rows // quarter
    pairs = width // PAIR
    is_attn = s % 2 == 0

    barrier = pltpu.get_barrier_semaphore()
    for by in range(1, sections):
        pl.semaphore_signal(
            barrier, inc=1, device_id={"section": (s + by) % sections}, device_id_type=MESH
        )
    pl.semaphore_wait(barrier, sections - 1)

    def local_in(source, target, sem, m, c):
        span = pl.ds(pl.multiple_of(c * rows, rows), rows)
        return pltpu.make_async_copy(source.at[m, span], target.at[m, span], sem.at[m, c])

    def hop(source, target, send, recv, m, c, by):
        span = pl.ds(pl.multiple_of(c * rows, rows), rows)
        return pltpu.make_async_remote_copy(
            src_ref=source.at[m, span],
            dst_ref=target.at[m, span],
            send_sem=send.at[m, c],
            recv_sem=recv.at[m, c],
            device_id={"section": (s + by + sections) % sections},
            device_id_type=MESH,
        )

    def share(source, target, send, recv, m, j):
        span = pl.ds(pl.multiple_of(j * quarter, quarter), quarter)
        return pltpu.make_async_remote_copy(
            src_ref=source.at[m, span],
            dst_ref=target.at[m],
            send_sem=send.at[m, j],
            recv_sem=recv.at[m],
            device_id={"section": j},
            device_id_type=MESH,
        )

    @pl.when(s == 0)
    def _():
        for m in range(micro):
            for c in range(chunks):
                local_in(pages, h_in, frecv, m, c).start()

    @pl.when(s == last)
    def _():
        for m in range(micro):
            for c in range(chunks):
                local_in(cot, g_in, brecv, m, c).start()

    def wait_h(m, c):
        @pl.when(s == 0)
        def _():
            local_in(pages, h_in, frecv, m, c).wait()

        @pl.when(s != 0)
        def _():
            hop(h_out, h_in, fsend, frecv, m, c, 1).wait_recv()

    def wait_g(m, c):
        @pl.when(s == last)
        def _():
            local_in(cot, g_in, brecv, m, c).wait()

        @pl.when(s != last)
        def _():
            hop(g_out, g_in, bsend, brecv, m, c, -1).wait_recv()

    def send_h(m, c):
        @pl.when(s != last)
        def _():
            hop(h_out, h_in, fsend, frecv, m, c, 1).start()

        @pl.when(s == last)
        def _():
            for i in range(per_chunk):
                j = c * per_chunk + i

                @pl.when(j != s)
                def _():
                    share(h_out, fin_in, fin_send, fin_recv, m, j).start()

    def send_g(m, c):
        @pl.when(s != 0)
        def _():
            hop(g_out, g_in, bsend, brecv, m, c, -1).start()

        @pl.when(s == 0)
        def _():
            for i in range(per_chunk):
                j = c * per_chunk + i

                @pl.when(j != s)
                def _():
                    share(g_out, ig_in, ig_send, ig_recv, m, j).start()

    def span_of(c):
        return pl.ds(pl.multiple_of(c * rows, rows), rows)

    def norm_out(m, c, summed, gain, offset):
        span = span_of(c)
        mean = jnp.mean(summed, axis=1, keepdims=True)
        center = summed - mean
        spread = jnp.mean(center * center, axis=1, keepdims=True)
        inv = lax.rsqrt(spread + EPSILON)
        z = center * inv
        zed[m, span] = z
        rstd[m, span] = jnp.broadcast_to(inv, (rows, 128))
        h_out[m, span] = (z * gain + offset).astype(BF)
        send_h(m, c)

    def norm_back(m, c, gain, gain_at, bias_at):
        span = span_of(c)
        g = g_in[m, span].astype(F32)
        z = zed[m, span]
        inv = rstd[m, span][:, :1]
        u = g * gain
        mean_u = jnp.mean(u, axis=1, keepdims=True)
        mean_uz = jnp.mean(u * z, axis=1, keepdims=True)
        grad = (u - mean_u - z * mean_uz) * inv
        low = grad.astype(BF)
        db[m, span] = low
        small_o[1:2, width : 2 * width] += jnp.sum(g * z, axis=0, keepdims=True)
        small_o[1:2, 2 * width : 3 * width] += jnp.sum(g, axis=0, keepdims=True)
        at = bias_at
        small_o[at[0] : at[0] + 1, at[1] : at[1] + width] += jnp.sum(
            low.astype(F32), axis=0, keepdims=True
        )
        return grad, low

    small_o[...] = jnp.zeros_like(small_o)
    gain = vec[1:2, width : 2 * width]
    offset = vec[1:2, 2 * width : 3 * width]

    def flush(source, at_rows, at_cols, target, slot):
        return pltpu.make_async_copy(
            source, target.at[pl.ds(at_rows, width), pl.ds(at_cols, width)], stage_sem.at[slot]
        )

    @pl.when(is_attn)
    def _():
        lane = lax.broadcasted_iota(jnp.int32, (1, PAIR), 1) < HEAD_DIM
        lane2 = lax.broadcasted_iota(jnp.int32, (1, 2 * PAIR), 1) % PAIR < HEAD_DIM

        def places(idx, _):
            m, c = idx // chunks, idx % chunks
            span = span_of(c)
            qkvp[m, span, 3 * width :] = dot_nn(place[m, span], wa[:, 3 * width :]).astype(BF)
            return 0

        lax.fori_loop(0, micro * chunks, places, 0)

        def forward(m, _):
            def project(c, _):
                span = span_of(c)
                wait_h(m, c)
                h = h_in[m, span]
                q = dot_nn(h, wa[:, :width]) + vec[0:1, :width]
                qkvp[m, span, :width] = q.astype(BF)
                k = dot_nn(h, wa[:, width : 2 * width]).astype(BF)
                qkvp[m, span, width : 2 * width] = k
                kplus[m, span] = (
                    k.astype(F32) + qkvp[m, span, 3 * width :].astype(F32)
                ).astype(BF)
                v = dot_nn(h, wa[:, 2 * width : 3 * width]) + vec[0:1, width : 2 * width]
                qkvp[m, span, 2 * width : 3 * width] = v.astype(BF)
                return 0

            lax.fori_loop(0, chunks, project, 0)

            def attend(c, _):
                span = span_of(c)

                def heads(t, _):
                    off = pl.multiple_of(t * PAIR, PAIR)
                    left = jnp.concatenate(
                        [
                            qkvp[m, span, pl.ds(off, PAIR)],
                            qkvp[m, span, pl.ds(off + 3 * width, PAIR)],
                        ],
                        axis=1,
                    )
                    right = jnp.concatenate(
                        [kplus[m, :, pl.ds(off, PAIR)], qkvp[m, :, pl.ds(off + width, PAIR)]],
                        axis=1,
                    )
                    v = qkvp[m, :, pl.ds(off + 2 * width, PAIR)]
                    bias = hide[m, span].astype(F32)
                    mixed = []
                    for side in range(2):
                        mask = lane2 if side == 0 else jnp.logical_not(lane2)
                        part = jnp.where(mask, left, jnp.zeros_like(left))
                        score = dot_nt(part, right) * (SCORE_SCALE * LOG2E) + bias
                        top = jnp.max(score, axis=1, keepdims=True)
                        power = jnp.exp2(score - top)
                        total = jnp.sum(power, axis=1, keepdims=True)
                        prob = (power * (1.0 / total)).astype(BF)
                        at = pl.multiple_of((2 * t + side) * length, length)
                        saved[m, span, pl.ds(at, length)] = prob
                        mixed.append(dot_nn(prob, v))
                    context[m, span, pl.ds(off, PAIR)] = jnp.where(
                        lane, mixed[0], mixed[1]
                    ).astype(BF)
                    return 0

                lax.fori_loop(0, pairs, heads, 0)
                branch = dot_nn(context[m, span], wb[:width, :])
                summed = h_in[m, span].astype(F32) + branch + vec[0:1, 2 * width : 3 * width]
                norm_out(m, c, summed, gain, offset)
                return 0

            lax.fori_loop(0, chunks, attend, 0)
            return 0

        lax.fori_loop(0, micro, forward, 0)

        def backward(m, _):
            def enter(c, _):
                span = span_of(c)
                wait_g(m, c)
                grad, low = norm_back(m, c, gain, None, (0, 2 * width))
                dy[span] = grad
                dc[span] = dot_nt(low, wb[:width, :]).astype(BF)
                return 0

            lax.fori_loop(0, chunks, enter, 0)

            def heads(t, _):
                off = pl.multiple_of(t * PAIR, PAIR)
                left = jnp.concatenate(
                    [qkvp[m, :, pl.ds(off, PAIR)], qkvp[m, :, pl.ds(off + 3 * width, PAIR)]],
                    axis=1,
                )
                right = jnp.concatenate(
                    [kplus[m, :, pl.ds(off, PAIR)], qkvp[m, :, pl.ds(off + width, PAIR)]],
                    axis=1,
                )
                v = qkvp[m, :, pl.ds(off + 2 * width, PAIR)]
                grad_c = dc[:, pl.ds(off, PAIR)]
                got = []
                for side in range(2):
                    mask = lane if side == 0 else jnp.logical_not(lane)
                    at = pl.multiple_of((2 * t + side) * length, length)
                    prob = saved[m, :, pl.ds(at, length)]
                    wide_p = prob.astype(F32)
                    grad_p = dot_nt(jnp.where(mask, grad_c, jnp.zeros_like(grad_c)), v)
                    dot_row = jnp.sum(wide_p * grad_p, axis=1, keepdims=True)
                    grad_s = (wide_p * (grad_p - dot_row)).astype(BF)
                    got.append(
                        (dot_tn(prob, grad_c), dot_nn(grad_s, right), dot_tn(grad_s, left))
                    )
                grad_v = jnp.where(lane, got[0][0], got[1][0]).astype(BF)
                grad_l = jnp.where(lane2, got[0][1], got[1][1])
                grad_r = jnp.where(lane2, got[0][2], got[1][2])
                grad_q = (grad_l[:, :PAIR] * SCORE_SCALE).astype(BF)
                grad_k = ((grad_r[:, :PAIR] + grad_r[:, PAIR:]) * SCORE_SCALE).astype(BF)
                grad_pl = ((grad_l[:, PAIR:] + grad_r[:, :PAIR]) * SCORE_SCALE).astype(BF)
                qkvp[m, :, pl.ds(off, PAIR)] = grad_q
                qkvp[m, :, pl.ds(off + width, PAIR)] = grad_k
                qkvp[m, :, pl.ds(off + 2 * width, PAIR)] = grad_v
                qkvp[m, :, pl.ds(off + 3 * width, PAIR)] = grad_pl
                small_o[0:1, pl.ds(off, PAIR)] += jnp.sum(
                    grad_q.astype(F32), axis=0, keepdims=True
                )
                small_o[0:1, pl.ds(off + width, PAIR)] += jnp.sum(
                    grad_v.astype(F32), axis=0, keepdims=True
                )
                return 0

            lax.fori_loop(0, pairs, heads, 0)

            def leave(c, _):
                span = span_of(c)
                total = dy[span] + dot_nt(qkvp[m, span, : 3 * width], wa[:, : 3 * width])
                g_out[m, span] = total.astype(BF)
                send_g(m, c)
                return 0

            lax.fori_loop(0, chunks, leave, 0)
            return 0

        lax.fori_loop(0, micro, backward, 0)

    blocks = hidden // width

    @pl.when(jnp.logical_not(is_attn))
    def _():
        def forward(idx, _):
            m, c = idx // chunks, idx % chunks
            span = span_of(c)
            wait_h(m, c)
            h = h_in[m, span]
            summed = h.astype(F32) + vec[1:2, :width]
            for f in range(blocks):
                at = f * width
                inner = dot_nn(h, wa[:, at : at + width]) + vec[0:1, at : at + width]
                value, slope = gelu_and_slope(inner)
                low = value.astype(BF)
                saved[m, span, at : at + width] = low
                saved[m, span, hidden + at : hidden + at + width] = slope.astype(BF)
                summed = summed + dot_nn(low, wb[at : at + width, :])
            norm_out(m, c, summed, gain, offset)
            return 0

        lax.fori_loop(0, micro * chunks, forward, 0)

        def backward(idx, _):
            m, c = idx // chunks, idx % chunks
            span = span_of(c)
            wait_g(m, c)
            total, low = norm_back(m, c, gain, None, (1, 0))
            for f in range(blocks):
                at = f * width
                grad_a = dot_nt(low, wb[at : at + width, :]).astype(BF).astype(F32)
                slope = saved[m, span, hidden + at : hidden + at + width].astype(F32)
                grad_i = (grad_a * slope).astype(BF)
                saved[m, span, hidden + at : hidden + at + width] = grad_i
                small_o[0:1, at : at + width] += jnp.sum(
                    grad_i.astype(F32), axis=0, keepdims=True
                )
                total = total + dot_nt(grad_i, wa[:, at : at + width])
            g_out[m, span] = total.astype(BF)
            send_g(m, c)
            return 0

        lax.fori_loop(0, micro * chunks, backward, 0)

    tokens = micro * length

    def tall(ref, at):
        return ref[:, :, pl.ds(at, width)].reshape(tokens, width)

    def put(value, slot, at_rows, at_cols, target):
        stage[slot] = value.astype(BF)
        flush(stage.at[slot], at_rows, at_cols, target, slot).start()

    def drain(slot):
        flush(stage.at[slot], 0, 0, dwa_o, slot).wait()

    def write_all(n, value_of, target, by_rows):
        def step(i, _):
            slot = i % 2

            @pl.when(i >= 2)
            def _():
                drain(slot)

            at = pl.multiple_of(i * width, width)
            if by_rows:
                put(value_of(at), slot, at, 0, target)
            else:
                put(value_of(at), slot, 0, at, target)
            return 0

        lax.fori_loop(0, n, step, 0)
        for i in range(max(n - 2, 0), n):
            drain(i % 2)

    @pl.when(is_attn)
    def _():
        write_all(3, lambda at: dot_tn(tall(h_in, 0), tall(qkvp, at)), dwa_o, False)
        put(dot_tn(tall(place, 0), tall(qkvp, 3 * width)), 0, 0, 3 * width, dwa_o)
        put(dot_tn(tall(context, 0), tall(db, 0)), 1, 0, 0, dwb_o)
        drain(0)
        drain(1)

    @pl.when(jnp.logical_not(is_attn))
    def _():
        write_all(
            blocks,
            lambda at: dot_tn(tall(h_in, 0), tall(saved, pl.multiple_of(at + hidden, width))),
            dwa_o,
            False,
        )
        write_all(blocks, lambda at: dot_tn(tall(saved, at), tall(db, 0)), dwb_o, True)

    for m in range(micro):
        for c in range(chunks):

            @pl.when(s != last)
            def _():
                hop(h_out, h_in, fsend, frecv, m, c, 1).wait_send()

            @pl.when(s != 0)
            def _():
                hop(g_out, g_in, bsend, brecv, m, c, -1).wait_send()

    @pl.when(s == last)
    def _():
        for m in range(micro):
            for j in range(sections - 1):
                share(h_out, fin_in, fin_send, fin_recv, m, j).wait_send()
            final_o[m] = h_out[m, (sections - 1) * quarter :]

    @pl.when(s != last)
    def _():
        for m in range(micro):
            share(h_out, fin_in, fin_send, fin_recv, m, 0).wait_recv()
            final_o[m] = fin_in[m]

    @pl.when(s == 0)
    def _():
        for m in range(micro):
            for j in range(1, sections):
                share(g_out, ig_in, ig_send, ig_recv, m, j).wait_send()
            igrad_o[m] = g_out[m, :quarter].astype(F32)

    @pl.when(s != 0)
    def _():
        for m in range(micro):
            share(g_out, ig_in, ig_send, ig_recv, m, 1).wait_recv()
            igrad_o[m] = ig_in[m].astype(F32)


def pipeline(pages, cot, place, hide, wa, wb, vec):
    micro, length, width = pages.shape
    hidden = wa.shape[1]
    sections = lax.axis_size("section")
    rows = length // 2
    chunks = length // rows
    quarter = length // sections
    heads = width // HEAD_DIM
    wide = max(2 * hidden, heads * length)
    hbm = pl.BlockSpec(memory_space=pl.ANY)
    vmem = pl.BlockSpec(memory_space=pltpu.VMEM)
    act = (micro, length, width)
    dma = pltpu.SemaphoreType.DMA
    return pl.pallas_call(
        partial(pipeline_kernel, rows),
        out_shape=(
            jax.ShapeDtypeStruct((micro, quarter, width), BF),
            jax.ShapeDtypeStruct((micro, quarter, width), F32),
            jax.ShapeDtypeStruct((width, hidden), BF),
            jax.ShapeDtypeStruct((hidden, width), BF),
            jax.ShapeDtypeStruct((8, hidden), F32),
        ),
        in_specs=[hbm, hbm, vmem, vmem, vmem, vmem, vmem],
        out_specs=(vmem, vmem, hbm, hbm, vmem),
        scratch_shapes=[
            pltpu.VMEM(act, BF),
            pltpu.VMEM(act, BF),
            pltpu.VMEM(act, BF),
            pltpu.VMEM(act, BF),
            pltpu.VMEM((micro, length, wide), BF),
            pltpu.VMEM((micro, length, 4 * width), BF),
            pltpu.VMEM(act, BF),
            pltpu.VMEM(act, BF),
            pltpu.VMEM(act, F32),
            pltpu.VMEM((micro, length, 128), F32),
            pltpu.VMEM(act, BF),
            pltpu.VMEM((length, width), BF),
            pltpu.VMEM((length, width), F32),
            pltpu.VMEM((micro, quarter, width), BF),
            pltpu.VMEM((micro, quarter, width), BF),
            pltpu.VMEM((2, width, width), BF),
            dma((micro, chunks)),
            dma((micro, chunks)),
            dma((micro, chunks)),
            dma((micro, chunks)),
            dma((micro, sections)),
            dma((micro,)),
            dma((micro, sections)),
            dma((micro,)),
            dma((2,)),
        ],
        compiler_params=pltpu.CompilerParams(
            collective_id=0, has_side_effects=True, vmem_limit_bytes=63 * 1024 * 1024
        ),
        name="pipeline",
    )(pages, cot, place, hide, wa, wb, vec)


def sinusoid(coord_pair, model_width):
    quarter = model_width // 4
    frequency = jnp.exp(jnp.arange(quarter, dtype=F32) * (-math.log(10000.0) / quarter))
    angles = coord_pair.astype(F32)[:, :, :, None] * frequency
    waves = jnp.stack([jnp.sin(angles), jnp.cos(angles)], axis=3)
    pages, axes, length = coord_pair.shape
    return waves.transpose(0, 2, 1, 3, 4).reshape(pages, length, model_width).astype(BF)


def hidden_bias(boxes, length):
    spots = jnp.arange(length, dtype=jnp.int32)
    row_hit = (spots >= boxes[:, :, 0:1]) & (spots < boxes[:, :, 1:2])
    col_hit = (spots >= boxes[:, :, 2:3]) & (spots < boxes[:, :, 3:4])
    covered = jnp.einsum(
        "pbi,pbj->pij", row_hit.astype(BF), col_hit.astype(BF), preferred_element_type=F32
    )
    return jnp.where(covered < 0.5, 0.0, NEGATIVE).astype(BF)


def shards(
    pages_in,
    coords,
    boxes,
    qkv_weight,
    attn_bias,
    pos_weight,
    out_weight,
    ffn_in,
    ffn_in_bias,
    ffn_out,
    ffn_out_bias,
    ln_gain,
    ln_bias,
    cotangent,
):
    groups = lax.axis_size("dp")
    s = lax.axis_index("section")
    layer = s // 2
    is_attn = s % 2 == 0
    micro, length, width = pages_in.shape
    hidden = ffn_in.shape[2]
    part = width // groups
    part_h = hidden // groups

    def pick(array):
        return lax.dynamic_index_in_dim(array, layer, 0, keepdims=False)

    own_a = jnp.where(
        is_attn, jnp.concatenate([pick(qkv_weight), pick(pos_weight)], axis=1), pick(ffn_in)
    )
    own_b = jnp.where(
        is_attn, jnp.pad(pick(out_weight), ((0, part_h - part), (0, 0))), pick(ffn_out)
    )
    wa = lax.all_gather(own_a, "dp", axis=0, tiled=True)
    wb_all = lax.all_gather(own_b, "dp", axis=0, tiled=False)
    wb = jnp.where(
        is_attn,
        jnp.pad(wb_all[:, :part].reshape(width, width), ((0, hidden - width), (0, 0))),
        wb_all.reshape(hidden, width),
    )

    norm_row = jnp.where(is_attn, 0, 1)
    gain_own = lax.dynamic_index_in_dim(pick(ln_gain), norm_row, 0, keepdims=False)
    offset_own = lax.dynamic_index_in_dim(pick(ln_bias), norm_row, 0, keepdims=False)
    bias_own = jnp.where(
        is_attn,
        jnp.pad(pick(attn_bias).reshape(-1), (0, part_h - 3 * part)),
        pick(ffn_in_bias),
    )
    vec_own = jnp.concatenate([bias_own, pick(ffn_out_bias), gain_own, offset_own])
    vec_all = lax.all_gather(vec_own, "dp", axis=0, tiled=False).astype(F32)
    first = jnp.where(
        is_attn,
        jnp.pad(
            vec_all[:, : 3 * part].reshape(groups, 3, part).transpose(1, 0, 2).reshape(-1),
            (0, hidden - 3 * width),
        ),
        vec_all[:, :part_h].reshape(-1),
    )
    rest = vec_all[:, part_h:].reshape(groups, 3, part).transpose(1, 0, 2).reshape(-1)
    vec = jnp.pad(
        jnp.stack([first, jnp.pad(rest, (0, hidden - 3 * width))]), ((0, 6), (0, 0))
    )

    place = sinusoid(coords, width)
    hide = hidden_bias(boxes, length)

    final, igrad, dwa, dwb, small = pipeline(pages_in, cotangent, place, hide, wa, wb, vec)

    shard_a = lax.psum_scatter(dwa, "dp", scatter_dimension=0, tiled=True)
    dwb_cut = jnp.where(
        is_attn,
        jnp.pad(
            dwb[:width].reshape(groups, part, width), ((0, 0), (0, part_h - part), (0, 0))
        ),
        dwb.reshape(groups, part_h, width),
    )
    shard_b = lax.psum_scatter(dwb_cut, "dp", scatter_dimension=0, tiled=True).reshape(
        part_h, width
    )
    small_first = jnp.where(
        is_attn,
        jnp.pad(
            small[0, : 3 * width].reshape(3, groups, part).transpose(1, 0, 2).reshape(groups, -1),
            ((0, 0), (0, part_h - 3 * part)),
        ),
        small[0].reshape(groups, part_h),
    )
    small_rest = (
        small[1, : 3 * width].reshape(3, groups, part).transpose(1, 0, 2).reshape(groups, -1)
    )
    small_cut = jnp.concatenate([small_first, small_rest], axis=1)
    shard_s = lax.psum_scatter(small_cut, "dp", scatter_dimension=0, tiled=True).reshape(-1)

    all_a = lax.all_gather(shard_a, "section", axis=0, tiled=False)
    all_b = lax.all_gather(shard_b, "section", axis=0, tiled=False)
    all_s = lax.all_gather(shard_s, "section", axis=0, tiled=False)

    attn_a, feed_a = all_a[0::2], all_a[1::2]
    attn_s, feed_s = all_s[0::2], all_s[1::2]
    rest_s = all_s[:, part_h:].reshape(-1, 2, 3, part)
    return (
        final,
        igrad,
        attn_a[:, :, : 3 * width].astype(F32),
        attn_s[:, : 3 * part].reshape(-1, 3, part),
        attn_a[:, :, 3 * width :].astype(F32),
        all_b[0::2, :part].astype(F32),
        feed_a.astype(F32),
        feed_s[:, :part_h],
        all_b[1::2].astype(F32),
        feed_s[:, part_h : part_h + part],
        rest_s[:, :, 1],
        rest_s[:, :, 2],
    )


def solution(mesh):
    in_specs = (
        P("dp", None, None),
        P("dp", None, None),
        P("dp", None, None),
        P(None, "dp", None),
        P(None, None, "dp"),
        P(None, "dp", None),
        P(None, "dp", None),
        P(None, "dp", None),
        P(None, "dp"),
        P(None, "dp", None),
        P(None, "dp"),
        P(None, None, "dp"),
        P(None, None, "dp"),
        P("dp", None, None),
    )
    out_specs = (
        P("dp", "section", None),
        P("dp", "section", None),
        P(None, "dp", None),
        P(None, None, "dp"),
        P(None, "dp", None),
        P(None, "dp", None),
        P(None, "dp", None),
        P(None, "dp"),
        P(None, "dp", None),
        P(None, "dp"),
        P(None, None, "dp"),
        P(None, None, "dp"),
    )
    return jax.shard_map(shards, mesh=mesh, in_specs=in_specs, out_specs=out_specs, check_vma=False)
```

time: 1820 us -> 529 us (0.29)
  waiting for transfers between devices: 950 us -> 202 us
  local copies, waits for them, and re-layouts: 322 us -> 14 us
  other arithmetic: 258 us -> 26.4 us
  Pallas kernels: 0 us -> 206 us
  matrix products: 126 us -> 1.58 us
  starting transfers between devices: 79.3 us -> 0.24 us
  loops' own time: 53 us -> 0 us
  blocking collectives: 12.4 us -> 63 us
    ppermute x10 -> x0, waiting for transfers between devices: 429 us -> none  [shifted(): return lax.ppermute(array, axis, pairs)]
    unnamed x7 -> x6, waiting for transfers between devices: 371 us -> 0.1 us
    pallas_call x0 -> x1, Pallas kernels: none -> 206 us  [pipeline(): pl.pallas_call(partial(pipeline_kernel, rows), out_shape=(jax.ShapeDtypeS...]
    dot_general x42 -> x1, matrix products: 126 us -> 1.58 us  [hidden_bias(): jnp.einsum('pbi,pbj->pij', row_hit.astype(BF), col_hit.astype(BF), prefer...]
    psum x1 -> x0, waiting for transfers between devices: 122 us -> none  [shards(): lax.psum(qkv_part.astype(jnp.bfloat16), 'section').astype(jnp.float32)]
    add x9 -> x0, other arithmetic: 96 us -> none  [the longest x5 95.9 us: backward_step(): accum = accum + grad_bundle]
    all_gather x0 -> x4, waiting for transfers between devices: none -> 94 us  [the longest x1 45.2 us: shards(): all_b = lax.all_gather(shard_b, 'section', axis=0, tiled=False)]
    reduce_scatter x2, waiting for transfers between devices: 27.4 us -> 108 us  [the longest x1 57.5 us: shards(): lax.psum_scatter(dwb_cut, 'dp', scatter_dimension=0, tiled=True)]
  transfers between devices with their start and end apart: 15 -> 6, of which waited for: 13 -> 6; matrix products, arithmetic and copies ran while one was open for 10% -> 6% of each run, Pallas kernels for 0% -> 0%
where the time goes in v1:
time: 529 us
  Pallas kernels  206 us (39%)
  waiting for transfers between devices  202 us (38%)
  blocking collectives  63 us (12%)
  other arithmetic  26.4 us (5%)
  between operations  15.2 us (3%)
  local copies, waits for them, and re-layouts  14 us (3%)
    pallas_call x1, Pallas kernels, pipeline(): pl.pallas_call(partial(pipeline_kernel, rows), out_shape=(jax.ShapeDtypeS...  206 us
    reduce_scatter x1, waiting for transfers between devices, shards(): lax.psum_scatter(dwb_cut, 'dp', scatter_dimension=0, tiled=True)  57.5 us
    reduce_scatter x1, waiting for transfers between devices, shards(): shard_a = lax.psum_scatter(dwa, 'dp', scatter_dimension=0, tiled=True)  50.4 us
    unnamed x2, blocking collectives  49.7 us
    all_gather x1, waiting for transfers between devices, shards(): all_b = lax.all_gather(shard_b, 'section', axis=0, tiled=False)  45.2 us
    all_gather x1, waiting for transfers between devices, shards(): wa = lax.all_gather(own_a, 'dp', axis=0, tiled=True)  37 us
    all_gather x1, blocking collectives, shards(): all_s = lax.all_gather(shard_s, 'section', axis=0, tiled=False)  13.3 us
  transfers between devices with their start and end apart: 6, of which 6 were waited for; matrix products, arithmetic and copies ran while one was open for 6% of the time, Pallas kernels for 0%

profile of v1, /device:TPU:0, one launch (start us, length us, event | category | flops | bytes accessed | tf_op | source)
XLA Modules:
  0.0 528.7 jit_solution(614998696703208173)
XLA Ops:
  7.2 0.0 copy-start
  7.2 0.0 all-gather.13.cloned.1.call-start
  7.3 1.1 dynamic-slice_bitcast_fusion.1
  8.4 2.0 bitcast_select_fusion
  10.4 0.0 all-gather.13.cloned.1.call-update
  10.5 0.0 all-gather.9.cloned.1.call-start
  10.6 1.0 maximum_select_fusion
  11.6 0.0 all-gather.9.cloned.1.call-update
  11.6 0.0 reduce-scatter.3.cloned.1.call-start
  11.7 0.1 reshape.90
  11.8 0.6 fusion.18
  13.2 0.1 pad_maximum_fusion.2
  13.3 0.2 dynamic-update-slice
  13.5 25.8 %all-reduce.8 = bf16[5376]{0:T(1024)(128)(2,1)S(1)} all-reduce(bf16[5376]{0:T(1024)(128)(2,1)S(1)} %dynamic-update-slice), channel_id=3, replica_groups=mesh['section'=4,'dp'=8] {'dp'}, use_global_device_ids=true, to_apply=%add.8 | all-reduce | flops 5376 | bytes 21504
  39.3 0.1 reshape.105
  39.4 0.1 reshape.91
  39.5 0.1 reshape.92
  39.6 0.1 reshape.94
  39.6 0.1 reshape.95
  39.7 6.1 %fusion = (bf16[2,2,512,1,192]{2,4,3,1,0:T(8,128)(2,1)S(1)}, bf16[2,2,512,1,192]{2,4,3,1,0:T(8,128)(2,1)S(1)}) fusion(f32[192]{0:T(256)S(1)} %multiply_exponential_fusion, f32[2,2,512]{2,1,0:T(2,128)S(1)} %convert_element_type.46), kind=kLoop, calls=%fused_computation.5 | loop fusion | flops 1179648 | bytes 1581824 | tf_op jit(solution)/shard_map/convert
  45.8 0.1 pad_maximum_fusion
  46.0 1.6 copy.36.place
  47.6 1.6 select_convert_fusion.hide
  49.2 0.7 select_maximum_fusion.vec
  49.8 2.4 all-gather.13.cloned.1.call-done
  52.2 1.3 slice.104
  53.6 3.0 pad_select_fusion.1.wb
  56.6 37.0 %all-gather.9.cloned.1.call-done.wa = bf16[768,3072]{1,0:T(8,128)(2,1)} async-done(((bf16[96,3072]{1,0:T(8,128)(2,1)}), bf16[768,3072]{1,0:T(8,128)(2,1)}) %all-gather.9.cloned.1.call-update) | async-done | bytes 4718608 | tf_op jit(solution)/shard_map/all_gather | solution.py:617
  93.6 206.4 %pipeline.1 = (bf16[2,128,768]{2,1,0:T(8,128)(2,1)}, f32[2,128,768]{2,1,0:T(8,128)}, bf16[768,3072]{1,0:T(8,128)(2,1)}, bf16[3072,768]{1,0:T(8,128)(2,1)}, f32[8,3072]{1,0:T(8,128)}) custom-call(bf16[2,512,768]{2,1,0:T(8,128)(2,1)} %pages.1, bf16[2,512,768]{2,1,0:T(8,128)(2,1)} %cot.1, bf16[2,512,768]{2,1,0:T(8,128)(2,1)} %copy.36.place, ...), custom_call_target="tpu_custom_call" | custom-call | tf_op jit(solution)/shard_map/pipeline/pallas_call | solution.py:519
  300.0 0.0 reduce-scatter.3.cloned.1.call-update
  300.1 0.0 reduce-scatter.5.cloned.1.call-start
  300.1 1.3 slice.94
  301.5 3.1 pad_select_fusion
  304.6 0.0 reduce-scatter.5.cloned.1.call-update
  304.6 0.0 all-gather.15.cloned.1.call-start
  304.6 50.4 %reduce-scatter.3.cloned.1.call-done = bf16[96,3072]{1,0:T(8,128)(2,1)} async-done(((bf16[768,3072]{1,0:T(8,128)(2,1)}), bf16[96,3072]{1,0:T(8,128)(2,1)}) %reduce-scatter.3.cloned.1.call-update) | async-done | bytes 589840 | tf_op jit(solution)/shard_map/reduce_scatter | solution.py:653
  355.0 0.0 all-gather.15.cloned.1.call-update
  355.1 0.0 all-gather.11.cloned.1.call-start
  355.1 57.5 %reduce-scatter.5.cloned.1.call-done = bf16[1,384,768]{2,1,0:T(8,128)(2,1)} async-done(((bf16[8,384,768]{2,1,0:T(8,128)(2,1)}), bf16[1,384,768]{2,1,0:T(8,128)(2,1)}) %reduce-scatter.5.cloned.1.call-update) | async-done | bytes 589840 | tf_op jit(solution)/shard_map/reduce_scatter | solution.py:661
  412.6 0.0 all-gather.11.cloned.1.call-update
  412.7 1.0 slice_reduce_fusion.2
  413.7 0.1 reshape_squeeze.9
  413.7 0.9 slice_reduce_fusion
  414.7 0.1 reshape.96
  414.8 0.1 reshape_squeeze.11
  414.9 0.1 reshape.97
  415.0 23.9 %all-reduce.9 = f32[8,672]{1,0:T(8,128)S(1)} all-reduce(f32[8,672]{1,0:T(8,128)S(1)} %pad_maximum_fusion.1), channel_id=6, replica_groups=mesh['section'=4,'dp'=8] {'dp'}, use_global_device_ids=true, to_apply=%region_1.2.clone | all-reduce | flops 5376 | bytes 43008
  438.8 0.7 dynamic-slice_bitcast_fusion.3
  439.5 13.3 %all-gather.3 = f32[4,1,672]{2,1,0:T(1,128)S(1)} all-gather(f32[1,1,672]{2,1,0:T(1,128)S(1)} %dynamic-slice_bitcast_fusion.3), channel_id=1, replica_groups=mesh['section'=4,'dp'=8] {'section'}, dimensions={0}, use_global_device_ids=true | all-gather | bytes 13440 | tf_op jit(solution)/shard_map/all_gather | solution.py:680
  452.8 0.6 slice.112
  453.4 0.6 slice.111
  454.0 0.1 reshape.98
  454.1 0.6 copy.39
  454.7 0.1 reshape.101
  454.7 0.6 fusion.16
  455.3 9.4 %all-gather.15.cloned.1.call-done = bf16[384,3072]{1,0:T(8,128)(2,1)} async-done(((bf16[96,3072]{1,0:T(8,128)(2,1)}), bf16[384,3072]{1,0:T(8,128)(2,1)}) %all-gather.15.cloned.1.call-update) | async-done | bytes 2359312 | tf_op jit(solution)/shard_map/all_gather | solution.py:678
  464.7 3.4 slice_convert_fusion.1
  468.1 0.9 slice_convert_fusion.3
  468.9 1.3 slice_convert_fusion.2
  470.2 45.2 %all-gather.11.cloned.1.call-done = bf16[4,384,768]{2,1,0:T(8,128)(2,1)} async-done(((bf16[1,384,768]{2,1,0:T(8,128)(2,1)}), bf16[4,384,768]{2,1,0:T(8,128)(2,1)}) %all-gather.11.cloned.1.call-update) | async-done | bytes 2359312 | tf_op jit(solution)/shard_map/all_gather | solution.py:679
  515.5 1.8 slice_convert_fusion.4
  517.3 2.9 slice_convert_fusion
  520.2 0.7 copy.50
  521.0 0.9 copy.51
  (53 shorter events, 0.4 us)
Async XLA Ops:
  7.2 3.4 copy-start
  7.2 3.3 copy-start.4
  7.2 3.4 copy-start.3
  7.2 45.0 %all-gather.13.cloned.1.call-start = ((), (), s32[]{:S(2)}) async-start(), calls=%async_computation.6 | async-start | bytes 5308416 | tf_op jit(solution)/shard_map/all_gather | solution.py:618
  10.4 1.3 copy-start.8
  10.4 1.4 copy-start.5
  10.4 1.4 copy-start.7
  10.4 2.7 copy-start.9
  10.4 2.7 copy-start.12
  10.4 2.7 copy-start.10
  10.4 2.7 copy-start.11
  10.5 83.1 %all-gather.9.cloned.1.call-start = ((), (), s32[]{:S(2)}) async-start(), calls=%async_computation.2 | async-start | bytes 5308416 | tf_op jit(solution)/shard_map/all_gather | solution.py:617
  11.6 343.4 %reduce-scatter.3.cloned.1.call-start = ((), (), s32[]{:S(2)}) async-start(), calls=%async_computation.3 | async-start | bytes 5308416 | tf_op jit(solution)/shard_map/reduce_scatter | solution.py:653
  46.0 1.6 copy-start.6
  300.1 112.6 %reduce-scatter.5.cloned.1.call-start = ((), (), s32[]{:S(2)}) async-start(), calls=%async_computation.4 | async-start | bytes 5308416 | tf_op jit(solution)/shard_map/reduce_scatter | solution.py:661
  304.6 160.1 %all-gather.15.cloned.1.call-start = ((), (), s32[]{:S(2)}) async-start(), calls=%async_computation.7 | async-start | bytes 2949120 | tf_op jit(solution)/shard_map/all_gather | solution.py:678
  355.1 160.4 %all-gather.11.cloned.1.call-start = ((), (), s32[]{:S(2)}) async-start(), calls=%async_computation.5 | async-start | bytes 2949120 | tf_op jit(solution)/shard_map/all_gather | solution.py:679
  517.3 2.9 copy-start.2
  517.3 3.7 copy-start.1
Sparse Core Ops, SparseCore 0:
  10.5 41.6 all-gather.12
  54.7 38.8 all-gather.8
  300.2 54.8 reduce-scatter.2
  358.7 53.8 reduce-scatter.4
  414.0 50.6 all-gather.14
  466.1 49.2 all-gather.10

commit v2 on v1

--- a/solution.py
+++ b/solution.py
@@ -43,124 +43,130 @@
     return x * cdf, cdf + x * bell * (1.0 / math.sqrt(2.0 * math.pi))
 
 
-def pipeline_kernel(
-    rows,
-    pages,
-    cot,
-    place,
-    hide,
-    wa,
-    wb,
-    vec,
-    final_o,
-    igrad_o,
-    dwa_o,
-    dwb_o,
-    small_o,
-    h_in,
-    g_in,
-    h_out,
-    g_out,
-    saved,
-    qkvp,
-    kplus,
-    context,
-    zed,
-    rstd,
-    db,
-    dc,
-    dy,
-    fin_in,
-    ig_in,
-    stage,
-    fsend,
-    frecv,
-    bsend,
-    brecv,
-    fin_send,
-    fin_recv,
-    ig_send,
-    ig_recv,
-    stage_sem,
-):
+class Refs:
+    def __init__(self, names, refs):
+        self.__dict__.update(zip(names, refs, strict=True))
+
+
+def pipeline_kernel(names, rows, fused, *refs):
+    r = Refs(names, refs)
+    h_in, g_in, h_out, g_out = r.h_in, r.g_in, r.h_out, r.g_out
+    saved, qkvp, kplus, context, zed, rstd = r.saved, r.qkvp, r.kplus, r.context, r.zed, r.rstd
+    db, dc, dy, w, place, hide = r.db, r.dc, r.dy, r.w, r.place, r.hide
+    vec, colsum = r.vec, r.colsum
     sections = lax.axis_size("section")
     s = lax.axis_index("section")
+    kind = s % 2
+    layer = s // 2
     last = sections - 1
     micro, length, width = h_in.shape
-    hidden = wa.shape[1]
+    hidden = w.shape[0] // 2
     chunks = length // rows
     quarter = length // sections
     per_chunk = rows // quarter
     pairs = width // PAIR
-    is_attn = s % 2 == 0
+    blocks = hidden // width
+    is_attn = kind == 0
+    is_feed = kind == 1
+
+    if fused:
+        d = lax.axis_index("dp")
+        part = width // 8
+        half = part // 2
+        core, cx, cy = d % 2, (d // 2) % 2, d // 4
+        chip = d // 2
+        near_c = d + 1 - 2 * core
+        near_x = d + 2 - 4 * cx
+        near_y = d + 4 - 8 * cy
+        diag = near_x + 4 - 8 * cy
+        units = 5 + 3 * kind
+        tail_units = 1 + 3 * kind
 
     barrier = pltpu.get_barrier_semaphore()
     for by in range(1, sections):
         pl.semaphore_signal(
             barrier, inc=1, device_id={"section": (s + by) % sections}, device_id_type=MESH
         )
-    pl.semaphore_wait(barrier, sections - 1)
+    if fused:
+        for near in (near_c, near_x, near_y):
+            pl.semaphore_signal(barrier, inc=1, device_id={"dp": near}, device_id_type=MESH)
+    pl.semaphore_wait(barrier, sections - 1 + (3 if fused else 0))
+
+    def to_section(source, target, send, recv, at):
+        return pltpu.make_async_remote_copy(
+            src_ref=source,
+            dst_ref=target,
+            send_sem=send,
+            recv_sem=recv,
+            device_id={"section": at},
+            device_id_type=MESH,
+        )
+
+    def to_near(source, target, send, recv, near):
+        return pltpu.make_async_remote_copy(
+            src_ref=source,
+            dst_ref=target,
+            send_sem=send,
+            recv_sem=recv,
+            device_id={"dp": near},
+            device_id_type=MESH,
+        )
+
+    def span_of(c):
+        return pl.ds(pl.multiple_of(c * rows, rows), rows)
 
     def local_in(source, target, sem, m, c):
-        span = pl.ds(pl.multiple_of(c * rows, rows), rows)
+        span = span_of(c)
         return pltpu.make_async_copy(source.at[m, span], target.at[m, span], sem.at[m, c])
 
     def hop(source, target, send, recv, m, c, by):
-        span = pl.ds(pl.multiple_of(c * rows, rows), rows)
-        return pltpu.make_async_remote_copy(
-            src_ref=source.at[m, span],
-            dst_ref=target.at[m, span],
-            send_sem=send.at[m, c],
-            recv_sem=recv.at[m, c],
-            device_id={"section": (s + by + sections) % sections},
-            device_id_type=MESH,
+        span = span_of(c)
+        return to_section(
+            source.at[m, span],
+            target.at[m, span],
+            send.at[m, c],
+            recv.at[m, c],
+            (s + by + sections) % sections,
         )
 
     def share(source, target, send, recv, m, j):
         span = pl.ds(pl.multiple_of(j * quarter, quarter), quarter)
-        return pltpu.make_async_remote_copy(
-            src_ref=source.at[m, span],
-            dst_ref=target.at[m],
-            send_sem=send.at[m, j],
-            recv_sem=recv.at[m],
-            device_id={"section": j},
-            device_id_type=MESH,
-        )
+        return to_section(source.at[m, span], target.at[m], send.at[m, j], recv.at[m], j)
 
     @pl.when(s == 0)
     def _():
         for m in range(micro):
             for c in range(chunks):
-                local_in(pages, h_in, frecv, m, c).start()
+                local_in(r.pages, h_in, r.frecv, m, c).start()
 
     @pl.when(s == last)
     def _():
         for m in range(micro):
             for c in range(chunks):
-                local_in(cot, g_in, brecv, m, c).start()
+                local_in(r.cot, g_in, r.brecv, m, c).start()
 
     def wait_h(m, c):
         @pl.when(s == 0)
         def _():
-            local_in(pages, h_in, frecv, m, c).wait()
+            local_in(r.pages, h_in, r.frecv, m, c).wait()
 
         @pl.when(s != 0)
         def _():
-            hop(h_out, h_in, fsend, frecv, m, c, 1).wait_recv()
+            hop(h_out, h_in, r.fsend, r.frecv, m, c, 1).wait_recv()
 
     def wait_g(m, c):
         @pl.when(s == last)
         def _():
-            local_in(cot, g_in, brecv, m, c).wait()
+            local_in(r.cot, g_in, r.brecv, m, c).wait()
 
         @pl.when(s != last)
         def _():
-            hop(g_out, g_in, bsend, brecv, m, c, -1).wait_recv()
+            hop(g_out, g_in, r.bsend, r.brecv, m, c, -1).wait_recv()
 
     def send_h(m, c):
         @pl.when(s != last)
         def _():
-            hop(h_out, h_in, fsend, frecv, m, c, 1).start()
+            hop(h_out, h_in, r.fsend, r.frecv, m, c, 1).start()
 
         @pl.when(s == last)
         def _():
@@ -169,12 +175,12 @@
 
                 @pl.when(j != s)
                 def _():
-                    share(h_out, fin_in, fin_send, fin_recv, m, j).start()
+                    share(h_out, r.fin_in, r.fin_send, r.fin_recv, m, j).start()
 
     def send_g(m, c):
         @pl.when(s != 0)
         def _():
-            hop(g_out, g_in, bsend, brecv, m, c, -1).start()
+            hop(g_out, g_in, r.bsend, r.brecv, m, c, -1).start()
 
         @pl.when(s == 0)
         def _():
@@ -183,10 +189,132 @@
 
                 @pl.when(j != s)
                 def _():
-                    share(g_out, ig_in, ig_send, ig_recv, m, j).start()
-
-    def span_of(c):
-        return pl.ds(pl.multiple_of(c * rows, rows), rows)
+                    share(g_out, r.ig_in, r.ig_send, r.ig_recv, m, j).start()
+
+    def block_of(i):
+        return w[i * width : (i + 1) * width, :]
+
+    if fused:
+
+        def shard_rows(tail, i, shard, count, first=0):
+            if tail:
+                at = hidden + shard * (part + 3 * part * kind) + i * part + first
+            else:
+                at = i * width + shard * part + first
+            return pl.ds(pl.multiple_of(at, half), count)
+
+        def gather(tail, i, t, shard, near, count=None, first=0):
+            span = shard_rows(tail, i, shard, count or part, first)
+            u = 4 + i if tail else i
+            return to_near(w.at[span], w.at[span], r.ag_send.at[u, t], r.ag_recv.at[u, t], near)
+
+        def over_units(step):
+            def head(i, _):
+                step(False, i)
+                return 0
+
+            def rest(i, _):
+                step(True, i)
+                return 0
+
+            lax.fori_loop(0, 4, head, 0)
+            lax.fori_loop(0, tail_units, rest, 0)
+
+        def own_copy(source, tail, i):
+            u = 4 + i if tail else i
+            return pltpu.make_async_copy(
+                source, w.at[shard_rows(tail, i, d, part)], r.own_sem.at[u]
+            )
+
+        @pl.when(is_attn)
+        def _():
+            for i in range(3):
+                own_copy(
+                    r.qkv_w.at[layer, :, pl.ds(i * width, width)], False, i
+                ).start()
+            own_copy(r.pos_w.at[layer], False, 3).start()
+            own_copy(r.out_w.at[layer], True, 0).start()
+
+        @pl.when(is_feed)
+        def _():
+            for i in range(4):
+                own_copy(r.in_w.at[layer, :, pl.ds(i * width, width)], False, i).start()
+            for i in range(4):
+                own_copy(r.down_w.at[layer, pl.ds(i * part, part), :], True, i).start()
+
+        def first_round(tail, i):
+            own_copy(r.pos_w.at[layer], tail, i).wait()
+            gather(tail, i, 0, d, near_x).start()
+            gather(tail, i, 1, d, near_y).start()
+            gather(tail, i, 2, d, near_c).start()
+
+        def second_round(tail, i):
+            gather(tail, i, 0, near_x, near_x).wait_recv()
+            gather(tail, i, 3, near_x, near_y, half, 0).start()
+            gather(tail, i, 5, near_x, near_c).start()
+            gather(tail, i, 1, near_y, near_y).wait_recv()
+            gather(tail, i, 4, near_y, near_x, half, half).start()
+            gather(tail, i, 6, near_y, near_c).start()
+
+        def third_round(tail, i):
+            gather(tail, i, 3, diag, near_y, half, 0).wait_recv()
+            gather(tail, i, 4, diag, near_x, half, half).wait_recv()
+            gather(tail, i, 7, diag, near_c).start()
+
+        def last_round(tail, i):
+            flip = 1 - 2 * core
+            gather(tail, i, 2, near_c, near_c).wait_recv()
+            gather(tail, i, 5, near_x + flip, near_c).wait_recv()
+            gather(tail, i, 6, near_y + flip, near_c).wait_recv()
+            gather(tail, i, 7, diag + flip, near_c).wait_recv()
+
+        def gather_sent(tail, i):
+            for t, (shard, near) in enumerate(((d, near_x), (d, near_y), (d, near_c))):
+                gather(tail, i, t, shard, near).wait_send()
+            gather(tail, i, 3, near_x, near_y, half, 0).wait_send()
+            gather(tail, i, 4, near_y, near_x, half, half).wait_send()
+            gather(tail, i, 5, near_x, near_c).wait_send()
+            gather(tail, i, 6, near_y, near_c).wait_send()
+            gather(tail, i, 7, diag, near_c).wait_send()
+
+        over_units(first_round)
+
+        v = r.vec_all
+        v[cy, cx, core] = r.vec_own[...]
+        swaps = [
+            (v.at[cy, cx, core], v.at[cy, cx, 1 - core], near_c),
+            (v.at[cy, cx], v.at[cy, 1 - cx], near_x),
+            (v.at[cy], v.at[1 - cy], near_y),
+        ]
+        for t, (mine, theirs, near) in enumerate(swaps):
+            to_near(mine, mine, r.v_send.at[t], r.v_recv.at[t], near).start()
+            to_near(mine, theirs, r.v_send.at[t], r.v_recv.at[t], near).wait_recv()
+        for dest in range(8):
+            row = v[dest // 4, (dest // 2) % 2, dest % 2]
+            at = dest * part
+
+            @pl.when(is_attn)
+            def _(row=row, at=at):
+                for i in range(3):
+                    vec[0:1, i * width + at : i * width + at + part] = row[i : i + 1, :part]
+
+            @pl.when(is_feed)
+            def _(row=row, dest=dest):
+                for i in range(3):
+                    lane_at = dest * 4 * part + i * 128
+                    vec[0:1, lane_at : lane_at + 128] = row[i : i + 1, :]
+
+            for i in range(3):
+                vec[1:2, i * width + at : i * width + at + part] = row[3 + i : 4 + i, :part]
+
+        over_units(second_round)
+        over_units(third_round)
+        over_units(last_round)
+    else:
+        whole = pltpu.make_async_copy(r.w_in, w, r.own_sem)
+        whole.start()
+        vec[...] = r.vec_in[...]
+        whole.wait()
 
     def norm_out(m, c, summed, gain, offset):
         span = span_of(c)
@@ -200,7 +328,7 @@
         h_out[m, span] = (z * gain + offset).astype(BF)
         send_h(m, c)
 
-    def norm_back(m, c, gain, gain_at, bias_at):
+    def norm_back(m, c, gain, bias_at):
         span = span_of(c)
         g = g_in[m, span].astype(F32)
         z = zed[m, span]
@@ -211,22 +339,17 @@
         grad = (u - mean_u - z * mean_uz) * inv
         low = grad.astype(BF)
         db[m, span] = low
-        small_o[1:2, width : 2 * width] += jnp.sum(g * z, axis=0, keepdims=True)
-        small_o[1:2, 2 * width : 3 * width] += jnp.sum(g, axis=0, keepdims=True)
+        colsum[1:2, width : 2 * width] += jnp.sum(g * z, axis=0, keepdims=True)
+        colsum[1:2, 2 * width : 3 * width] += jnp.sum(g, axis=0, keepdims=True)
         at = bias_at
-        small_o[at[0] : at[0] + 1, at[1] : at[1] + width] += jnp.sum(
+        colsum[at[0] : at[0] + 1, at[1] : at[1] + width] += jnp.sum(
             low.astype(F32), axis=0, keepdims=True
         )
         return grad, low
 
-    small_o[...] = jnp.zeros_like(small_o)
+    colsum[...] = jnp.zeros_like(colsum)
     gain = vec[1:2, width : 2 * width]
     offset = vec[1:2, 2 * width : 3 * width]
-
-    def flush(source, at_rows, at_cols, target, slot):
-        return pltpu.make_async_copy(
-            source, target.at[pl.ds(at_rows, width), pl.ds(at_cols, width)], stage_sem.at[slot]
-        )
 
     @pl.when(is_attn)
     def _():
@@ -236,7 +359,7 @@
         def places(idx, _):
             m, c = idx // chunks, idx % chunks
             span = span_of(c)
-            qkvp[m, span, 3 * width :] = dot_nn(place[m, span], wa[:, 3 * width :]).astype(BF)
+            qkvp[m, span, 3 * width :] = dot_nn(place[m, span], block_of(3)).astype(BF)
             return 0
 
         lax.fori_loop(0, micro * chunks, places, 0)
@@ -246,14 +369,14 @@
                 span = span_of(c)
                 wait_h(m, c)
                 h = h_in[m, span]
-                q = dot_nn(h, wa[:, :width]) + vec[0:1, :width]
+                q = dot_nn(h, block_of(0)) + vec[0:1, :width]
                 qkvp[m, span, :width] = q.astype(BF)
-                k = dot_nn(h, wa[:, width : 2 * width]).astype(BF)
+                k = dot_nn(h, block_of(1)).astype(BF)
                 qkvp[m, span, width : 2 * width] = k
                 kplus[m, span] = (
                     k.astype(F32) + qkvp[m, span, 3 * width :].astype(F32)
                 ).astype(BF)
-                v = dot_nn(h, wa[:, 2 * width : 3 * width]) + vec[0:1, width : 2 * width]
+                v = dot_nn(h, block_of(2)) + vec[0:1, width : 2 * width]
                 qkvp[m, span, 2 * width : 3 * width] = v.astype(BF)
                 return 0
 
@@ -280,8 +403,8 @@
                     mixed = []
                     for side in range(2):
                         mask = lane2 if side == 0 else jnp.logical_not(lane2)
-                        part = jnp.where(mask, left, jnp.zeros_like(left))
-                        score = dot_nt(part, right) * (SCORE_SCALE * LOG2E) + bias
+                        masked = jnp.where(mask, left, jnp.zeros_like(left))
+                        score = dot_nt(masked, right) * (SCORE_SCALE * LOG2E) + bias
                         top = jnp.max(score, axis=1, keepdims=True)
                         power = jnp.exp2(score - top)
                         total = jnp.sum(power, axis=1, keepdims=True)
@@ -295,7 +418,7 @@
                     return 0
 
                 lax.fori_loop(0, pairs, heads, 0)
-                branch = dot_nn(context[m, span], wb[:width, :])
+                branch = dot_nn(context[m, span], block_of(4))
                 summed = h_in[m, span].astype(F32) + branch + vec[0:1, 2 * width : 3 * width]
                 norm_out(m, c, summed, gain, offset)
                 return 0
@@ -309,9 +432,9 @@
             def enter(c, _):
                 span = span_of(c)
                 wait_g(m, c)
-                grad, low = norm_back(m, c, gain, None, (0, 2 * width))
+                grad, low = norm_back(m, c, gain, (0, 2 * width))
                 dy[span] = grad
-                dc[span] = dot_nt(low, wb[:width, :]).astype(BF)
+                dc[span] = dot_nt(low, block_of(4)).astype(BF)
                 return 0
 
             lax.fori_loop(0, chunks, enter, 0)
@@ -350,10 +473,10 @@
                 qkvp[m, :, pl.ds(off + width, PAIR)] = grad_k
                 qkvp[m, :, pl.ds(off + 2 * width, PAIR)] = grad_v
                 qkvp[m, :, pl.ds(off + 3 * width, PAIR)] = grad_pl
-                small_o[0:1, pl.ds(off, PAIR)] += jnp.sum(
+                colsum[0:1, pl.ds(off, PAIR)] += jnp.sum(
                     grad_q.astype(F32), axis=0, keepdims=True
                 )
-                small_o[0:1, pl.ds(off + width, PAIR)] += jnp.sum(
+                colsum[0:1, pl.ds(off + width, PAIR)] += jnp.sum(
                     grad_v.astype(F32), axis=0, keepdims=True
                 )
                 return 0
@@ -362,7 +485,11 @@
 
             def leave(c, _):
                 span = span_of(c)
-                total = dy[span] + dot_nt(qkvp[m, span, : 3 * width], wa[:, : 3 * width])
+                total = dy[span]
+                for i in range(3):
+                    total = total + dot_nt(
+                        qkvp[m, span, i * width : (i + 1) * width], block_of(i)
+                    )
                 g_out[m, span] = total.astype(BF)
                 send_g(m, c)
                 return 0
@@ -372,9 +499,7 @@
 
         lax.fori_loop(0, micro, backward, 0)
 
-    blocks = hidden // width
-
-    @pl.when(jnp.logical_not(is_attn))
+    @pl.when(is_feed)
     def _():
         def forward(idx, _):
             m, c = idx // chunks, idx % chunks
@@ -384,12 +509,12 @@
             summed = h.astype(F32) + vec[1:2, :width]
             for f in range(blocks):
                 at = f * width
-                inner = dot_nn(h, wa[:, at : at + width]) + vec[0:1, at : at + width]
+                inner = dot_nn(h, block_of(f)) + vec[0:1, at : at + width]
                 value, slope = gelu_and_slope(inner)
                 low = value.astype(BF)
                 saved[m, span, at : at + width] = low
                 saved[m, span, hidden + at : hidden + at + width] = slope.astype(BF)
-                summed = summed + dot_nn(low, wb[at : at + width, :])
+                summed = summed + dot_nn(low, block_of(blocks + f))
             norm_out(m, c, summed, gain, offset)
             return 0
 
@@ -399,17 +524,17 @@
             m, c = idx // chunks, idx % chunks
             span = span_of(c)
             wait_g(m, c)
-            total, low = norm_back(m, c, gain, None, (1, 0))
+            total, low = norm_back(m, c, gain, (1, 0))
             for f in range(blocks):
                 at = f * width
-                grad_a = dot_nt(low, wb[at : at + width, :]).astype(BF).astype(F32)
+                grad_a = dot_nt(low, block_of(blocks + f)).astype(BF).astype(F32)
                 slope = saved[m, span, hidden + at : hidden + at + width].astype(F32)
                 grad_i = (grad_a * slope).astype(BF)
                 saved[m, span, hidden + at : hidden + at + width] = grad_i
-                small_o[0:1, at : at + width] += jnp.sum(
+                colsum[0:1, at : at + width] += jnp.sum(
                     grad_i.astype(F32), axis=0, keepdims=True
                 )
-                total = total + dot_nt(grad_i, wa[:, at : at + width])
+                total = total + dot_nt(grad_i, block_of(f))
             g_out[m, span] = total.astype(BF)
             send_g(m, c)
             return 0
@@ -417,148 +542,530 @@
         lax.fori_loop(0, micro * chunks, backward, 0)
 
     tokens = micro * length
+    stage = r.stage
 
     def tall(ref, at):
         return ref[:, :, pl.ds(at, width)].reshape(tokens, width)
 
-    def put(value, slot, at_rows, at_cols, target):
-        stage[slot] = value.astype(BF)
-        flush(stage.at[slot], at_rows, at_cols, target, slot).start()
-
-    def drain(slot):
-        flush(stage.at[slot], 0, 0, dwa_o, slot).wait()
-
-    def write_all(n, value_of, target, by_rows):
-        def step(i, _):
-            slot = i % 2
-
-            @pl.when(i >= 2)
+    if fused:
+        table, own = r.table, r.own
+
+        def spot(ref, e, by_chip):
+            return ref.at[pl.ds(4, 4), e - 4] if by_chip else ref.at[e]
+
+        def keep(e, by_chip):
+            slot = e % 2
+            return pltpu.make_async_copy(
+                stage.at[slot, :, core], spot(own, e, by_chip), r.keep_sem.at[slot]
+            )
+
+        def give(e, by_chip):
+            slot = e % 2
+            return to_near(
+                stage.at[slot, :, 1 - core],
+                spot(table, e, by_chip),
+                r.p0_send.at[slot],
+                r.p0_recv.at[e],
+                near_c,
+            )
+
+        def emit(e, value, by_chip):
+            slot = e % 2
+
+            @pl.when(e >= 2)
             def _():
-                drain(slot)
-
-            at = pl.multiple_of(i * width, width)
-            if by_rows:
-                put(value_of(at), slot, at, 0, target)
+                keep(e, by_chip).wait()
+                give(e, by_chip).wait_send()
+
+            low = value.astype(BF)
+            if by_chip:
+                for p in range(2):
+                    for j in range(4):
+                        at = (p * 4 + j) * part
+                        stage[slot, j, p] = low[at : at + part]
             else:
-                put(value_of(at), slot, 0, at, target)
-            return 0
-
-        lax.fori_loop(0, n, step, 0)
-        for i in range(max(n - 2, 0), n):
-            drain(i % 2)
+                stage[slot] = low.reshape(4, 2, part, width)
+            keep(e, by_chip).start()
+            give(e, by_chip).start()
+
+        def settle(e, by_chip):
+            keep(e, by_chip).wait()
+            give(e, by_chip).wait_send()
+
+        def finish(count, by_chip):
+            settle(count - 2, by_chip)
+            settle(count - 1, by_chip)
+    else:
+
+        def flush(slot, at):
+            return pltpu.make_async_copy(
+                stage.at[slot], r.dw_o.at[pl.ds(at, width)], r.keep_sem.at[slot]
+            )
+
+        def emit(e, value, by_chip):
+            slot = e % 2
+
+            @pl.when(e >= 2)
+            def _():
+                flush(slot, 0).wait()
+
+            stage[slot] = value.astype(BF)
+            flush(slot, pl.multiple_of(e * width, width)).start()
+
+        def finish(count, by_chip):
+            flush(0, 0).wait()
+            flush(1, 0).wait()
 
     @pl.when(is_attn)
     def _():
-        write_all(3, lambda at: dot_tn(tall(h_in, 0), tall(qkvp, at)), dwa_o, False)
-        put(dot_tn(tall(place, 0), tall(qkvp, 3 * width)), 0, 0, 3 * width, dwa_o)
-        put(dot_tn(tall(context, 0), tall(db, 0)), 1, 0, 0, dwb_o)
-        drain(0)
-        drain(1)
-
-    @pl.when(jnp.logical_not(is_attn))
+        def step(e, _):
+            at = pl.multiple_of(e * width, width)
+            emit(e, dot_tn(tall(h_in, 0), tall(qkvp, at)), False)
+            return 0
+
+        lax.fori_loop(0, 3, step, 0)
+        emit(3, dot_tn(tall(place, 0), tall(qkvp, 3 * width)), False)
+        emit(4, dot_tn(tall(context, 0), tall(db, 0)), False)
+        finish(5, False)
+
+    @pl.when(is_feed)
     def _():
-        write_all(
-            blocks,
-            lambda at: dot_tn(tall(h_in, 0), tall(saved, pl.multiple_of(at + hidden, width))),
-            dwa_o,
-            False,
-        )
-        write_all(blocks, lambda at: dot_tn(tall(saved, at), tall(db, 0)), dwb_o, True)
+        def step(e, _):
+            at = pl.multiple_of(e * width + hidden, width)
+            emit(e, dot_tn(tall(h_in, 0), tall(saved, at)), False)
+            return 0
+
+        lax.fori_loop(0, blocks, step, 0)
+
+        def step_b(i, _):
+            at = pl.multiple_of(i * width, width)
+            emit(i + blocks, dot_tn(tall(saved, at), tall(db, 0)), True)
+            return 0
+
+        lax.fori_loop(0, blocks, step_b, 0)
+        finish(2 * blocks, True)
+
+    if not fused:
+        r.small_o[...] = colsum[...]
+    else:
+        low_half, high_half = pl.ds(0, half), pl.ds(half, half)
+
+        def fetch(u):
+            slot = u % 2
+            return pltpu.make_async_copy(own.at[u], stage.at[slot, :, 0], r.keep_sem.at[slot])
+
+        def add(target, other):
+            return (target.astype(F32) + other.astype(F32)).astype(BF)
+
+        def one_x(u, y):
+            return to_near(
+                table.at[u, 2 * y + 1 - cx, low_half],
+                r.land_x.at[u, y],
+                r.p1x_send.at[u, y],
+                r.p1x_recv.at[u, y],
+                near_x,
+            )
+
+        def one_y(u):
+            return to_near(
+                table.at[u, pl.ds(2 - 2 * cy, 2), high_half],
+                r.land_y.at[u],
+                r.p1y_send.at[u],
+                r.p1y_recv.at[u],
+                near_y,
+            )
+
+        def two_y(u):
+            return to_near(
+                table.at[u, 2 - 2 * cy + cx, low_half],
+                r.land_y2.at[u],
+                r.p2y_send.at[u],
+                r.p2y_recv.at[u],
+                near_y,
+            )
+
+        def two_x(u):
+            return to_near(
+                table.at[u, 2 * cy + 1 - cx, high_half],
+                r.land_x2.at[u],
+                r.p2x_send.at[u],
+                r.p2x_recv.at[u],
+                near_x,
+            )
+
+        sm = r.small
+        for dest in range(8):
+            row = sm.at[dest // 4, (dest // 2) % 2, dest % 2]
+            at = dest * part
+
+            @pl.when(is_attn)
+            def _(row=row, at=at):
+                for i in range(3):
+                    row[i : i + 1, :part] = colsum[0:1, i * width + at : i * width + at + part]
+
+            @pl.when(is_feed)
+            def _(row=row, dest=dest):
+                for i in range(3):
+                    lane_at = dest * 4 * part + i * 128
+                    row[i : i + 1, :] = colsum[0:1, lane_at : lane_at + 128]
+
+            for i in range(3):
+                row[3 + i : 4 + i, :part] = colsum[1:2, i * width + at : i * width + at + part]
+        small_c = to_near(
+            sm.at[:, :, 1 - core], r.small_0, r.s_send.at[0], r.s_recv.at[0], near_c
+        )
+        small_x = to_near(
+            sm.at[:, 1 - cx, core], r.small_1, r.s_send.at[1], r.s_recv.at[1], near_x
+        )
+        small_y = to_near(
+            sm.at[1 - cy, cx, core], r.small_2, r.s_send.at[2], r.s_recv.at[2], near_y
+        )
+        small_c.start()
+
+        fetch(0).start()
+
+        def merge_core(u, _):
+            @pl.when(u + 1 < units)
+            def _():
+                fetch(u + 1).start()
+
+            @pl.when(u <= 4)
+            def _():
+                give(u, False).wait_recv()
+
+            @pl.when(jnp.logical_and(u == 4, is_feed))
+            def _():
+                for e in range(5, 8):
+                    give(e, True).wait_recv()
+
+            fetch(u).wait()
+            table[u] = add(table[u], stage[u % 2, :, 0])
+            for y in range(2):
+                one_x(u, y).start()
+            one_y(u).start()
+            return 0
+
+        lax.fori_loop(0, units, merge_core, 0)
+
+        small_c.wait_recv()
+        for y in range(2):
+            for x in range(2):
+                sm[y, x, core] = sm[y, x, core] + r.small_0[y, x]
+        small_x.start()
+
+        def merge_one(u, _):
+            for y in range(2):
+                one_x(u, y).wait_recv()
+                at = 2 * y + cx
+                table[u, at, :half] = add(table[u, at, :half], r.land_x[u, y])
+            two_y(u).start()
+            one_y(u).wait_recv()
+            for x in range(2):
+                at = 2 * cy + x
+                table[u, at, half:] = add(table[u, at, half:], r.land_y[u, x])
+            two_x(u).start()
+            return 0
+
+        lax.fori_loop(0, units, merge_one, 0)
+
+        small_x.wait_recv()
+        for y in range(2):
+            sm[y, cx, core] = sm[y, cx, core] + r.small_1[y]
+        small_y.start()
+
+        def left(u, by):
+            return to_section(
+                table.at[u, chip],
+                r.all_w.at[s, u],
+                r.left_send.at[by, u],
+                r.all_recv.at[s, u],
+                (s - by + sections) % sections,
+            )
+
+        def right_own(u):
+            return to_section(
+                table.at[u, chip],
+                r.all_w.at[s, u],
+                r.right_send.at[s, u],
+                r.all_recv.at[s, u],
+                (s + 1) % sections,
+            )
+
+        def right_on(t, u):
+            return to_section(
+                r.all_w.at[t, u],
+                r.all_w.at[t, u],
+                r.right_send.at[t, u],
+                r.all_recv.at[t, u],
+                (s + 1) % sections,
+            )
+
+        def mine(u):
+            return pltpu.make_async_copy(table.at[u, chip], r.all_w.at[s, u], r.own_sem.at[u])
+
+        def merge_two(u, _):
+            two_y(u).wait_recv()
+            table[u, chip, :half] = add(table[u, chip, :half], r.land_y2[u])
+            two_x(u).wait_recv()
+            table[u, chip, half:] = add(table[u, chip, half:], r.land_x2[u])
+
+            @pl.when(s != last)
+            def _():
+                right_own(u).start()
+
+            for by in range(1, sections):
+
+                @pl.when(s >= by)
+                def _(by=by):
+                    left(u, by).start()
+
+            mine(u).start()
+            return 0
+
+        lax.fori_loop(0, units, merge_two, 0)
+
+        small_y.wait_recv()
+        sm[cy, cx, core] = sm[cy, cx, core] + r.small_2[...]
+        small_z = [
+            to_section(
+                sm.at[cy, cx, core],
+                r.all_s.at[s],
+                r.sz_send.at[by - 1],
+                r.sz_recv.at[s],
+                (s + by) % sections,
+            )
+            for by in range(1, sections)
+        ]
+        for copy in small_z:
+            copy.start()
+
+        for by in range(1, sections):
+
+            @pl.when(s >= by)
+            def _(by=by):
+                t = s - by
+
+                def relay(u, _):
+                    right_on(t, u).wait_recv()
+
+                    @pl.when(s != last)
+                    def _():
+                        right_on(t, u).start()
+
+                    return 0
+
+                lax.fori_loop(0, 5 + 3 * (t % 2), relay, 0)
+
+        for by in range(1, sections):
+
+            @pl.when(s + by < sections)
+            def _(by=by):
+                t = s + by
+
+                def arrive(u, _):
+                    right_on(t, u).wait_recv()
+                    return 0
+
+                lax.fori_loop(0, 5 + 3 * (t % 2), arrive, 0)
+
+        for by in range(1, sections):
+            t = (s + by) % sections
+            to_section(
+                sm.at[cy, cx, core],
+                r.all_s.at[t],
+                r.sz_send.at[by - 1],
+                r.sz_recv.at[t],
+                t,
+            ).wait_recv()
+        r.all_s[s] = sm[cy, cx, core]
+
+        over_units(gather_sent)
+        for t, (mine_v, theirs, near) in enumerate(swaps):
+            to_near(mine_v, mine_v, r.v_send.at[t], r.v_recv.at[t], near).wait_send()
+        small_c.wait_send()
+        small_x.wait_send()
+        small_y.wait_send()
+        for copy in small_z:
+            copy.wait_send()
+
+        def sent(u, _):
+            for y in range(2):
+                one_x(u, y).wait_send()
+            one_y(u).wait_send()
+            two_y(u).wait_send()
+            two_x(u).wait_send()
+            mine(u).wait()
+
+            @pl.when(s != last)
+            def _():
+                right_own(u).wait_send()
+
+            for by in range(1, sections):
+
+                @pl.when(s >= by)
+                def _(by=by):
+                    left(u, by).wait_send()
+
+            return 0
+
+        lax.fori_loop(0, units, sent, 0)
+        for by in range(1, sections):
+
+            @pl.when(jnp.logical_and(s >= by, s != last))
+            def _(by=by):
+                t = s - by
+
+                def relayed(u, _):
+                    right_on(t, u).wait_send()
+                    return 0
+
+                lax.fori_loop(0, 5 + 3 * (t % 2), relayed, 0)
 
     for m in range(micro):
         for c in range(chunks):
 
             @pl.when(s != last)
             def _():
-                hop(h_out, h_in, fsend, frecv, m, c, 1).wait_send()
+                hop(h_out, h_in, r.fsend, r.frecv, m, c, 1).wait_send()
 
             @pl.when(s != 0)
             def _():
-                hop(g_out, g_in, bsend, brecv, m, c, -1).wait_send()
+                hop(g_out, g_in, r.bsend, r.brecv, m, c, -1).wait_send()
 
     @pl.when(s == last)
     def _():
         for m in range(micro):
             for j in range(sections - 1):
-                share(h_out, fin_in, fin_send, fin_recv, m, j).wait_send()
-            final_o[m] = h_out[m, (sections - 1) * quarter :]
+                share(h_out, r.fin_in, r.fin_send, r.fin_recv, m, j).wait_send()
+            r.final_o[m] = h_out[m, (sections - 1) * quarter :]
 
     @pl.when(s != last)
     def _():
         for m in range(micro):
-            share(h_out, fin_in, fin_send, fin_recv, m, 0).wait_recv()
-            final_o[m] = fin_in[m]
+            share(h_out, r.fin_in, r.fin_send, r.fin_recv, m, 0).wait_recv()
+            r.final_o[m] = r.fin_in[m]
 
     @pl.when(s == 0)
     def _():
         for m in range(micro):
             for j in range(1, sections):
-                share(g_out, ig_in, ig_send, ig_recv, m, j).wait_send()
-            igrad_o[m] = g_out[m, :quarter].astype(F32)
+                share(g_out, r.ig_in, r.ig_send, r.ig_recv, m, j).wait_send()
+            r.igrad_o[m] = g_out[m, :quarter].astype(F32)
 
     @pl.when(s != 0)
     def _():
         for m in range(micro):
-            share(g_out, ig_in, ig_send, ig_recv, m, 1).wait_recv()
-            igrad_o[m] = ig_in[m].astype(F32)
-
-
-def pipeline(pages, cot, place, hide, wa, wb, vec):
-    micro, length, width = pages.shape
-    hidden = wa.shape[1]
+            share(g_out, r.ig_in, r.ig_send, r.ig_recv, m, 1).wait_recv()
+            r.igrad_o[m] = r.ig_in[m].astype(F32)
+
+
+def pipeline(fused, hidden, inputs):
+    micro, length, width = inputs["pages"].shape
     sections = lax.axis_size("section")
     rows = length // 2
     chunks = length // rows
     quarter = length // sections
     heads = width // HEAD_DIM
     wide = max(2 * hidden, heads * length)
+    part = width // 8
+    half = part // 2
     hbm = pl.BlockSpec(memory_space=pl.ANY)
     vmem = pl.BlockSpec(memory_space=pltpu.VMEM)
     act = (micro, length, width)
     dma = pltpu.SemaphoreType.DMA
-    return pl.pallas_call(
-        partial(pipeline_kernel, rows),
-        out_shape=(
-            jax.ShapeDtypeStruct((micro, quarter, width), BF),
-            jax.ShapeDtypeStruct((micro, quarter, width), F32),
-            jax.ShapeDtypeStruct((width, hidden), BF),
-            jax.ShapeDtypeStruct((hidden, width), BF),
-            jax.ShapeDtypeStruct((8, hidden), F32),
-        ),
-        in_specs=[hbm, hbm, vmem, vmem, vmem, vmem, vmem],
-        out_specs=(vmem, vmem, hbm, hbm, vmem),
-        scratch_shapes=[
-            pltpu.VMEM(act, BF),
-            pltpu.VMEM(act, BF),
-            pltpu.VMEM(act, BF),
-            pltpu.VMEM(act, BF),
-            pltpu.VMEM((micro, length, wide), BF),
-            pltpu.VMEM((micro, length, 4 * width), BF),
-            pltpu.VMEM(act, BF),
-            pltpu.VMEM(act, BF),
-            pltpu.VMEM(act, F32),
-            pltpu.VMEM((micro, length, 128), F32),
-            pltpu.VMEM(act, BF),
-            pltpu.VMEM((length, width), BF),
-            pltpu.VMEM((length, width), F32),
-            pltpu.VMEM((micro, quarter, width), BF),
-            pltpu.VMEM((micro, quarter, width), BF),
-            pltpu.VMEM((2, width, width), BF),
-            dma((micro, chunks)),
-            dma((micro, chunks)),
-            dma((micro, chunks)),
-            dma((micro, chunks)),
-            dma((micro, sections)),
-            dma((micro,)),
-            dma((micro, sections)),
-            dma((micro,)),
-            dma((2,)),
-        ],
+    spec = {name: hbm for name in inputs}
+    for name in ("place", "hide", "vec_in", "vec_own"):
+        if name in spec:
+            spec[name] = vmem
+    outs = {
+        "final_o": (vmem, (micro, quarter, width), BF),
+        "igrad_o": (vmem, (micro, quarter, width), F32),
+    }
+    scratch = {
+        "h_in": pltpu.VMEM(act, BF),
+        "g_in": pltpu.VMEM(act, BF),
+        "h_out": pltpu.VMEM(act, BF),
+        "g_out": pltpu.VMEM(act, BF),
+        "saved": pltpu.VMEM((micro, length, wide), BF),
+        "qkvp": pltpu.VMEM((micro, length, 4 * width), BF),
+        "kplus": pltpu.VMEM(act, BF),
+        "context": pltpu.VMEM(act, BF),
+        "zed": pltpu.VMEM(act, F32),
+        "rstd": pltpu.VMEM((micro, length, 128), F32),
+        "db": pltpu.VMEM(act, BF),
+        "dc": pltpu.VMEM((length, width), BF),
+        "dy": pltpu.VMEM((length, width), F32),
+        "w": pltpu.VMEM((2 * hidden, width), BF),
+        "vec": pltpu.VMEM((8, hidden), F32),
+        "colsum": pltpu.VMEM((8, hidden), F32),
+        "fin_in": pltpu.VMEM((micro, quarter, width), BF),
+        "ig_in": pltpu.VMEM((micro, quarter, width), BF),
+        "fsend": dma((micro, chunks)),
+        "frecv": dma((micro, chunks)),
+        "bsend": dma((micro, chunks)),
+        "brecv": dma((micro, chunks)),
+        "fin_send": dma((micro, sections)),
+        "fin_recv": dma((micro,)),
+        "ig_send": dma((micro, sections)),
+        "ig_recv": dma((micro,)),
+        "keep_sem": dma((2,)),
+    }
+    if fused:
+        outs["all_w"] = (hbm, (sections, 8, part, width), BF)
+        outs["all_s"] = (vmem, (sections, 8, 128), F32)
+        outs["own"] = (hbm, (8, 4, part, width), BF)
+        scratch.update(
+            stage=pltpu.VMEM((2, 4, 2, part, width), BF),
+            vec_all=pltpu.VMEM((2, 2, 2, 8, 128), F32),
+            small=pltpu.VMEM((2, 2, 2, 8, 128), F32),
+            small_0=pltpu.VMEM((2, 2, 8, 128), F32),
+            small_1=pltpu.VMEM((2, 8, 128), F32),
+            small_2=pltpu.VMEM((8, 128), F32),
+            table=pltpu.VMEM((8, 4, part, width), BF),
+            land_x=pltpu.VMEM((8, 2, half, width), BF),
+            land_y=pltpu.VMEM((8, 2, half, width), BF),
+            land_x2=pltpu.VMEM((8, half, width), BF),
+            land_y2=pltpu.VMEM((8, half, width), BF),
+            own_sem=dma((8,)),
+            ag_send=dma((8, 8)),
+            ag_recv=dma((8, 8)),
+            v_send=dma((3,)),
+            v_recv=dma((3,)),
+            s_send=dma((3,)),
+            s_recv=dma((3,)),
+            sz_send=dma((sections - 1,)),
+            sz_recv=dma((sections,)),
+            p0_send=dma((2,)),
+            p0_recv=dma((8,)),
+            p1x_send=dma((8, 2)),
+            p1x_recv=dma((8, 2)),
+            p1y_send=dma((8,)),
+            p1y_recv=dma((8,)),
+            p2x_send=dma((8,)),
+            p2x_recv=dma((8,)),
+            p2y_send=dma((8,)),
+            p2y_recv=dma((8,)),
+            left_send=dma((sections, 8)),
+            right_send=dma((sections, 8)),
+            all_recv=dma((sections, 8)),
+        )
+    else:
+        outs["dw_o"] = (hbm, (2 * hidden, width), BF)
+        outs["small_o"] = (vmem, (8, hidden), F32)
+        scratch.update(stage=pltpu.VMEM((2, width, width), BF), own_sem=dma)
+    names = [*inputs, *outs, *scratch]
+    got = pl.pallas_call(
+        partial(pipeline_kernel, names, rows, fused),
+        out_shape=tuple(jax.ShapeDtypeStruct(shape, kind) for _, shape, kind in outs.values()),
+        in_specs=list(spec.values()),
+        out_specs=tuple(where for where, _, _ in outs.values()),
+        scratch_shapes=list(scratch.values()),
         compiler_params=pltpu.CompilerParams(
             collective_id=0, has_side_effects=True, vmem_limit_bytes=63 * 1024 * 1024
         ),
         name="pipeline",
-    )(pages, cot, place, hide, wa, wb, vec)
+    )(*inputs.values())
+    return dict(zip(outs, got, strict=True))
 
 
 def sinusoid(coord_pair, model_width):
@@ -608,6 +1115,55 @@
     def pick(array):
         return lax.dynamic_index_in_dim(array, layer, 0, keepdims=False)
 
+    norm_row = s % 2
+    gain_own = lax.dynamic_index_in_dim(pick(ln_gain), norm_row, 0, keepdims=False)
+    offset_own = lax.dynamic_index_in_dim(pick(ln_bias), norm_row, 0, keepdims=False)
+    inputs = {
+        "pages": pages_in,
+        "cot": cotangent,
+        "place": sinusoid(coords, width),
+        "hide": hidden_bias(boxes, length),
+    }
+    if groups == 8:
+        first = jnp.where(
+            is_attn,
+            jnp.pad(pick(attn_bias), ((0, 0), (0, 128 - part))),
+            pick(ffn_in_bias).reshape(3, 128),
+        )
+        rest = jnp.pad(
+            jnp.stack([pick(ffn_out_bias), gain_own, offset_own]), ((0, 0), (0, 128 - part))
+        )
+        inputs["vec_own"] = jnp.pad(
+            jnp.concatenate([first, rest], axis=0).astype(F32), ((0, 2), (0, 0))
+        )
+        inputs.update(
+            qkv_w=qkv_weight, pos_w=pos_weight, out_w=out_weight, in_w=ffn_in, down_w=ffn_out
+        )
+        got = pipeline(True, hidden, inputs)
+        sections = lax.axis_size("section")
+        shares, sums = got["all_w"], got["all_s"]
+        attn, feed = shares[0::2], shares[1::2]
+        layers = sections // 2
+
+        def side_by_side(blocks):
+            return blocks.transpose(0, 2, 1, 3).reshape(layers, part, -1).astype(F32)
+
+        rest = sums[:, 3:6, :part].reshape(layers, 2, 3, part)
+        return (
+            got["final_o"],
+            got["igrad_o"],
+            side_by_side(attn[:, :3]),
+            sums[0::2, :3, :part],
+            attn[:, 3].astype(F32),
+            attn[:, 4].astype(F32),
+            side_by_side(feed[:, :4]),
+            sums[1::2, :3].reshape(layers, part_h),
+            feed[:, 4:].reshape(layers, part_h, width).astype(F32),
+            rest[:, 1, 0],
+            rest[:, :, 1],
+            rest[:, :, 2],
+        )
+
     own_a = jnp.where(
         is_attn, jnp.concatenate([pick(qkv_weight), pick(pos_weight)], axis=1), pick(ffn_in)
     )
@@ -621,10 +1177,6 @@
         jnp.pad(wb_all[:, :part].reshape(width, width), ((0, hidden - width), (0, 0))),
         wb_all.reshape(hidden, width),
     )
-
-    norm_row = jnp.where(is_attn, 0, 1)
-    gain_own = lax.dynamic_index_in_dim(pick(ln_gain), norm_row, 0, keepdims=False)
-    offset_own = lax.dynamic_index_in_dim(pick(ln_bias), norm_row, 0, keepdims=False)
     bias_own = jnp.where(
         is_attn,
         jnp.pad(pick(attn_bias).reshape(-1), (0, part_h - 3 * part)),
@@ -641,14 +1193,16 @@
         vec_all[:, :part_h].reshape(-1),
     )
     rest = vec_all[:, part_h:].reshape(groups, 3, part).transpose(1, 0, 2).reshape(-1)
-    vec = jnp.pad(
+    inputs["vec_in"] = jnp.pad(
         jnp.stack([first, jnp.pad(rest, (0, hidden - 3 * width))]), ((0, 6), (0, 0))
     )
-
-    place = sinusoid(coords, width)
-    hide = hidden_bias(boxes, length)
-
-    final, igrad, dwa, dwb, small = pipeline(pages_in, cotangent, place, hide, wa, wb, vec)
+    wide_blocks = wa.reshape(width, hidden // width, width).transpose(1, 0, 2)
+    inputs["w_in"] = jnp.concatenate([wide_blocks.reshape(hidden, width), wb], axis=0)
+    got = pipeline(False, hidden, inputs)
+    final, igrad, dw, small = got["final_o"], got["igrad_o"], got["dw_o"], got["small_o"]
+    dwa = dw[:hidden].reshape(hidden // width, width, width).transpose(1, 0, 2)
+    dwa = dwa.reshape(width, hidden)
+    dwb = dw[hidden:]
 
     shard_a = lax.psum_scatter(dwa, "dp", scatter_dimension=0, tiled=True)
     dwb_cut = jnp.where(

time: 529 us -> 340 us (0.64)
  the two profiles are of different devices: /device:TPU:0 before, /device:TPU:24 now
where the time goes in v2:
time: 340 us; the launch traced here: 339 us
  Pallas kernels  310 us (91%)
  local copies, waits for them, and re-layouts  16.2 us (5%)
  other arithmetic  10.7 us (3%)
    pallas_call x1, Pallas kernels, pipeline(): pl.pallas_call(partial(pipeline_kernel, names, rows, fused), out_shape=tu...  310 us

profile of v2, /device:TPU:24, one launch (start us, length us, event | category | flops | bytes accessed | tf_op | source)
XLA Modules:
  0.0 339.5 jit_solution(12709292942625641847)
XLA Ops:
  0.6 0.0 copy-start
  0.7 0.7 fusion.21
  1.4 0.7 constant_dynamic-slice_fusion.2
  2.1 0.0 copy-done
  2.1 0.7 constant_dynamic-slice_fusion.3
  2.8 0.6 fusion.15.refs_4_
  3.4 0.8 fusion.26
  4.2 0.7 convert_element_type.55
  5.0 1.6 select_convert_fusion.refs_3_
  6.5 6.1 %fusion = (bf16[2,2,512,1,192]{2,4,3,1,0:T(8,128)(2,1)S(1)}, bf16[2,2,512,1,192]{2,4,3,1,0:T(8,128)(2,1)S(1)}) fusion(f32[192]{0:T(256)S(1)} %multiply_exponential_fusion, f32[2,2,512]{2,1,0:T(2,128)S(1)} %convert_element_type.55), kind=kLoop, calls=%fused_computation.5 | loop fusion | flops 1179648 | bytes 1581824 | tf_op jit(solution)/shard_map/convert.9
  12.6 0.1 pad_maximum_fusion
  12.7 1.6 copy.31.refs_2_
  14.3 310.2 %pipeline.1 = (bf16[2,128,768]{2,1,0:T(8,128)(2,1)}, f32[2,128,768]{2,1,0:T(8,128)}, bf16[4,8,96,768]{3,2,1,0:T(8,128)(2,1)}, f32[4,8,128]{2,1,0:T(8,128)}, bf16[8,4,96,768]{3,2,1,0:T(8,128)(2,1)}) custom-call(bf16[2,512,768]{2,1,0:T(8,128)(2,1)} %refs_0_.1, bf16[2,512,768]{2,1,0:T(8,128)(2,1)} %refs_1_.1, bf16[2,512,768]{2,1,0:T(8,128)(2,1)} %copy.31.refs_2_, ...), custom_call_target="tpu_custom_call" | custom-call | tf_op jit(solution)/shard_map/pipeline/pallas_call | solution.py:1057
  324.5 0.7 slice_bitcast_fusion.2
  325.2 0.6 copy.47
  325.8 0.7 slice.57
  326.5 0.7 slice.64
  327.2 0.6 copy.37
  327.8 0.6 slice.73
  328.3 0.6 fusion.25
  328.9 2.7 fusion.23
  331.6 0.3 fusion.24
  331.9 1.7 bitcast_convert_fusion
  333.5 1.1 fusion.2
  334.6 0.1 convert_bitcast_fusion.1
  334.8 1.3 copy.42
  336.1 0.0 copy-start.2
  336.1 0.0 copy-start.1
  336.1 1.7 copy.43
  337.8 0.0 copy-done.2
  337.8 0.7 copy.51
  338.6 0.0 copy-done.1
  338.6 0.9 copy.52
  (5 shorter events, 0.1 us)
Async XLA Ops:
  0.6 1.4 copy-start
  336.1 1.7 copy-start.2
  336.1 2.4 copy-start.1

commit v3 on v2

--- a/solution.py
+++ b/solution.py
@@ -3,6 +3,7 @@
 
 import jax
 import jax.numpy as jnp
+import numpy as np
 from jax import lax
 from jax.experimental import pallas as pl
 from jax.experimental.pallas import tpu as pltpu
@@ -43,6 +44,30 @@
     return x * cdf, cdf + x * bell * (1.0 / math.sqrt(2.0 * math.pi))
 
 
+TURN_TERMS = [
+    (-1.0) ** n * (2.0 * math.pi) ** (2 * n + 1) / math.factorial(2 * n + 1) for n in range(6)
+]
+
+
+def sine_of_turns(turns):
+    rest = turns - jnp.floor(turns + 0.5)
+    size = 0.25 - jnp.abs(jnp.abs(rest) - 0.25)
+    square = size * size
+    series = TURN_TERMS[5]
+    for term in TURN_TERMS[4::-1]:
+        series = series * square + term
+    return jnp.where(rest < 0.0, -size, size) * series
+
+
+def turns_per_unit(width):
+    quarter = width // 4
+    wave = 10000.0 ** (-np.arange(quarter) / quarter) / (2.0 * math.pi)
+    table = np.zeros((2, width))
+    table[0, : 2 * quarter] = np.tile(wave, 2)
+    table[1, 2 * quarter :] = np.tile(wave, 2)
+    return jnp.asarray(table, F32)
+
+
 class Refs:
     def __init__(self, names, refs):
         self.__dict__.update(zip(names, refs, strict=True))
@@ -52,7 +77,7 @@
     r = Refs(names, refs)
     h_in, g_in, h_out, g_out = r.h_in, r.g_in, r.h_out, r.g_out
     saved, qkvp, kplus, context, zed, rstd = r.saved, r.qkvp, r.kplus, r.context, r.zed, r.rstd
-    db, dc, dy, w, place, hide = r.db, r.dc, r.dy, r.w, r.place, r.hide
+    db, w, place, hide = r.db, r.w, r.place, r.hide
     vec, colsum = r.vec, r.colsum
     sections = lax.axis_size("section")
     s = lax.axis_index("section")
@@ -62,8 +87,9 @@
     micro, length, width = h_in.shape
     hidden = w.shape[0] // 2
     chunks = length // rows
+    big = 2 * rows
+    bigs = length // big
     quarter = length // sections
-    per_chunk = rows // quarter
     pairs = width // PAIR
     blocks = hidden // width
     is_attn = kind == 0
@@ -82,15 +108,21 @@
         units = 5 + 3 * kind
         tail_units = 1 + 3 * kind
 
+        def peer(t):
+            tc, tx, ty = t % 2, (t // 2) % 2, t // 4
+            return (
+                d + tc * (1 - 2 * core) + 2 * tx * (1 - 2 * cx) + 4 * ty * (1 - 2 * cy)
+            )
+
     barrier = pltpu.get_barrier_semaphore()
     for by in range(1, sections):
         pl.semaphore_signal(
             barrier, inc=1, device_id={"section": (s + by) % sections}, device_id_type=MESH
         )
     if fused:
-        for near in (near_c, near_x, near_y):
-            pl.semaphore_signal(barrier, inc=1, device_id={"dp": near}, device_id_type=MESH)
-    pl.semaphore_wait(barrier, sections - 1 + (3 if fused else 0))
+        for t in range(1, 8):
+            pl.semaphore_signal(barrier, inc=1, device_id={"dp": peer(t)}, device_id_type=MESH)
+    pl.semaphore_wait(barrier, sections - 1 + (7 if fused else 0))
 
     def to_section(source, target, send, recv, at):
         return pltpu.make_async_remote_copy(
@@ -112,8 +144,8 @@
             device_id_type=MESH,
         )
 
-    def span_of(c):
-        return pl.ds(pl.multiple_of(c * rows, rows), rows)
+    def span_of(c, size=rows):
+        return pl.ds(pl.multiple_of(c * size, size), size)
 
     def local_in(source, target, sem, m, c):
         span = span_of(c)
@@ -168,31 +200,49 @@
         def _():
             hop(h_out, h_in, r.fsend, r.frecv, m, c, 1).start()
 
-        @pl.when(s == last)
-        def _():
-            for i in range(per_chunk):
-                j = c * per_chunk + i
-
-                @pl.when(j != s)
-                def _():
-                    share(h_out, r.fin_in, r.fin_send, r.fin_recv, m, j).start()
+        @pl.when(jnp.logical_and(jnp.logical_and(s == last, c != s), m < micro - 1))
+        def _():
+            share(h_out, r.fin_in, r.fin_send, r.fin_recv, m, c).start()
 
     def send_g(m, c):
         @pl.when(s != 0)
         def _():
             hop(g_out, g_in, r.bsend, r.brecv, m, c, -1).start()
 
-        @pl.when(s == 0)
-        def _():
-            for i in range(per_chunk):
-                j = c * per_chunk + i
-
-                @pl.when(j != s)
-                def _():
-                    share(g_out, r.ig_in, r.ig_send, r.ig_recv, m, j).start()
+        @pl.when(jnp.logical_and(s == 0, c != s))
+        def _():
+            share(g_out, r.ig_in, r.ig_send, r.ig_recv, m, c).start()
 
     def block_of(i):
         return w[i * width : (i + 1) * width, :]
+
+    def spots():
+        columns = lax.broadcasted_iota(jnp.int32, (1, width), 1)
+        phase = jnp.where((columns // (width // 4)) % 2 == 1, 0.25, 0.0)
+        tokens_at = lax.broadcasted_iota(jnp.int32, (length, r.boxes.shape[2]), 0)
+
+        def page(m, _):
+            turns = lax.dot_general(
+                r.coords[m].astype(F32),
+                r.waves[...],
+                (((0,), (0,)), ((), ())),
+                precision=lax.Precision.HIGHEST,
+                preferred_element_type=F32,
+            )
+            place[m] = sine_of_turns(turns + phase).astype(BF)
+            box = r.boxes[m]
+
+            def hit(low, high):
+                inside = jnp.logical_and(
+                    tokens_at >= box[low : low + 1], tokens_at < box[high : high + 1]
+                )
+                return jnp.where(inside, 1.0, 0.0)
+
+            covered = dot_nt(hit(0, 1), hit(2, 3))
+            hide[m] = jnp.where(covered < 0.5, 0.0, NEGATIVE).astype(BF)
+            return 0
+
+        lax.fori_loop(0, micro, page, 0)
 
     if fused:
 
@@ -277,20 +327,47 @@
             gather(tail, i, 6, near_y, near_c).wait_send()
             gather(tail, i, 7, diag, near_c).wait_send()
 
+        def of_layer(ref):
+            whole = ref[...].astype(F32)
+            row = whole[0:1]
+            for i in range(1, whole.shape[0]):
+                row = jnp.where(layer == i, whole[i : i + 1], row)
+            return row
+
+        mine_v = r.vec_all.at[d]
+        pair = jnp.concatenate([r.gain_w[layer], r.offset_w[layer]], axis=0).astype(F32)
+        mine_v[3:4, :part] = of_layer(r.down_b)
+        mine_v[4:5, :part] = jnp.where(is_attn, pair[0:1], pair[1:2])
+        mine_v[5:6, :part] = jnp.where(is_attn, pair[2:3], pair[3:4])
+
+        @pl.when(is_attn)
+        def _():
+            for i in range(3):
+                mine_v[i : i + 1, :part] = of_layer(r.attn_b.at[i])
+
+        @pl.when(is_feed)
+        def _():
+            row = of_layer(r.in_b)
+            for i in range(3):
+                mine_v[i : i + 1, :] = row[:, i * 128 : (i + 1) * 128]
+
+        def vec_copy(t, source):
+            return to_near(
+                mine_v, r.vec_all.at[source], r.v_send.at[t - 1], r.v_recv.at[t - 1], peer(t)
+            )
+
+        for t in range(1, 8):
+            vec_copy(t, d).start()
         over_units(first_round)
 
-        v = r.vec_all
-        v[cy, cx, core] = r.vec_own[...]
-        swaps = [
-            (v.at[cy, cx, core], v.at[cy, cx, 1 - core], near_c),
-            (v.at[cy, cx], v.at[cy, 1 - cx], near_x),
-            (v.at[cy], v.at[1 - cy], near_y),
-        ]
-        for t, (mine, theirs, near) in enumerate(swaps):
-            to_near(mine, mine, r.v_send.at[t], r.v_recv.at[t], near).start()
-            to_near(mine, theirs, r.v_send.at[t], r.v_recv.at[t], near).wait_recv()
+        @pl.when(is_attn)
+        def _():
+            spots()
+
+        for t in range(1, 8):
+            vec_copy(t, peer(t)).wait_recv()
         for dest in range(8):
-            row = v[dest // 4, (dest // 2) % 2, dest % 2]
+            row = r.vec_all[dest]
             at = dest * part
 
             @pl.when(is_attn)
@@ -314,22 +391,24 @@
         whole = pltpu.make_async_copy(r.w_in, w, r.own_sem)
         whole.start()
         vec[...] = r.vec_in[...]
+        spots()
         whole.wait()
 
-    def norm_out(m, c, summed, gain, offset):
-        span = span_of(c)
+    def norm_out(m, c, summed, gain, offset, size=rows):
+        span = span_of(c, size)
         mean = jnp.mean(summed, axis=1, keepdims=True)
         center = summed - mean
         spread = jnp.mean(center * center, axis=1, keepdims=True)
         inv = lax.rsqrt(spread + EPSILON)
         z = center * inv
         zed[m, span] = z
-        rstd[m, span] = jnp.broadcast_to(inv, (rows, 128))
+        rstd[m, span] = jnp.broadcast_to(inv, (size, 128))
         h_out[m, span] = (z * gain + offset).astype(BF)
-        send_h(m, c)
-
-    def norm_back(m, c, gain, bias_at):
-        span = span_of(c)
+        for i in range(size // rows):
+            send_h(m, c * (size // rows) + i)
+
+    def norm_back(m, c, gain, bias_at, size=rows):
+        span = span_of(c, size)
         g = g_in[m, span].astype(F32)
         z = zed[m, span]
         inv = rstd[m, span][:, :1]
@@ -357,17 +436,18 @@
         lane2 = lax.broadcasted_iota(jnp.int32, (1, 2 * PAIR), 1) % PAIR < HEAD_DIM
 
         def places(idx, _):
-            m, c = idx // chunks, idx % chunks
-            span = span_of(c)
+            m, c = idx // bigs, idx % bigs
+            span = span_of(c, big)
             qkvp[m, span, 3 * width :] = dot_nn(place[m, span], block_of(3)).astype(BF)
             return 0
 
-        lax.fori_loop(0, micro * chunks, places, 0)
+        lax.fori_loop(0, micro * bigs, places, 0)
 
         def forward(m, _):
             def project(c, _):
-                span = span_of(c)
-                wait_h(m, c)
+                span = span_of(c, big)
+                wait_h(m, 2 * c)
+                wait_h(m, 2 * c + 1)
                 h = h_in[m, span]
                 q = dot_nn(h, block_of(0)) + vec[0:1, :width]
                 qkvp[m, span, :width] = q.astype(BF)
@@ -380,10 +460,10 @@
                 qkvp[m, span, 2 * width : 3 * width] = v.astype(BF)
                 return 0
 
-            lax.fori_loop(0, chunks, project, 0)
+            lax.fori_loop(0, bigs, project, 0)
 
             def attend(c, _):
-                span = span_of(c)
+                span = span_of(c, big)
 
                 def heads(t, _):
                     off = pl.multiple_of(t * PAIR, PAIR)
@@ -420,24 +500,25 @@
                 lax.fori_loop(0, pairs, heads, 0)
                 branch = dot_nn(context[m, span], block_of(4))
                 summed = h_in[m, span].astype(F32) + branch + vec[0:1, 2 * width : 3 * width]
-                norm_out(m, c, summed, gain, offset)
+                norm_out(m, c, summed, gain, offset, big)
                 return 0
 
-            lax.fori_loop(0, chunks, attend, 0)
+            lax.fori_loop(0, bigs, attend, 0)
             return 0
 
         lax.fori_loop(0, micro, forward, 0)
 
         def backward(m, _):
             def enter(c, _):
-                span = span_of(c)
-                wait_g(m, c)
-                grad, low = norm_back(m, c, gain, (0, 2 * width))
-                dy[span] = grad
-                dc[span] = dot_nt(low, block_of(4)).astype(BF)
+                span = span_of(c, big)
+                wait_g(m, 2 * c)
+                wait_g(m, 2 * c + 1)
+                grad, low = norm_back(m, c, gain, (0, 2 * width), big)
+                zed[m, span] = grad
+                g_in[m, span] = dot_nt(low, block_of(4)).astype(BF)
                 return 0
 
-            lax.fori_loop(0, chunks, enter, 0)
+            lax.fori_loop(0, bigs, enter, 0)
 
             def heads(t, _):
                 off = pl.multiple_of(t * PAIR, PAIR)
@@ -450,7 +531,7 @@
                     axis=1,
                 )
                 v = qkvp[m, :, pl.ds(off + 2 * width, PAIR)]
-                grad_c = dc[:, pl.ds(off, PAIR)]
+                grad_c = g_in[m, :, pl.ds(off, PAIR)]
                 got = []
                 for side in range(2):
                     mask = lane if side == 0 else jnp.logical_not(lane)
@@ -484,17 +565,18 @@
             lax.fori_loop(0, pairs, heads, 0)
 
             def leave(c, _):
-                span = span_of(c)
-                total = dy[span]
+                span = span_of(c, big)
+                total = zed[m, span]
                 for i in range(3):
                     total = total + dot_nt(
                         qkvp[m, span, i * width : (i + 1) * width], block_of(i)
                     )
                 g_out[m, span] = total.astype(BF)
-                send_g(m, c)
+                send_g(m, 2 * c)
+                send_g(m, 2 * c + 1)
                 return 0
 
-            lax.fori_loop(0, chunks, leave, 0)
+            lax.fori_loop(0, bigs, leave, 0)
             return 0
 
         lax.fori_loop(0, micro, backward, 0)
@@ -548,22 +630,17 @@
         return ref[:, :, pl.ds(at, width)].reshape(tokens, width)
 
     if fused:
-        table, own = r.table, r.own
-
-        def spot(ref, e, by_chip):
-            return ref.at[pl.ds(4, 4), e - 4] if by_chip else ref.at[e]
-
-        def keep(e, by_chip):
-            slot = e % 2
-            return pltpu.make_async_copy(
-                stage.at[slot, :, core], spot(own, e, by_chip), r.keep_sem.at[slot]
-            )
+        table = r.table
+        low_half, high_half = pl.ds(0, half), pl.ds(half, half)
+
+        def add(target, other):
+            return (target.astype(F32) + other.astype(F32)).astype(BF)
 
         def give(e, by_chip):
             slot = e % 2
             return to_near(
-                stage.at[slot, :, 1 - core],
-                spot(table, e, by_chip),
+                stage.at[slot],
+                table.at[pl.ds(4, 4), e - 4] if by_chip else table.at[e],
                 r.p0_send.at[slot],
                 r.p0_recv.at[e],
                 near_c,
@@ -574,88 +651,28 @@
 
             @pl.when(e >= 2)
             def _():
-                keep(e, by_chip).wait()
                 give(e, by_chip).wait_send()
 
             low = value.astype(BF)
             if by_chip:
-                for p in range(2):
-                    for j in range(4):
-                        at = (p * 4 + j) * part
-                        stage[slot, j, p] = low[at : at + part]
+                sides = [low[: 4 * part].reshape(4, part, width), low[4 * part :].reshape(4, part, width)]
             else:
-                stage[slot] = low.reshape(4, 2, part, width)
-            keep(e, by_chip).start()
+                grid = low.reshape(4, 2, part, width)
+                sides = [grid[:, 0], grid[:, 1]]
+            stage[slot] = jnp.where(core == 0, sides[1], sides[0])
             give(e, by_chip).start()
-
-        def settle(e, by_chip):
-            keep(e, by_chip).wait()
-            give(e, by_chip).wait_send()
+            kept = jnp.where(core == 0, sides[0], sides[1])
+            if by_chip:
+                for j in range(4):
+                    at = pl.multiple_of(((4 + j) * 4 + e - 4) * part, part)
+                    w[pl.ds(at, part), :] = kept[j]
+            else:
+                at = pl.multiple_of(e * 4 * part, 4 * part)
+                w[pl.ds(at, 4 * part), :] = kept.reshape(4 * part, width)
 
         def finish(count, by_chip):
-            settle(count - 2, by_chip)
-            settle(count - 1, by_chip)
-    else:
-
-        def flush(slot, at):
-            return pltpu.make_async_copy(
-                stage.at[slot], r.dw_o.at[pl.ds(at, width)], r.keep_sem.at[slot]
-            )
-
-        def emit(e, value, by_chip):
-            slot = e % 2
-
-            @pl.when(e >= 2)
-            def _():
-                flush(slot, 0).wait()
-
-            stage[slot] = value.astype(BF)
-            flush(slot, pl.multiple_of(e * width, width)).start()
-
-        def finish(count, by_chip):
-            flush(0, 0).wait()
-            flush(1, 0).wait()
-
-    @pl.when(is_attn)
-    def _():
-        def step(e, _):
-            at = pl.multiple_of(e * width, width)
-            emit(e, dot_tn(tall(h_in, 0), tall(qkvp, at)), False)
-            return 0
-
-        lax.fori_loop(0, 3, step, 0)
-        emit(3, dot_tn(tall(place, 0), tall(qkvp, 3 * width)), False)
-        emit(4, dot_tn(tall(context, 0), tall(db, 0)), False)
-        finish(5, False)
-
-    @pl.when(is_feed)
-    def _():
-        def step(e, _):
-            at = pl.multiple_of(e * width + hidden, width)
-            emit(e, dot_tn(tall(h_in, 0), tall(saved, at)), False)
-            return 0
-
-        lax.fori_loop(0, blocks, step, 0)
-
-        def step_b(i, _):
-            at = pl.multiple_of(i * width, width)
-            emit(i + blocks, dot_tn(tall(saved, at), tall(db, 0)), True)
-            return 0
-
-        lax.fori_loop(0, blocks, step_b, 0)
-        finish(2 * blocks, True)
-
-    if not fused:
-        r.small_o[...] = colsum[...]
-    else:
-        low_half, high_half = pl.ds(0, half), pl.ds(half, half)
-
-        def fetch(u):
-            slot = u % 2
-            return pltpu.make_async_copy(own.at[u], stage.at[slot, :, 0], r.keep_sem.at[slot])
-
-        def add(target, other):
-            return (target.astype(F32) + other.astype(F32)).astype(BF)
+            give(count - 2, by_chip).wait_send()
+            give(count - 1, by_chip).wait_send()
 
         def one_x(u, y):
             return to_near(
@@ -693,42 +710,46 @@
                 near_x,
             )
 
-        sm = r.small
-        for dest in range(8):
-            row = sm.at[dest // 4, (dest // 2) % 2, dest % 2]
-            at = dest * part
-
-            @pl.when(is_attn)
-            def _(row=row, at=at):
-                for i in range(3):
-                    row[i : i + 1, :part] = colsum[0:1, i * width + at : i * width + at + part]
-
-            @pl.when(is_feed)
-            def _(row=row, dest=dest):
-                for i in range(3):
-                    lane_at = dest * 4 * part + i * 128
-                    row[i : i + 1, :] = colsum[0:1, lane_at : lane_at + 128]
-
-            for i in range(3):
-                row[3 + i : 4 + i, :part] = colsum[1:2, i * width + at : i * width + at + part]
-        small_c = to_near(
-            sm.at[:, :, 1 - core], r.small_0, r.s_send.at[0], r.s_recv.at[0], near_c
-        )
-        small_x = to_near(
-            sm.at[:, 1 - cx, core], r.small_1, r.s_send.at[1], r.s_recv.at[1], near_x
-        )
-        small_y = to_near(
-            sm.at[1 - cy, cx, core], r.small_2, r.s_send.at[2], r.s_recv.at[2], near_y
-        )
-        small_c.start()
-
-        fetch(0).start()
-
-        def merge_core(u, _):
-            @pl.when(u + 1 < units)
-            def _():
-                fetch(u + 1).start()
-
+        def left_own(u):
+            return to_section(
+                table.at[u, chip],
+                r.all_w.at[s, u],
+                r.left_send.at[s, u],
+                r.all_recv.at[s, u],
+                (s - 1 + sections) % sections,
+            )
+
+        def left_on(t, u):
+            return to_section(
+                r.all_w.at[t, u],
+                r.all_w.at[t, u],
+                r.left_send.at[t, u],
+                r.all_recv.at[t, u],
+                (s - 1 + sections) % sections,
+            )
+
+        def right_own(u):
+            return to_section(
+                table.at[u, chip],
+                r.all_w.at[s, u],
+                r.right_send.at[s, u],
+                r.all_recv.at[s, u],
+                (s + 1) % sections,
+            )
+
+        def right_on(t, u):
+            return to_section(
+                r.all_w.at[t, u],
+                r.all_w.at[t, u],
+                r.right_send.at[t, u],
+                r.all_recv.at[t, u],
+                (s + 1) % sections,
+            )
+
+        def mine(u):
+            return pltpu.make_async_copy(table.at[u, chip], r.all_w.at[s, u], r.own_sem.at[u])
+
+        def merge_core(u):
             @pl.when(u <= 4)
             def _():
                 give(u, False).wait_recv()
@@ -738,22 +759,13 @@
                 for e in range(5, 8):
                     give(e, True).wait_recv()
 
-            fetch(u).wait()
-            table[u] = add(table[u], stage[u % 2, :, 0])
+            at = pl.multiple_of(u * 4 * part, 4 * part)
+            table[u] = add(table[u], w[pl.ds(at, 4 * part), :].reshape(4, part, width))
             for y in range(2):
                 one_x(u, y).start()
             one_y(u).start()
-            return 0
-
-        lax.fori_loop(0, units, merge_core, 0)
-
-        small_c.wait_recv()
-        for y in range(2):
-            for x in range(2):
-                sm[y, x, core] = sm[y, x, core] + r.small_0[y, x]
-        small_x.start()
-
-        def merge_one(u, _):
+
+        def merge_one(u):
             for y in range(2):
                 one_x(u, y).wait_recv()
                 at = 2 * y + cx
@@ -764,46 +776,8 @@
                 at = 2 * cy + x
                 table[u, at, half:] = add(table[u, at, half:], r.land_y[u, x])
             two_x(u).start()
-            return 0
-
-        lax.fori_loop(0, units, merge_one, 0)
-
-        small_x.wait_recv()
-        for y in range(2):
-            sm[y, cx, core] = sm[y, cx, core] + r.small_1[y]
-        small_y.start()
-
-        def left(u, by):
-            return to_section(
-                table.at[u, chip],
-                r.all_w.at[s, u],
-                r.left_send.at[by, u],
-                r.all_recv.at[s, u],
-                (s - by + sections) % sections,
-            )
-
-        def right_own(u):
-            return to_section(
-                table.at[u, chip],
-                r.all_w.at[s, u],
-                r.right_send.at[s, u],
-                r.all_recv.at[s, u],
-                (s + 1) % sections,
-            )
-
-        def right_on(t, u):
-            return to_section(
-                r.all_w.at[t, u],
-                r.all_w.at[t, u],
-                r.right_send.at[t, u],
-                r.all_recv.at[t, u],
-                (s + 1) % sections,
-            )
-
-        def mine(u):
-            return pltpu.make_async_copy(table.at[u, chip], r.all_w.at[s, u], r.own_sem.at[u])
-
-        def merge_two(u, _):
+
+        def merge_two(u):
             two_y(u).wait_recv()
             table[u, chip, :half] = add(table[u, chip, :half], r.land_y2[u])
             two_x(u).wait_recv()
@@ -813,31 +787,180 @@
             def _():
                 right_own(u).start()
 
-            for by in range(1, sections):
-
-                @pl.when(s >= by)
-                def _(by=by):
-                    left(u, by).start()
+            @pl.when(s != 0)
+            def _():
+                left_own(u).start()
 
             mine(u).start()
-            return 0
-
-        lax.fori_loop(0, units, merge_two, 0)
-
-        small_y.wait_recv()
-        sm[cy, cx, core] = sm[cy, cx, core] + r.small_2[...]
-        small_z = [
-            to_section(
-                sm.at[cy, cx, core],
+
+        late = 3 * kind
+
+        def at_step(q, merge):
+            @pl.when(jnp.logical_and(q >= 0, q < 4))
+            def _():
+                merge(q)
+
+            @pl.when(jnp.logical_and(q >= 4 + late, q < units + late))
+            def _():
+                merge(q - late)
+
+        def advance(q):
+            at_step(q, merge_core)
+            at_step(q - 2, merge_one)
+            at_step(q - 4, merge_two)
+
+        beyond = last - s
+        hand_on = jnp.where(s > 0, 13 * (beyond // 2) + 8 * (beyond % 2), 0)
+
+        def relay_left(k):
+            @pl.when(jnp.logical_and(k >= 0, k < hand_on))
+            def _():
+                odd = (k % 13) // 8
+                t = last - 2 * (k // 13) - odd
+                copy = left_on(t, k % 13 - 8 * odd)
+                copy.wait_recv()
+                copy.start()
+
+        sm = r.small
+        for dest in range(8):
+            at = dest * part
+
+            @pl.when(is_attn)
+            def _(dest=dest, at=at):
+                for i in range(3):
+                    sm[dest, i : i + 1, :part] = colsum[
+                        0:1, i * width + at : i * width + at + part
+                    ]
+
+            @pl.when(is_feed)
+            def _(dest=dest):
+                for i in range(3):
+                    lane_at = dest * 4 * part + i * 128
+                    sm[dest, i : i + 1, :] = colsum[0:1, lane_at : lane_at + 128]
+
+            for i in range(3):
+                sm[dest, 3 + i : 4 + i, :part] = colsum[
+                    1:2, i * width + at : i * width + at + part
+                ]
+
+        def small_copy(t):
+            return to_near(
+                sm.at[peer(t)], r.small_in.at[t - 1], r.s_send.at[t - 1], r.s_recv.at[t - 1], peer(t)
+            )
+
+        def small_share(by):
+            return to_section(
+                r.small_sum,
                 r.all_s.at[s],
                 r.sz_send.at[by - 1],
                 r.sz_recv.at[s],
                 (s + by) % sections,
             )
-            for by in range(1, sections)
-        ]
-        for copy in small_z:
-            copy.start()
+
+        for t in range(1, 8):
+            small_copy(t).start()
+        over_units(gather_sent)
+        for t in range(1, 8):
+            vec_copy(t, d).wait_send()
+    else:
+
+        def flush(slot, at):
+            return pltpu.make_async_copy(
+                stage.at[slot], r.dw_o.at[pl.ds(at, width)], r.keep_sem.at[slot]
+            )
+
+        def emit(e, value, by_chip):
+            slot = e % 2
+
+            @pl.when(e >= 2)
+            def _():
+                flush(slot, 0).wait()
+
+            stage[slot] = value.astype(BF)
+            flush(slot, pl.multiple_of(e * width, width)).start()
+
+        def finish(count, by_chip):
+            flush(0, 0).wait()
+            flush(1, 0).wait()
+
+        def advance(u):
+            pass
+
+        def relay_left(k):
+            pass
+
+    @pl.when(is_attn)
+    def _():
+        def step(e, _):
+            at = pl.multiple_of(e * width, width)
+            emit(e, dot_tn(tall(h_in, 0), tall(qkvp, at)), False)
+            advance(e - 1)
+            return 0
+
+        lax.fori_loop(0, 3, step, 0)
+        emit(3, dot_tn(tall(place, 0), tall(qkvp, 3 * width)), False)
+        advance(jnp.int32(2))
+        emit(4, dot_tn(tall(context, 0), tall(db, 0)), False)
+        advance(jnp.int32(3))
+        finish(5, False)
+
+    @pl.when(is_feed)
+    def _():
+        def step(e, _):
+            at = pl.multiple_of(e * width + hidden, width)
+            emit(e, dot_tn(tall(h_in, 0), tall(saved, at)), False)
+            advance(e - 1)
+            relay_left(e - 2)
+            return 0
+
+        lax.fori_loop(0, blocks, step, 0)
+
+        def step_b(i, _):
+            at = pl.multiple_of(i * width, width)
+            emit(i + blocks, dot_tn(tall(saved, at), tall(db, 0)), True)
+            advance(i + blocks - 1)
+            relay_left(i + blocks - 2)
+            return 0
+
+        lax.fori_loop(0, blocks, step_b, 0)
+        finish(2 * blocks, True)
+
+    if not fused:
+        r.small_o[...] = colsum[...]
+
+        @pl.when(s == last)
+        def _():
+            for j in range(sections - 1):
+                share(h_out, r.fin_in, r.fin_send, r.fin_recv, micro - 1, j).start()
+    else:
+
+        def go_on(q, _):
+            advance(q)
+            relay_left(kind * (q - 1) + (1 - kind) * (2 * q - 8))
+            relay_left((1 - kind) * (2 * q - 7) - kind)
+            return 0
+
+        for t in range(1, 8):
+            small_copy(t).wait_recv()
+        total = sm[d]
+        for t in range(7):
+            total = total + r.small_in[t]
+        r.small_sum[...] = total
+        for by in range(1, sections):
+            small_share(by).start()
+        lax.fori_loop(4 + late, units + late + 4, go_on, 0)
+
+        def rest_left(k, _):
+            relay_left(k)
+            return 0
+
+        lax.fori_loop(10 + 4 * kind, hand_on, rest_left, 0)
+
+        @pl.when(s == last)
+        def _():
+            for j in range(sections - 1):
+                share(h_out, r.fin_in, r.fin_send, r.fin_recv, micro - 1, j).start()
+
 
         for by in range(1, sections):
 
@@ -858,12 +981,12 @@
 
         for by in range(1, sections):
 
-            @pl.when(s + by < sections)
+            @pl.when(jnp.logical_and(s + by < sections, s == 0))
             def _(by=by):
                 t = s + by
 
                 def arrive(u, _):
-                    right_on(t, u).wait_recv()
+                    left_on(t, u).wait_recv()
                     return 0
 
                 lax.fori_loop(0, 5 + 3 * (t % 2), arrive, 0)
@@ -871,22 +994,14 @@
         for by in range(1, sections):
             t = (s + by) % sections
             to_section(
-                sm.at[cy, cx, core],
-                r.all_s.at[t],
-                r.sz_send.at[by - 1],
-                r.sz_recv.at[t],
-                t,
+                r.small_sum, r.all_s.at[t], r.sz_send.at[by - 1], r.sz_recv.at[t], t
             ).wait_recv()
-        r.all_s[s] = sm[cy, cx, core]
-
-        over_units(gather_sent)
-        for t, (mine_v, theirs, near) in enumerate(swaps):
-            to_near(mine_v, mine_v, r.v_send.at[t], r.v_recv.at[t], near).wait_send()
-        small_c.wait_send()
-        small_x.wait_send()
-        small_y.wait_send()
-        for copy in small_z:
-            copy.wait_send()
+        r.all_s[s] = r.small_sum[...]
+
+        for t in range(1, 8):
+            small_copy(t).wait_send()
+        for by in range(1, sections):
+            small_share(by).wait_send()
 
         def sent(u, _):
             for y in range(2):
@@ -900,11 +1015,9 @@
             def _():
                 right_own(u).wait_send()
 
-            for by in range(1, sections):
-
-                @pl.when(s >= by)
-                def _(by=by):
-                    left(u, by).wait_send()
+            @pl.when(s != 0)
+            def _():
+                left_own(u).wait_send()
 
             return 0
 
@@ -917,6 +1030,18 @@
 
                 def relayed(u, _):
                     right_on(t, u).wait_send()
+                    return 0
+
+                lax.fori_loop(0, 5 + 3 * (t % 2), relayed, 0)
+
+        for by in range(1, sections):
+
+            @pl.when(jnp.logical_and(s + by < sections, s != 0))
+            def _(by=by):
+                t = s + by
+
+                def relayed(u, _):
+                    left_on(t, u).wait_send()
                     return 0
 
                 lax.fori_loop(0, 5 + 3 * (t % 2), relayed, 0)
@@ -962,7 +1087,7 @@
 def pipeline(fused, hidden, inputs):
     micro, length, width = inputs["pages"].shape
     sections = lax.axis_size("section")
-    rows = length // 2
+    rows = length // sections
     chunks = length // rows
     quarter = length // sections
     heads = width // HEAD_DIM
@@ -974,14 +1099,16 @@
     act = (micro, length, width)
     dma = pltpu.SemaphoreType.DMA
     spec = {name: hbm for name in inputs}
-    for name in ("place", "hide", "vec_in", "vec_own"):
-        if name in spec:
+    for name in spec:
+        if name not in ("pages", "cot", "w_in", "qkv_w", "pos_w", "out_w", "in_w", "down_w"):
             spec[name] = vmem
     outs = {
         "final_o": (vmem, (micro, quarter, width), BF),
         "igrad_o": (vmem, (micro, quarter, width), F32),
     }
     scratch = {
+        "place": pltpu.VMEM(act, BF),
+        "hide": pltpu.VMEM((micro, length, length), BF),
         "h_in": pltpu.VMEM(act, BF),
         "g_in": pltpu.VMEM(act, BF),
         "h_out": pltpu.VMEM(act, BF),
@@ -993,8 +1120,6 @@
         "zed": pltpu.VMEM(act, F32),
         "rstd": pltpu.VMEM((micro, length, 128), F32),
         "db": pltpu.VMEM(act, BF),
-        "dc": pltpu.VMEM((length, width), BF),
-        "dy": pltpu.VMEM((length, width), F32),
         "w": pltpu.VMEM((2 * hidden, width), BF),
         "vec": pltpu.VMEM((8, hidden), F32),
         "colsum": pltpu.VMEM((8, hidden), F32),
@@ -1013,14 +1138,12 @@
     if fused:
         outs["all_w"] = (hbm, (sections, 8, part, width), BF)
         outs["all_s"] = (vmem, (sections, 8, 128), F32)
-        outs["own"] = (hbm, (8, 4, part, width), BF)
         scratch.update(
-            stage=pltpu.VMEM((2, 4, 2, part, width), BF),
-            vec_all=pltpu.VMEM((2, 2, 2, 8, 128), F32),
-            small=pltpu.VMEM((2, 2, 2, 8, 128), F32),
-            small_0=pltpu.VMEM((2, 2, 8, 128), F32),
-            small_1=pltpu.VMEM((2, 8, 128), F32),
-            small_2=pltpu.VMEM((8, 128), F32),
+            stage=pltpu.VMEM((2, 4, part, width), BF),
+            vec_all=pltpu.VMEM((8, 8, 128), F32),
+            small=pltpu.VMEM((8, 8, 128), F32),
+            small_in=pltpu.VMEM((7, 8, 128), F32),
+            small_sum=pltpu.VMEM((8, 128), F32),
             table=pltpu.VMEM((8, 4, part, width), BF),
             land_x=pltpu.VMEM((8, 2, half, width), BF),
             land_y=pltpu.VMEM((8, 2, half, width), BF),
@@ -1029,10 +1152,10 @@
             own_sem=dma((8,)),
             ag_send=dma((8, 8)),
             ag_recv=dma((8, 8)),
-            v_send=dma((3,)),
-            v_recv=dma((3,)),
-            s_send=dma((3,)),
-            s_recv=dma((3,)),
+            v_send=dma((7,)),
+            v_recv=dma((7,)),
+            s_send=dma((7,)),
+            s_recv=dma((7,)),
             sz_send=dma((sections - 1,)),
             sz_recv=dma((sections,)),
             p0_send=dma((2,)),
@@ -1068,25 +1191,6 @@
     return dict(zip(outs, got, strict=True))
 
 
-def sinusoid(coord_pair, model_width):
-    quarter = model_width // 4
-    frequency = jnp.exp(jnp.arange(quarter, dtype=F32) * (-math.log(10000.0) / quarter))
-    angles = coord_pair.astype(F32)[:, :, :, None] * frequency
-    waves = jnp.stack([jnp.sin(angles), jnp.cos(angles)], axis=3)
-    pages, axes, length = coord_pair.shape
-    return waves.transpose(0, 2, 1, 3, 4).reshape(pages, length, model_width).astype(BF)
-
-
-def hidden_bias(boxes, length):
-    spots = jnp.arange(length, dtype=jnp.int32)
-    row_hit = (spots >= boxes[:, :, 0:1]) & (spots < boxes[:, :, 1:2])
-    col_hit = (spots >= boxes[:, :, 2:3]) & (spots < boxes[:, :, 3:4])
-    covered = jnp.einsum(
-        "pbi,pbj->pij", row_hit.astype(BF), col_hit.astype(BF), preferred_element_type=F32
-    )
-    return jnp.where(covered < 0.5, 0.0, NEGATIVE).astype(BF)
-
-
 def shards(
     pages_in,
     coords,
@@ -1115,29 +1219,25 @@
     def pick(array):
         return lax.dynamic_index_in_dim(array, layer, 0, keepdims=False)
 
-    norm_row = s % 2
-    gain_own = lax.dynamic_index_in_dim(pick(ln_gain), norm_row, 0, keepdims=False)
-    offset_own = lax.dynamic_index_in_dim(pick(ln_bias), norm_row, 0, keepdims=False)
     inputs = {
         "pages": pages_in,
         "cot": cotangent,
-        "place": sinusoid(coords, width),
-        "hide": hidden_bias(boxes, length),
+        "coords": coords,
+        "boxes": boxes.transpose(0, 2, 1),
+        "waves": turns_per_unit(width),
     }
     if groups == 8:
-        first = jnp.where(
-            is_attn,
-            jnp.pad(pick(attn_bias), ((0, 0), (0, 128 - part))),
-            pick(ffn_in_bias).reshape(3, 128),
-        )
-        rest = jnp.pad(
-            jnp.stack([pick(ffn_out_bias), gain_own, offset_own]), ((0, 0), (0, 128 - part))
-        )
-        inputs["vec_own"] = jnp.pad(
-            jnp.concatenate([first, rest], axis=0).astype(F32), ((0, 2), (0, 0))
-        )
         inputs.update(
-            qkv_w=qkv_weight, pos_w=pos_weight, out_w=out_weight, in_w=ffn_in, down_w=ffn_out
+            qkv_w=qkv_weight,
+            pos_w=pos_weight,
+            out_w=out_weight,
+            in_w=ffn_in,
+            down_w=ffn_out,
+            attn_b=attn_bias.transpose(1, 0, 2),
+            in_b=ffn_in_bias,
+            down_b=ffn_out_bias,
+            gain_w=ln_gain,
+            offset_w=ln_bias,
         )
         got = pipeline(True, hidden, inputs)
         sections = lax.axis_size("section")
@@ -1164,6 +1264,9 @@
             rest[:, :, 2],
         )
 
+    norm_row = s % 2
+    gain_own = lax.dynamic_index_in_dim(pick(ln_gain), norm_row, 0, keepdims=False)
+    offset_own = lax.dynamic_index_in_dim(pick(ln_bias), norm_row, 0, keepdims=False)
     own_a = jnp.where(
         is_attn, jnp.concatenate([pick(qkv_weight), pick(pos_weight)], axis=1), pick(ffn_in)
     )

time: 340 us -> 296 us (0.87)
  the two profiles are of different devices: /device:TPU:24 before, /device:TPU:0 now
where the time goes in v3:
time: 296 us; the launch traced here: 294 us
  Pallas kernels  281 us (95%)
  local copies, waits for them, and re-layouts  9.67 us (3%)
  other arithmetic  3.18 us (1%)
    pallas_call x1, Pallas kernels, pipeline(): pl.pallas_call(partial(pipeline_kernel, names, rows, fused), out_shape=tu...  281 us

profile of v3, /device:TPU:0, one launch (start us, length us, event | category | flops | bytes accessed | tf_op | source)
XLA Modules:
  0.0 294.2 jit_solution(1159455523078437293)
XLA Ops:
  0.6 280.6 %pipeline.1 = (bf16[2,128,768]{2,1,0:T(8,128)(2,1)}, f32[2,128,768]{2,1,0:T(8,128)}, bf16[4,8,96,768]{3,2,1,0:T(8,128)(2,1)}, f32[4,8,128]{2,1,0:T(8,128)}) custom-call(bf16[2,512,768]{2,1,0:T(8,128)(2,1)} %refs_0_.1, bf16[2,512,768]{2,1,0:T(8,128)(2,1)} %refs_1_.1, s32[2,2,512]{2,1,0:T(2,128)} %refs_2_.1, s32[2,4,16]{2,1,0:T(4,128)} %bitcast.42, ...), custom_call_target="tpu_custom_call" | custom-call | tf_op jit(solution)/shard_map/pipeline/pallas_call | solution.py:1180
  281.3 2.7 fusion.2
  284.0 0.1 convert_bitcast_fusion.1
  284.1 0.0 copy-start.2
  284.1 1.3 copy.40
  285.5 0.0 copy-done.2
  285.5 0.6 copy.36
  286.1 1.1 fusion
  287.2 0.3 fusion.3
  287.4 1.7 copy.41
  289.1 0.0 copy-start.1
  289.1 0.0 copy-start
  289.2 0.6 copy.44
  289.7 1.7 bitcast_convert_fusion
  291.4 0.6 slice.57
  292.0 0.6 fusion.4
  292.5 0.0 copy-done.1
  292.5 0.7 copy.47
  293.3 0.0 copy-done
  293.3 0.9 copy.48
  (3 shorter events, 0.0 us)
Async XLA Ops:
  284.1 1.3 copy-start.2
  289.1 3.4 %copy-start.1 = (bf16[2,128,768]{2,1,0:T(8,128)(2,1)S(1)}, bf16[2,128,768]{2,1,0:T(8,128)(2,1)}, u32[]{:S(2)}) copy-start(bf16[2,128,768]{2,1,0:T(8,128)(2,1)} %get-tuple-element.64) | copy-start | bytes 1179652
  289.1 4.1 %copy-start = (f32[2,128,768]{2,1,0:T(8,128)S(1)}, f32[2,128,768]{2,1,0:T(8,128)}, u32[]{:S(2)}) copy-start(f32[2,128,768]{2,1,0:T(8,128)} %get-tuple-element.65) | copy-start | bytes 2359300

commit v4 on v3

--- a/solution.py
+++ b/solution.py
@@ -122,7 +122,6 @@
     if fused:
         for t in range(1, 8):
             pl.semaphore_signal(barrier, inc=1, device_id={"dp": peer(t)}, device_id_type=MESH)
-    pl.semaphore_wait(barrier, sections - 1 + (7 if fused else 0))
 
     def to_section(source, target, send, recv, at):
         return pltpu.make_async_remote_copy(
@@ -200,9 +199,6 @@
         def _():
             hop(h_out, h_in, r.fsend, r.frecv, m, c, 1).start()
 
-        @pl.when(jnp.logical_and(jnp.logical_and(s == last, c != s), m < micro - 1))
-        def _():
-            share(h_out, r.fin_in, r.fin_send, r.fin_recv, m, c).start()
 
     def send_g(m, c):
         @pl.when(s != 0)
@@ -356,6 +352,7 @@
                 mine_v, r.vec_all.at[source], r.v_send.at[t - 1], r.v_recv.at[t - 1], peer(t)
             )
 
+        pl.semaphore_wait(barrier, sections - 1 + 7)
         for t in range(1, 8):
             vec_copy(t, d).start()
         over_units(first_round)
@@ -385,13 +382,33 @@
                 vec[1:2, i * width + at : i * width + at + part] = row[3 + i : 4 + i, :part]
 
         over_units(second_round)
-        over_units(third_round)
-        over_units(last_round)
+
+        def rounds(tail, i):
+            third_round(tail, i)
+            last_round(tail, i)
+
+        def over_head(step):
+            def head(i, _):
+                step(False, i)
+                return 0
+
+            lax.fori_loop(0, 4, head, 0)
+
+        @pl.when(is_attn)
+        def _():
+            over_head(third_round)
+            over_head(last_round)
+
+        @pl.when(is_feed)
+        def _():
+            over_units(third_round)
+            over_units(last_round)
     else:
         whole = pltpu.make_async_copy(r.w_in, w, r.own_sem)
         whole.start()
         vec[...] = r.vec_in[...]
         spots()
+        pl.semaphore_wait(barrier, sections - 1)
         whole.wait()
 
     def norm_out(m, c, summed, gain, offset, size=rows):
@@ -462,42 +479,46 @@
 
             lax.fori_loop(0, bigs, project, 0)
 
+            def heads(t, _):
+                off = pl.multiple_of(t * PAIR, PAIR)
+                left = jnp.concatenate(
+                    [qkvp[m, :, pl.ds(off, PAIR)], qkvp[m, :, pl.ds(off + 3 * width, PAIR)]],
+                    axis=1,
+                )
+                right = jnp.concatenate(
+                    [kplus[m, :, pl.ds(off, PAIR)], qkvp[m, :, pl.ds(off + width, PAIR)]],
+                    axis=1,
+                )
+                v = qkvp[m, :, pl.ds(off + 2 * width, PAIR)]
+                bias = hide[m].astype(F32)
+                mixed = []
+                blank = jnp.zeros_like(left)
+                both = jnp.concatenate(
+                    [jnp.where(lane2, left, blank), jnp.where(lane2, blank, left)], axis=0
+                )
+                raw = dot_nt(both, right)
+                for side in range(2):
+                    score = raw[side * length : (side + 1) * length] * (SCORE_SCALE * LOG2E) + bias
+                    top = jnp.max(score, axis=1, keepdims=True)
+                    power = jnp.exp2(score - top)
+                    total = jnp.sum(power, axis=1, keepdims=True)
+                    prob = (power * (1.0 / total)).astype(BF)
+                    at = pl.multiple_of((2 * t + side) * length, length)
+                    saved[m, :, pl.ds(at, length)] = prob
+                    mixed.append(dot_nn(prob, v))
+                context[m, :, pl.ds(off, PAIR)] = jnp.where(lane, mixed[0], mixed[1]).astype(BF)
+                return 0
+
+            lax.fori_loop(0, pairs, heads, 0, unroll=2)
+
+            if fused:
+
+                @pl.when(m == 0)
+                def _():
+                    rounds(True, 0)
+
             def attend(c, _):
                 span = span_of(c, big)
-
-                def heads(t, _):
-                    off = pl.multiple_of(t * PAIR, PAIR)
-                    left = jnp.concatenate(
-                        [
-                            qkvp[m, span, pl.ds(off, PAIR)],
-                            qkvp[m, span, pl.ds(off + 3 * width, PAIR)],
-                        ],
-                        axis=1,
-                    )
-                    right = jnp.concatenate(
-                        [kplus[m, :, pl.ds(off, PAIR)], qkvp[m, :, pl.ds(off + width, PAIR)]],
-                        axis=1,
-                    )
-                    v = qkvp[m, :, pl.ds(off + 2 * width, PAIR)]
-                    bias = hide[m, span].astype(F32)
-                    mixed = []
-                    for side in range(2):
-                        mask = lane2 if side == 0 else jnp.logical_not(lane2)
-                        masked = jnp.where(mask, left, jnp.zeros_like(left))
-                        score = dot_nt(masked, right) * (SCORE_SCALE * LOG2E) + bias
-                        top = jnp.max(score, axis=1, keepdims=True)
-                        power = jnp.exp2(score - top)
-                        total = jnp.sum(power, axis=1, keepdims=True)
-                        prob = (power * (1.0 / total)).astype(BF)
-                        at = pl.multiple_of((2 * t + side) * length, length)
-                        saved[m, span, pl.ds(at, length)] = prob
-                        mixed.append(dot_nn(prob, v))
-                    context[m, span, pl.ds(off, PAIR)] = jnp.where(
-                        lane, mixed[0], mixed[1]
-                    ).astype(BF)
-                    return 0
-
-                lax.fori_loop(0, pairs, heads, 0)
                 branch = dot_nn(context[m, span], block_of(4))
                 summed = h_in[m, span].astype(F32) + branch + vec[0:1, 2 * width : 3 * width]
                 norm_out(m, c, summed, gain, offset, big)
@@ -532,21 +553,25 @@
                 )
                 v = qkvp[m, :, pl.ds(off + 2 * width, PAIR)]
                 grad_c = g_in[m, :, pl.ds(off, PAIR)]
-                got = []
+                blank = jnp.zeros_like(grad_c)
+                both = jnp.concatenate(
+                    [jnp.where(lane, grad_c, blank), jnp.where(lane, blank, grad_c)], axis=0
+                )
+                at = pl.multiple_of(2 * t * length, 2 * length)
+                prob = saved[m, :, pl.ds(at, 2 * length)]
+                grad_p = dot_nt(both, v)
+                grad_s = []
                 for side in range(2):
-                    mask = lane if side == 0 else jnp.logical_not(lane)
-                    at = pl.multiple_of((2 * t + side) * length, length)
-                    prob = saved[m, :, pl.ds(at, length)]
-                    wide_p = prob.astype(F32)
-                    grad_p = dot_nt(jnp.where(mask, grad_c, jnp.zeros_like(grad_c)), v)
-                    dot_row = jnp.sum(wide_p * grad_p, axis=1, keepdims=True)
-                    grad_s = (wide_p * (grad_p - dot_row)).astype(BF)
-                    got.append(
-                        (dot_tn(prob, grad_c), dot_nn(grad_s, right), dot_tn(grad_s, left))
-                    )
-                grad_v = jnp.where(lane, got[0][0], got[1][0]).astype(BF)
-                grad_l = jnp.where(lane2, got[0][1], got[1][1])
-                grad_r = jnp.where(lane2, got[0][2], got[1][2])
+                    wide_p = prob[:, side * length : (side + 1) * length].astype(F32)
+                    part_p = grad_p[side * length : (side + 1) * length]
+                    dot_row = jnp.sum(wide_p * part_p, axis=1, keepdims=True)
+                    grad_s.append((wide_p * (part_p - dot_row)).astype(BF))
+                got_v = dot_tn(prob, grad_c)
+                got_l = dot_nn(jnp.concatenate(grad_s, axis=0), right)
+                got_r = dot_tn(jnp.concatenate(grad_s, axis=1), left)
+                grad_v = jnp.where(lane, got_v[:length], got_v[length:]).astype(BF)
+                grad_l = jnp.where(lane2, got_l[:length], got_l[length:])
+                grad_r = jnp.where(lane2, got_r[:length], got_r[length:])
                 grad_q = (grad_l[:, :PAIR] * SCORE_SCALE).astype(BF)
                 grad_k = ((grad_r[:, :PAIR] + grad_r[:, PAIR:]) * SCORE_SCALE).astype(BF)
                 grad_pl = ((grad_l[:, PAIR:] + grad_r[:, :PAIR]) * SCORE_SCALE).astype(BF)
@@ -562,7 +587,7 @@
                 )
                 return 0
 
-            lax.fori_loop(0, pairs, heads, 0)
+            lax.fori_loop(0, pairs, heads, 0, unroll=2)
 
             def leave(c, _):
                 span = span_of(c, big)
@@ -600,13 +625,12 @@
             norm_out(m, c, summed, gain, offset)
             return 0
 
-        lax.fori_loop(0, micro * chunks, forward, 0)
-
-        def backward(idx, _):
-            m, c = idx // chunks, idx % chunks
-            span = span_of(c)
-            wait_g(m, c)
-            total, low = norm_back(m, c, gain, (1, 0))
+        def backward(m, c, size):
+            span = span_of(c, size)
+            hops = size // rows
+            for i in range(hops):
+                wait_g(m, c * hops + i)
+            total, low = norm_back(m, c, gain, (1, 0), size)
             for f in range(blocks):
                 at = f * width
                 grad_a = dot_nt(low, block_of(blocks + f)).astype(BF).astype(F32)
@@ -618,10 +642,29 @@
                 )
                 total = total + dot_nt(grad_i, block_of(f))
             g_out[m, span] = total.astype(BF)
-            send_g(m, c)
+            for i in range(hops):
+                send_g(m, c * hops + i)
+
+        def step(i, _):
+            page, c = i // chunks, i % chunks
+            turn = jnp.where(s == last, page % 2, page // micro)
+            m = jnp.where(s == last, page // 2, page % micro)
+
+            @pl.when(turn == 0)
+            def _():
+                forward(m * chunks + c, 0)
+
+            @pl.when(jnp.logical_and(turn == 1, s != last))
+            def _():
+                backward(m, c, rows)
+
+            @pl.when(jnp.logical_and(jnp.logical_and(turn == 1, s == last), c % 2 == 0))
+            def _():
+                backward(m, c // 2, big)
+
             return 0
 
-        lax.fori_loop(0, micro * chunks, backward, 0)
+        lax.fori_loop(0, 2 * micro * chunks, step, 0)
 
     tokens = micro * length
     stage = r.stage
@@ -787,7 +830,7 @@
             def _():
                 right_own(u).start()
 
-            @pl.when(s != 0)
+            @pl.when(s == last)
             def _():
                 left_own(u).start()
 
@@ -910,7 +953,7 @@
             at = pl.multiple_of(e * width + hidden, width)
             emit(e, dot_tn(tall(h_in, 0), tall(saved, at)), False)
             advance(e - 1)
-            relay_left(e - 2)
+            relay_left(e // 2 - 100 * (e % 2))
             return 0
 
         lax.fori_loop(0, blocks, step, 0)
@@ -919,7 +962,7 @@
             at = pl.multiple_of(i * width, width)
             emit(i + blocks, dot_tn(tall(saved, at), tall(db, 0)), True)
             advance(i + blocks - 1)
-            relay_left(i + blocks - 2)
+            relay_left((i + blocks) // 2 - 100 * (i % 2))
             return 0
 
         lax.fori_loop(0, blocks, step_b, 0)
@@ -930,14 +973,14 @@
 
         @pl.when(s == last)
         def _():
-            for j in range(sections - 1):
-                share(h_out, r.fin_in, r.fin_send, r.fin_recv, micro - 1, j).start()
+            for m in range(micro):
+                for j in range(sections - 1):
+                    share(h_out, r.fin_in, r.fin_send, r.fin_recv, m, j).start()
     else:
 
         def go_on(q, _):
             advance(q)
-            relay_left(kind * (q - 1) + (1 - kind) * (2 * q - 8))
-            relay_left((1 - kind) * (2 * q - 7) - kind)
+            relay_left(q - 4 + kind)
             return 0
 
         for t in range(1, 8):
@@ -954,12 +997,22 @@
             relay_left(k)
             return 0
 
-        lax.fori_loop(10 + 4 * kind, hand_on, rest_left, 0)
+        lax.fori_loop(5 + 7 * kind, hand_on, rest_left, 0)
+
+        @pl.when(jnp.logical_and(s > 0, s < last))
+        def _():
+            def own_left(u, _):
+                left_own(u).start()
+                return 0
+
+            lax.fori_loop(0, units, own_left, 0)
+
 
         @pl.when(s == last)
         def _():
-            for j in range(sections - 1):
-                share(h_out, r.fin_in, r.fin_send, r.fin_recv, micro - 1, j).start()
+            for m in range(micro):
+                for j in range(sections - 1):
+                    share(h_out, r.fin_in, r.fin_send, r.fin_recv, m, j).start()
 
 
         for by in range(1, sections):
@@ -1191,6 +1244,59 @@
     return dict(zip(outs, got, strict=True))
 
 
+def spread_kernel(final, igrad, shares, sums, final_o, igrad_o, qkv, bias, pos, out, into, into_b, down, down_b, gain, offset):
+    final_o[...] = final[...]
+    igrad_o[...] = igrad[...]
+    layers, part, width = pos.shape
+    for n in range(layers):
+        attn, feed = 2 * n, 2 * n + 1
+        for i in range(3):
+            qkv[n, :, i * width : (i + 1) * width] = shares[attn, i].astype(F32)
+        pos[n] = shares[attn, 3].astype(F32)
+        out[n] = shares[attn, 4].astype(F32)
+        for i in range(4):
+            into[n, :, i * width : (i + 1) * width] = shares[feed, i].astype(F32)
+            down[n, i * part : (i + 1) * part, :] = shares[feed, 4 + i].astype(F32)
+        bias[n] = sums[attn, 0:3, :part]
+        for i in range(3):
+            into_b[n : n + 1, i * 128 : (i + 1) * 128] = sums[feed, i : i + 1, :]
+        down_b[n : n + 1, :] = sums[feed, 3:4, :part]
+        for k in range(2):
+            gain[n, k : k + 1, :] = sums[2 * n + k, 4:5, :part]
+            offset[n, k : k + 1, :] = sums[2 * n + k, 5:6, :part]
+
+
+def spread_out(got, part, part_h):
+    final, igrad, shares, sums = got["final_o"], got["igrad_o"], got["all_w"], got["all_s"]
+    layers, width = shares.shape[0] // 2, shares.shape[3]
+    shapes = [
+        (layers, part, 3 * width),
+        (layers, 3, part),
+        (layers, part, width),
+        (layers, part, width),
+        (layers, part, 4 * width),
+        (layers, part_h),
+        (layers, part_h, width),
+        (layers, part),
+        (layers, 2, part),
+        (layers, 2, part),
+    ]
+    vmem = pl.BlockSpec(memory_space=pltpu.VMEM)
+    like = jax.ShapeDtypeStruct
+    return pl.pallas_call(
+        spread_kernel,
+        out_shape=(
+            like(final.shape, BF),
+            like(igrad.shape, F32),
+            *[like(shape, F32) for shape in shapes],
+        ),
+        in_specs=[vmem] * 4,
+        out_specs=(vmem,) * 12,
+        compiler_params=pltpu.CompilerParams(vmem_limit_bytes=48 * 1024 * 1024),
+        name="spread",
+    )(final, igrad, shares, sums)
+
+
 def shards(
     pages_in,
     coords,
@@ -1240,29 +1346,7 @@
             offset_w=ln_bias,
         )
         got = pipeline(True, hidden, inputs)
-        sections = lax.axis_size("section")
-        shares, sums = got["all_w"], got["all_s"]
-        attn, feed = shares[0::2], shares[1::2]
-        layers = sections // 2
-
-        def side_by_side(blocks):
-            return blocks.transpose(0, 2, 1, 3).reshape(layers, part, -1).astype(F32)
-
-        rest = sums[:, 3:6, :part].reshape(layers, 2, 3, part)
-        return (
-            got["final_o"],
-            got["igrad_o"],
-            side_by_side(attn[:, :3]),
-            sums[0::2, :3, :part],
-            attn[:, 3].astype(F32),
-            attn[:, 4].astype(F32),
-            side_by_side(feed[:, :4]),
-            sums[1::2, :3].reshape(layers, part_h),
-            feed[:, 4:].reshape(layers, part_h, width).astype(F32),
-            rest[:, 1, 0],
-            rest[:, :, 1],
-            rest[:, :, 2],
-        )
+        return spread_out(got, part, part_h)
 
     norm_row = s % 2
     gain_own = lax.dynamic_index_in_dim(pick(ln_gain), norm_row, 0, keepdims=False)

time: 296 us -> 285 us (0.963)
  local copies, waits for them, and re-layouts: 9.67 us -> 5.76 us
  other arithmetic: 3.18 us -> 0 us
  Pallas kernels: 281 us -> 278 us
    pallas_call x1, Pallas kernels: 281 us -> 274 us  [pipeline(): pl.pallas_call(partial(pipeline_kernel, names, rows, fused), out_shape=tu...]
    pallas_call x0 -> x1, Pallas kernels: none -> 3.94 us  [spread_out(): pl.pallas_call(spread_kernel, out_shape=(like(final.shape, BF), like(igra...]
    slice x5 -> x0, local copies, waits for them, and re-layouts: 3.84 us -> none  [the longest x1 2.69 us: shards(): attn, feed = (shares[0::2], shares[1::2])]
    convert_element_type x2 -> x0, local copies, waits for them, and re-layouts: 3.02 us -> none  [side_by_side(): return blocks.transpose(0, 2, 1, 3).reshape(layers, part, -1).astype(F32)]
where the time goes in v4:
time: 285 us
  Pallas kernels  278 us (98%)
  local copies, waits for them, and re-layouts  5.76 us (2%)
    pallas_call x1, Pallas kernels, pipeline(): pl.pallas_call(partial(pipeline_kernel, names, rows, fused), out_shape=tu...  274 us

profile of v4, /device:TPU:0, one launch (start us, length us, event | category | flops | bytes accessed | tf_op | source)
XLA Modules:
  0.0 284.6 jit_solution(2446368793784302479)
XLA Ops:
  0.6 274.3 %pipeline.1 = (bf16[2,128,768]{2,1,0:T(8,128)(2,1)}, f32[2,128,768]{2,1,0:T(8,128)}, bf16[4,8,96,768]{3,2,1,0:T(8,128)(2,1)}, f32[4,8,128]{2,1,0:T(8,128)}) custom-call(bf16[2,512,768]{2,1,0:T(8,128)(2,1)} %refs_0_.1, bf16[2,512,768]{2,1,0:T(8,128)(2,1)} %refs_1_.1, s32[2,2,512]{2,1,0:T(2,128)} %refs_2_.1, s32[2,4,16]{2,1,0:T(4,128)} %bitcast.2, ...), custom_call_target="tpu_custom_call" | custom-call | tf_op jit(solution)/shard_map/pipeline/pallas_call | solution.py:1233
  274.9 0.0 copy-start
  274.9 2.3 copy-done
  277.3 0.0 copy-start.1
  277.3 1.1 copy-done.1
  278.4 0.0 copy-start.2
  278.4 1.0 copy-done.2
  279.4 0.0 copy-start.3
  279.4 0.7 copy-done.3
  280.1 3.9 %spread.1 = (bf16[2,128,768]{2,1,0:T(8,128)(2,1)}, f32[2,128,768]{2,1,0:T(8,128)}, f32[2,96,2304]{2,1,0:T(8,128)}, f32[2,3,96]{2,1,0:T(4,128)S(1)}, f32[2,96,768...) custom-call(bf16[2,128,768]{2,1,0:T(8,128)(2,1)S(1)} %copy-done.2, ...), custom_call_target="tpu_custom_call" | custom-call | tf_op jit(solution)/shard_map/spread/pallas_call | solution.py:1286
  284.1 0.6 copy.27
Async XLA Ops:
  274.9 2.3 copy-start
  277.3 1.1 copy-start.1
  278.4 1.0 copy-start.2
  279.4 0.7 copy-start.3

commit v5 on v4

--- a/solution.py
+++ b/solution.py
@@ -953,7 +953,7 @@
             at = pl.multiple_of(e * width + hidden, width)
             emit(e, dot_tn(tall(h_in, 0), tall(saved, at)), False)
             advance(e - 1)
-            relay_left(e // 2 - 100 * (e % 2))
+            relay_left(e - 1)
             return 0
 
         lax.fori_loop(0, blocks, step, 0)
@@ -962,7 +962,7 @@
             at = pl.multiple_of(i * width, width)
             emit(i + blocks, dot_tn(tall(saved, at), tall(db, 0)), True)
             advance(i + blocks - 1)
-            relay_left((i + blocks) // 2 - 100 * (i % 2))
+            relay_left(i + blocks - 1)
             return 0
 
         lax.fori_loop(0, blocks, step_b, 0)
@@ -980,7 +980,12 @@
 
         def go_on(q, _):
             advance(q)
-            relay_left(q - 4 + kind)
+            relay_left(q - 4 + 4 * kind)
+
+            @pl.when(jnp.logical_and(jnp.logical_and(is_feed, s < last), q >= 9))
+            def _():
+                left_own(q - 9).start()
+
             return 0
 
         for t in range(1, 8):
@@ -997,7 +1002,7 @@
             relay_left(k)
             return 0
 
-        lax.fori_loop(5 + 7 * kind, hand_on, rest_left, 0)
+        lax.fori_loop(5 + 10 * kind, hand_on, rest_left, 0)
 
         @pl.when(jnp.logical_and(s > 0, s < last))
         def _():
@@ -1005,14 +1010,7 @@
                 left_own(u).start()
                 return 0
 
-            lax.fori_loop(0, units, own_left, 0)
-
-
-        @pl.when(s == last)
-        def _():
-            for m in range(micro):
-                for j in range(sections - 1):
-                    share(h_out, r.fin_in, r.fin_send, r.fin_recv, m, j).start()
+            lax.fori_loop(6 * kind, units, own_left, 0)
 
 
         for by in range(1, sections):
@@ -1021,8 +1019,14 @@
             def _(by=by):
                 t = s - by
 
-                def relay(u, _):
+                def relay(u, _, by=by):
                     right_on(t, u).wait_recv()
+                    if by == 2:
+                        @pl.when(jnp.logical_and(s == last, u == 3))
+                        def _():
+                            for m in range(micro):
+                                for j in range(sections - 1):
+                                    share(h_out, r.fin_in, r.fin_send, r.fin_recv, m, j).start()
 
                     @pl.when(s != last)
                     def _():
@@ -1244,19 +1248,66 @@
     return dict(zip(outs, got, strict=True))
 
 
-def spread_kernel(final, igrad, shares, sums, final_o, igrad_o, qkv, bias, pos, out, into, into_b, down, down_b, gain, offset):
-    final_o[...] = final[...]
-    igrad_o[...] = igrad[...]
+def spread_kernel(
+    final,
+    igrad,
+    shares,
+    sums,
+    final_o,
+    igrad_o,
+    qkv_o,
+    bias,
+    pos_o,
+    out_o,
+    into_o,
+    into_b,
+    down_o,
+    down_b,
+    gain,
+    offset,
+    got,
+    qkv,
+    pos,
+    out,
+    into,
+    down,
+    load_sem,
+    save_sem,
+):
     layers, part, width = pos.shape
+
+    def load(t):
+        return pltpu.make_async_copy(shares.at[t], got.at[t], load_sem.at[t])
+
+    def save(n, i):
+        source, target = (
+            (qkv, qkv_o),
+            (pos, pos_o),
+            (out, out_o),
+            (into, into_o),
+            (down, down_o),
+        )[i]
+        return pltpu.make_async_copy(source.at[n], target.at[n], save_sem.at[n, i])
+
+    for t in range(2 * layers):
+        load(t).start()
     for n in range(layers):
         attn, feed = 2 * n, 2 * n + 1
+        load(attn).wait()
         for i in range(3):
-            qkv[n, :, i * width : (i + 1) * width] = shares[attn, i].astype(F32)
-        pos[n] = shares[attn, 3].astype(F32)
-        out[n] = shares[attn, 4].astype(F32)
+            qkv[n, :, i * width : (i + 1) * width] = got[attn, i].astype(F32)
+        save(n, 0).start()
+        pos[n] = got[attn, 3].astype(F32)
+        save(n, 1).start()
+        out[n] = got[attn, 4].astype(F32)
+        save(n, 2).start()
+        load(feed).wait()
         for i in range(4):
-            into[n, :, i * width : (i + 1) * width] = shares[feed, i].astype(F32)
-            down[n, i * part : (i + 1) * part, :] = shares[feed, 4 + i].astype(F32)
+            into[n, :, i * width : (i + 1) * width] = got[feed, i].astype(F32)
+        save(n, 3).start()
+        for i in range(4):
+            down[n, i * part : (i + 1) * part, :] = got[feed, 4 + i].astype(F32)
+        save(n, 4).start()
         bias[n] = sums[attn, 0:3, :part]
         for i in range(3):
             into_b[n : n + 1, i * 128 : (i + 1) * 128] = sums[feed, i : i + 1, :]
@@ -1264,35 +1315,44 @@
         for k in range(2):
             gain[n, k : k + 1, :] = sums[2 * n + k, 4:5, :part]
             offset[n, k : k + 1, :] = sums[2 * n + k, 5:6, :part]
+    for n in range(layers):
+        for i in range(5):
+            save(n, i).wait()
+    final_o[...] = final[...]
+    igrad_o[...] = igrad[...]
 
 
 def spread_out(got, part, part_h):
     final, igrad, shares, sums = got["final_o"], got["igrad_o"], got["all_w"], got["all_s"]
     layers, width = shares.shape[0] // 2, shares.shape[3]
-    shapes = [
-        (layers, part, 3 * width),
-        (layers, 3, part),
-        (layers, part, width),
-        (layers, part, width),
-        (layers, part, 4 * width),
-        (layers, part_h),
-        (layers, part_h, width),
-        (layers, part),
-        (layers, 2, part),
-        (layers, 2, part),
+    vmem = pl.BlockSpec(memory_space=pltpu.VMEM)
+    hbm = pl.BlockSpec(memory_space=pl.ANY)
+    outs = [
+        (vmem, final.shape, BF),
+        (vmem, igrad.shape, F32),
+        (hbm, (layers, part, 3 * width), F32),
+        (vmem, (layers, 3, part), F32),
+        (hbm, (layers, part, width), F32),
+        (hbm, (layers, part, width), F32),
+        (hbm, (layers, part, 4 * width), F32),
+        (vmem, (layers, part_h), F32),
+        (hbm, (layers, part_h, width), F32),
+        (vmem, (layers, part), F32),
+        (vmem, (layers, 2, part), F32),
+        (vmem, (layers, 2, part), F32),
     ]
-    vmem = pl.BlockSpec(memory_space=pltpu.VMEM)
-    like = jax.ShapeDtypeStruct
     return pl.pallas_call(
         spread_kernel,
-        out_shape=(
-            like(final.shape, BF),
-            like(igrad.shape, F32),
-            *[like(shape, F32) for shape in shapes],
-        ),
-        in_specs=[vmem] * 4,
-        out_specs=(vmem,) * 12,
-        compiler_params=pltpu.CompilerParams(vmem_limit_bytes=48 * 1024 * 1024),
+        out_shape=tuple(jax.ShapeDtypeStruct(shape, kind) for _, shape, kind in outs),
+        in_specs=[vmem, vmem, hbm, vmem],
+        out_specs=tuple(where for where, _, _ in outs),
+        scratch_shapes=[
+            pltpu.VMEM(shares.shape, BF),
+            *[pltpu.VMEM(outs[i][1], F32) for i in (2, 4, 5, 6, 8)],
+            pltpu.SemaphoreType.DMA((2 * layers,)),
+            pltpu.SemaphoreType.DMA((layers, 5)),
+        ],
+        compiler_params=pltpu.CompilerParams(vmem_limit_bytes=62 * 1024 * 1024),
         name="spread",
     )(final, igrad, shares, sums)
 

time: 285 us -> 274 us (0.961)
  Pallas kernels: 278 us -> 272 us
  local copies, waits for them, and re-layouts: 5.76 us -> 1.26 us
    pallas_call x1, Pallas kernels: 274 us -> 265 us  [pipeline(): pl.pallas_call(partial(pipeline_kernel, names, rows, fused), out_shape=tu...]
    unnamed x8 -> x0, local copies, waits for them, and re-layouts: 5.17 us -> none
    pallas_call x1, Pallas kernels: 3.94 us -> 6.85 us  [spread_out(): pl.pallas_call(spread_kernel, out_shape=tuple((jax.ShapeDtypeStruct(shape...]
where the time goes in v5:
time: 274 us
  Pallas kernels  272 us (99%)
    pallas_call x1, Pallas kernels, pipeline(): pl.pallas_call(partial(pipeline_kernel, names, rows, fused), out_shape=tu...  265 us
    pallas_call x1, Pallas kernels, spread_out(): pl.pallas_call(spread_kernel, out_shape=tuple((jax.ShapeDtypeStruct(shape...  6.85 us

profile of v5, /device:TPU:0, one launch (start us, length us, event | category | flops | bytes accessed | tf_op | source)
XLA Modules:
  0.0 274.2 jit_solution(6792901181521707801)
XLA Ops:
  0.6 265.4 %pipeline.1 = (bf16[2,128,768]{2,1,0:T(8,128)(2,1)}, f32[2,128,768]{2,1,0:T(8,128)}, bf16[4,8,96,768]{3,2,1,0:T(8,128)(2,1)}, f32[4,8,128]{2,1,0:T(8,128)}) custom-call(bf16[2,512,768]{2,1,0:T(8,128)(2,1)} %refs_0_.1, bf16[2,512,768]{2,1,0:T(8,128)(2,1)} %refs_1_.1, s32[2,2,512]{2,1,0:T(2,128)} %refs_2_.1, s32[2,4,16]{2,1,0:T(4,128)} %bitcast.2, ...), custom_call_target="tpu_custom_call" | custom-call | tf_op jit(solution)/shard_map/pipeline/pallas_call | solution.py:1237
  266.1 6.9 %spread.1 = (bf16[2,128,768]{2,1,0:T(8,128)(2,1)}, f32[2,128,768]{2,1,0:T(8,128)}, f32[2,96,2304]{2,1,0:T(8,128)}, f32[2,3,96]{2,1,0:T(4,128)}, f32[2,96,768]{2,...) custom-call(bf16[2,128,768]{2,1,0:T(8,128)(2,1)} %get-tuple-element., ...), custom_call_target="tpu_custom_call" | custom-call | tf_op jit(solution)/shard_map/spread/pallas_call | solution.py:1344
  272.9 1.3 copy.27

commit v6 on v5

--- a/solution.py
+++ b/solution.py
@@ -980,11 +980,12 @@
 
         def go_on(q, _):
             advance(q)
-            relay_left(q - 4 + 4 * kind)
-
-            @pl.when(jnp.logical_and(jnp.logical_and(is_feed, s < last), q >= 9))
-            def _():
-                left_own(q - 9).start()
+            relay_left(kind * q + (1 - kind) * (2 * q - 8))
+            relay_left((1 - kind) * (2 * q - 7) - kind)
+
+            @pl.when(jnp.logical_and(jnp.logical_and(is_feed, s < last), q >= 8))
+            def _():
+                left_own(q - 8).start()
 
             return 0
 
@@ -1002,7 +1003,7 @@
             relay_left(k)
             return 0
 
-        lax.fori_loop(5 + 10 * kind, hand_on, rest_left, 0)
+        lax.fori_loop(10 + 5 * kind, hand_on, rest_left, 0)
 
         @pl.when(jnp.logical_and(s > 0, s < last))
         def _():
@@ -1010,7 +1011,7 @@
                 left_own(u).start()
                 return 0
 
-            lax.fori_loop(6 * kind, units, own_left, 0)
+            lax.fori_loop(7 * kind, units, own_left, 0)
 
 
         for by in range(1, sections):

time: 274 us -> 274 us (level)
  no operation moved by 1% of the time
where the time goes in v6:
time: 274 us
  Pallas kernels  272 us (99%)
    pallas_call x1, Pallas kernels, pipeline(): pl.pallas_call(partial(pipeline_kernel, names, rows, fused), out_shape=tu...  265 us
    pallas_call x1, Pallas kernels, spread_out(): pl.pallas_call(spread_kernel, out_shape=tuple((jax.ShapeDtypeStruct(shape...  6.85 us

profile of v6, /device:TPU:0, one launch (start us, length us, event | category | flops | bytes accessed | tf_op | source)
XLA Modules:
  0.0 274.2 jit_solution(15679238836706295145)
XLA Ops:
  0.6 265.4 %pipeline.1 = (bf16[2,128,768]{2,1,0:T(8,128)(2,1)}, f32[2,128,768]{2,1,0:T(8,128)}, bf16[4,8,96,768]{3,2,1,0:T(8,128)(2,1)}, f32[4,8,128]{2,1,0:T(8,128)}) custom-call(bf16[2,512,768]{2,1,0:T(8,128)(2,1)} %refs_0_.1, bf16[2,512,768]{2,1,0:T(8,128)(2,1)} %refs_1_.1, s32[2,2,512]{2,1,0:T(2,128)} %refs_2_.1, s32[2,4,16]{2,1,0:T(4,128)} %bitcast.2, ...), custom_call_target="tpu_custom_call" | custom-call | tf_op jit(solution)/shard_map/pipeline/pallas_call | solution.py:1238
  266.1 6.9 %spread.1 = (bf16[2,128,768]{2,1,0:T(8,128)(2,1)}, f32[2,128,768]{2,1,0:T(8,128)}, f32[2,96,2304]{2,1,0:T(8,128)}, f32[2,3,96]{2,1,0:T(4,128)}, f32[2,96,768]{2,...) custom-call(bf16[2,128,768]{2,1,0:T(8,128)(2,1)} %get-tuple-element., ...), custom_call_target="tpu_custom_call" | custom-call | tf_op jit(solution)/shard_map/spread/pallas_call | solution.py:1345
  272.9 1.3 copy.27
